TPU v7x, 32 devices: a whole 2x2x4 slice. The times are simulated.
32 devices in a mesh: dp: 4 (over y, core), pipe: 4 (over z), tensor: 2 (over x).
Axes of the slice: x: 2, y: 2, z: 4, core: 2. Of those that a mesh axis runs over, the one named last changes fastest.
Arguments:
- inputs: bfloat16 [4, 1024, 8192], P('pipe', 'dp', 'tensor'), may hold values from -900 to 900
- norm_gain: float32 [4, 8192], P('pipe', 'tensor'), may hold values from 0.1 to 1.9
- value_weight: bfloat16 [4, 1024, 8192], P('pipe', None, 'tensor'), may hold values from -1 to 1
- value_cotangent: bfloat16 [4, 1024, 1024], P('pipe', 'dp'), may hold values from -6 to 6
- upper_grad: bfloat16 [4, 1024, 8192], P('pipe', 'dp', 'tensor'), may hold values from -3 to 3
Outputs:
- input_grad: bfloat16 [4, 1024, 8192], P('pipe', 'dp', 'tensor')
- weight_grad: float32 [4, 1024, 8192], P('pipe', 'dp', 'tensor')
- gain_grad: float32 [4, 8192], P('pipe', 'tensor')
All inputs are finite; a program needn't handle non-finite values.
Results may differ from a plain program's by a relative error of at most 0.014.
Values may be sent and summed in bfloat16 or wider, within the bound.
No kernel may reach another device: no remote copies, remote signals or barrier semaphores. Data moves between devices by JAX's collectives and lax.ppermute only.
A program may use at most 64 MiB of HBM per device.

v0:
```python
import functools

import jax
import jax.numpy as jnp
from jax import lax
from jax.experimental import pallas as pl
from jax.experimental.pallas import tpu as pltpu
from jax.sharding import PartitionSpec as P

D = 8192
EPS = 1e-05
Y_PARTS = (5, 3)
MIB = 1 << 20
PARAMS = pltpu.CompilerParams(vmem_limit_bytes=16 * MIB)


def after(value, *others):
    return lax.optimization_barrier((value,) + others)[0]


def spans(total, parts):
    unit = total // sum(parts)
    ends = [unit * sum(parts[: i + 1]) for i in range(len(parts))]
    return list(zip([0] + ends[:-1], [unit * p for p in parts]))


def tile_of(width, largest):
    tile = min(width, largest)
    while width % tile:
        tile //= 2
    return tile


def from_others(array, axis):
    count = lax.axis_size(axis)
    return [lax.ppermute(array, axis, [(i, (i + by) % count) for i in range(count)]) for by in range(1, count)]


class Replicas:
    def __init__(self, axis):
        self.axis = axis
        self.count = lax.axis_size(axis)
        self.width = 2 if self.count % 2 == 0 else 1
        self.groups = self.count // self.width

    def to(self, index, high, low):
        return (index // self.width + high) % self.groups * self.width + (index % self.width + low) % self.width

    def index(self, high, low):
        return self.to(lax.axis_index(self.axis), high, low)

    def send(self, array, high, low):
        return lax.ppermute(array, self.axis, [(i, self.to(i, high, low)) for i in range(self.count)])


def lanes_to_row(sums):
    return jnp.sum(sums.T, axis=0, keepdims=True)


def row_to_column(row):
    return jnp.broadcast_to(row, (128, row.shape[1])).T[:, :1]


def fold_lanes(array):
    total = array[:, :128]
    for at in range(128, array.shape[1], 128):
        total = total + array[:, at : at + 128]
    return total


def inverse_row(sums):
    total = sums[0][...]
    for ref in sums[1:]:
        total = total + ref[...]
    return lax.rsqrt(total / D + EPS)


def scale_kernel(scale, *refs):
    sums, cot_ref, scaled_ref = refs[:-2], refs[-2], refs[-1]
    scaled_ref[...] = (cot_ref[...].astype(jnp.float32).T * (inverse_row(sums) * scale)).astype(jnp.bfloat16)


def scaled_cotangent(sums, cotangent, scale):
    return pl.pallas_call(
        functools.partial(scale_kernel, scale),
        out_shape=jax.ShapeDtypeStruct(cotangent.shape[::-1], jnp.bfloat16),
        compiler_params=PARAMS,
        cost_estimate=pl.CostEstimate(
            flops=2 * cotangent.size, bytes_accessed=4 * cotangent.size, transcendentals=0
        ),
    )(*sums, cotangent)


def grad_kernel(scale, others, *refs):
    sums = refs[: others + 1]
    cot_ref, weight_ref, x_ref, gain_ref, scaled_grad_ref, gain_grad_ref, center_ref = refs[others + 1 : -2]
    inverse, centers = refs[-2:]
    step = pl.program_id(0)

    @pl.when(step == 0)
    def _():
        inverse[...] = row_to_column(inverse_row(sums))
        centers[...] = jnp.zeros_like(centers)

    hidden_grad = jnp.dot(cot_ref[...], weight_ref[...], preferred_element_type=jnp.float32)
    scaled_grad = inverse[...] * hidden_grad
    product = scaled_grad * x_ref[...].astype(jnp.float32)
    gain_grad_ref[...] = jnp.sum(product, axis=0, keepdims=True) * scale
    centers[...] += fold_lanes(gain_ref[...] * product)
    scaled_grad_ref[...] = (gain_ref[...] * scaled_grad).astype(jnp.bfloat16)

    @pl.when(step == pl.num_programs(0) - 1)
    def _():
        center_ref[...] = lanes_to_row(centers[...])


def scaled_grads(sums, cotangent, weight, x, gain_row, scale):
    tokens, features = x.shape
    tile = tile_of(features, 1024)
    column = lambda c: (0, c)
    whole = lambda c: (0, 0)
    return pl.pallas_call(
        functools.partial(grad_kernel, scale, len(sums) - 1),
        grid=(features // tile,),
        in_specs=[pl.BlockSpec((1, tokens), whole)] * len(sums)
        + [
            pl.BlockSpec(cotangent.shape, whole),
            pl.BlockSpec((weight.shape[0], tile), column),
            pl.BlockSpec((tokens, tile), column),
            pl.BlockSpec((1, tile), column),
        ],
        out_specs=[
            pl.BlockSpec((tokens, tile), column),
            pl.BlockSpec((1, tile), column),
            pl.BlockSpec((1, tokens), whole),
        ],
        out_shape=[
            jax.ShapeDtypeStruct((tokens, features), jnp.bfloat16),
            jax.ShapeDtypeStruct((1, features), jnp.float32),
            jax.ShapeDtypeStruct((1, tokens), jnp.float32),
        ],
        scratch_shapes=[pltpu.VMEM((tokens, 1), jnp.float32), pltpu.VMEM((tokens, 128), jnp.float32)],
        compiler_params=PARAMS,
        cost_estimate=pl.CostEstimate(
            flops=2 * tokens * features * weight.shape[0],
            bytes_accessed=2 * (weight.size + cotangent.size + 2 * x.size),
            transcendentals=0,
        ),
    )(*sums, cotangent, weight, x, gain_row)


def add_kernel(others, *refs):
    sums, centers = refs[: others + 1], refs[others + 1 : 2 * others + 2]
    scaled_grad_ref, x_ref, received_ref, out_ref, factor = refs[2 * others + 2 :]

    @pl.when(pl.program_id(0) == 0)
    def _():
        inverse = inverse_row(sums)
        center = centers[0][...]
        for ref in centers[1:]:
            center = center + ref[...]
        factor[...] = row_to_column(inverse * inverse * (center / D))

    height = x_ref.shape[0]
    rows = pl.ds(pl.multiple_of(pl.program_id(0) * height, height), height)
    local = scaled_grad_ref[...].astype(jnp.float32) - x_ref[...].astype(jnp.float32) * factor[rows]
    out_ref[...] = (local + received_ref[...].astype(jnp.float32)).astype(out_ref.dtype)


def add_rows(sums, centers, scaled_grad, x, received):
    tokens, features = received.shape
    tile = tile_of(tokens, 128)
    block = pl.BlockSpec((tile, features), lambda r: (r, 0))
    return pl.pallas_call(
        functools.partial(add_kernel, len(sums) - 1),
        grid=(tokens // tile,),
        in_specs=[pl.BlockSpec((1, tokens), lambda r: (0, 0))] * (2 * len(sums)) + [block] * 3,
        out_specs=block,
        out_shape=jax.ShapeDtypeStruct(x.shape, received.dtype),
        scratch_shapes=[pltpu.VMEM((tokens, 1), jnp.float32)],
        compiler_params=PARAMS,
        cost_estimate=pl.CostEstimate(flops=4 * x.size, bytes_accessed=8 * x.size, transcendentals=0),
    )(*sums, *centers, scaled_grad, x, received)


def weight_kernel(groups, *refs):
    scaled_refs, gain_ref, blocks, out_ref = refs[:groups], refs[groups], refs[groups + 1 :], refs[-1]
    tokens = blocks[0].shape[0]
    width = scaled_refs[0].shape[1] // tokens
    total = None
    for at in range(groups * width):
        scaled = scaled_refs[at // width][:, at % width * tokens : (at % width + 1) * tokens]
        term = jnp.dot(scaled, blocks[at][...], preferred_element_type=jnp.float32)
        total = term if total is None else total + term
    out_ref[...] = total * gain_ref[...]


def weight_columns(scaled, held, received, gain_row, start, out):
    tokens, features = held[0].shape
    width = received[0].shape[1]
    rows = scaled[0].shape[0]
    tile = next(t for t in (1536, 1280, 768, 640, 512, 256, 128) if width % t == 0 and start % t == 0)
    first = start // tile
    whole = lambda c: (0, 0)
    placed = lambda c: (0, first + c)
    here = lambda c: (0, c)
    in_specs = [pl.BlockSpec(part.shape, whole) for part in scaled] + [pl.BlockSpec((1, tile), placed)]
    in_specs += [pl.BlockSpec((tokens, tile), placed)] * len(held)
    in_specs += [pl.BlockSpec((tokens, tile), here)] * len(received)
    args, aliases = [*scaled, gain_row, *held, *received], {}
    if out is not None:
        in_specs.append(pl.BlockSpec(memory_space=pl.ANY))
        aliases = {len(args): 0}
        args.append(out)
    sources = len(held) + len(received)
    return pl.pallas_call(
        functools.partial(weight_kernel, len(scaled)),
        grid=(width // tile,),
        in_specs=in_specs,
        out_specs=pl.BlockSpec((rows, tile), placed),
        out_shape=jax.ShapeDtypeStruct((rows, features), jnp.float32),
        input_output_aliases=aliases,
        compiler_params=PARAMS,
        cost_estimate=pl.CostEstimate(
            flops=2 * sources * tokens * rows * width,
            bytes_accessed=2 * sources * tokens * (rows + width) + 4 * rows * width,
            transcendentals=0,
        ),
    )(*args)


def per_device(inputs, norm_gain, value_weight, value_cotangent, upper_grad):
    replicas = Replicas("dp")
    sections = lax.axis_size("pipe")
    slices = lax.axis_size("tensor")
    x = inputs[0]
    tokens, features = x.shape
    gain_row = norm_gain
    cotangent = value_cotangent[0]
    rows = cotangent.shape[1] // replicas.count
    grad_scale = float(tokens * replicas.count) ** (-0.5)
    far = range(1, replicas.groups)
    near = range(1, replicas.width)

    columns = spans(features, Y_PARTS)
    column_part = lambda c, *gates: (after(x, *gates) if gates else x)[:, columns[c][0] : sum(columns[c])]
    part = column_part(0)
    far_x = [[replicas.send(part, high, 0) for high in far]]
    down = [(i, i - 1) for i in range(1, sections)]
    upper = lax.ppermute(upper_grad[0], "pipe", down)

    squares = jnp.sum(jnp.square(x.astype(jnp.float32)), axis=1)[None]
    sums = [squares] + from_others(squares, "tensor")
    scaled = scaled_cotangent(sums, cotangent, grad_scale)
    scaled_grad, gain_grad, center = scaled_grads(sums, cotangent, value_weight[0], x, gain_row, grad_scale)
    centers = [center] + from_others(center, "tensor")
    near_x = [replicas.send(after(x, scaled), 0, low) for low in near]

    by_core = scaled.reshape(replicas.count, rows, tokens)
    turn = replicas.width - 1
    rows_for = lambda high, low: lax.dynamic_index_in_dim(by_core, replicas.index(high, low), 0, False)
    pair = [[rows_for(high, turn if high else 0)] for high in range(replicas.groups)]
    for low in near:
        theirs = jnp.stack([rows_for(high, turn + low if high else low) for high in range(replicas.groups)])
        swapped = replicas.send(theirs, 0, low)
        for high in range(replicas.groups):
            pair[high].append(swapped[high])
    pair = [jnp.concatenate(blocks, axis=1) for blocks in pair]
    cots = [pair[0]]
    share = tokens * replicas.width // slices
    mine = lax.axis_index("tensor")
    got = [
        replicas.send(lax.dynamic_slice_in_dim(pair[high], mine * share, share, axis=1), high, turn) for high in far
    ]
    for block in got:
        shares = jnp.concatenate([block] + from_others(block, "tensor"), axis=1)
        pieces = [
            lax.dynamic_slice_in_dim(shares, (mine - at) % slices * share, share, axis=1) for at in range(slices)
        ]
        cots.append(jnp.concatenate(pieces, axis=1))
    gain_far = [replicas.send(gain_grad, high, turn) for high in far]
    gain_grad = sum(gain_far, gain_grad)
    gain_grad = sum([replicas.send(gain_grad, 0, low) for low in near], gain_grad)

    for c in range(1, len(columns)):
        part = column_part(c, *got, *gain_far)
        far_x.append([replicas.send(part, high, 0) for high in far])
    weight_grad = None
    for c, ((start, width), direct) in enumerate(zip(columns, far_x)):
        gates = got + gain_far
        if c == len(columns) - 1:
            input_grad = add_rows(sums, centers, scaled_grad, x, upper)
            gates = [input_grad, gain_grad, *cots]
        received = []
        for block in direct:
            handed = after(block, *gates) if gates else block
            received += [replicas.send(handed, 0, low) for low in near] + [block]
        weight_grad = weight_columns(cots, [x] + near_x, received, gain_row, start, weight_grad)
    return (input_grad[None], weight_grad[None], gain_grad)


def solution(mesh):
    return jax.shard_map(
        per_device,
        mesh=mesh,
        in_specs=(
            P("pipe", "dp", "tensor"),
            P("pipe", "tensor"),
            P("pipe", None, "tensor"),
            P("pipe", "dp", None),
            P("pipe", "dp", "tensor"),
        ),
        out_specs=(P("pipe", "dp", "tensor"), P("pipe", "dp", "tensor"), P("pipe", "tensor")),
        check_vma=False,
    )
```

profile of v0, /device:TPU:0, one launch (start us, length us, event | category | flops | bytes accessed | tf_op | source)
XLA Modules:
  0.0 67.8 jit_solution(2560666323202863549)
XLA Ops:
  0.6 0.0 copy-start
  0.6 0.0 copy-start.2
  0.6 2.6 %slice.18 = bf16[256,2560]{1,0:T(8,128)(2,1)} slice(bf16[256,4096]{1,0:T(8,128)(2,1)} %bitcast.17), slice={[0:256], [0:2560]} | slice | bytes 2621440 | tf_op jit(solution)/shard_map/slice | solution.py:246
  3.3 3.0 %collective-permute-start.11 = (bf16[256,2560]{1,0:T(8,128)(2,1)}, bf16[256,2560]{1,0:T(8,128)(2,1)}, u32[]{:S(2)}, u32[]{:S(2)}) collective-permute-start(bf16[256,2560]{1,0:T(8,128)(2,1)} %slice.18), channel_id=1, source_target_pairs={{0,16},{8,24},{16,0},{24,8},{1,17},{9,25},{17,1},{25,9},{2,18},{10... | collective-permute-start | bytes 3932168 | tf_op jit(solution)/shard_map/ppermute | solution.py:53
  6.2 1.3 %collective-permute-start.2 = (bf16[256,4096]{1,0:T(8,128)(2,1)}, bf16[256,4096]{1,0:T(8,128)(2,1)}, u32[]{:S(2)}, u32[]{:S(2)}) collective-permute-start(bf16[256,4096]{1,0:T(8,128)(2,1)} %bitcast.34), channel_id=1, source_target_pairs={{2,0},{4,2},{6,4},{3,1},{5,3},{7,5},{10,8},{12,10},{14,12},{11,9},... | collective-permute-start | bytes 6291464 | tf_op jit(solution)/shard_map/ppermute | solution.py:250
  7.5 0.0 copy-done
  7.5 0.5 multiply_reduce_fusion
  8.0 0.0 copy-start.5
  8.0 1.6 %collective-permute-start = (f32[1,256]{1,0:T(1,128)S(1)}, f32[1,256]{1,0:T(1,128)S(1)}, u32[]{:S(2)}, u32[]{:S(2)}) collective-permute-start(f32[1,256]{1,0:T(1,128)S(1)} %bitcast.28), channel_id=1, source_target_pairs={{0,1},{1,0},{2,3},{3,2},{4,5},{5,4},{6,7},{7,6},{8,9},{9,8},{10,11... | collective-permute-start | bytes 3080 | tf_op jit(solution)/shard_map/ppermute | solution.py:36
  9.6 2.1 %collective-permute-done.refs_1_ = f32[1,256]{1,0:T(1,128)S(1)} collective-permute-done((f32[1,256]{1,0:T(1,128)S(1)}, f32[1,256]{1,0:T(1,128)S(1)}, u32[]{:S(2)}, u32[]{:S(2)}) %collective-permute-start) | collective-permute-done | bytes 1056 | tf_op jit(solution)/shard_map/ppermute | solution.py:36
  11.7 0.0 copy-done.2
  11.7 0.2 shard_map.78
  11.9 0.7 %dynamic-slice_bitcast_fusion = (bf16[256,256]{1,0:T(8,128)(2,1)S(1)}, bf16[1,256,256]{2,1,0:T(8,128)(2,1)S(1)}, bf16[1,256,256]{2,1,0:T(8,128)(2,1)S(1)}, bf16[256,256]{1,0:T(8,128)(2,1)}) fusion(bf16[4,256,256]{2,1,0:T(8,128)(2,1)S(1)} %bitcast.27, s32[]{:T(128)S(6)} %select_n.86, s32[]{:T(128)S(6)} %select_n.85, s32[]{:T(128)S(6)} %select_n.82, ...), kind=kLoop, calls=%fused_computation.9 | loop fusion | bytes 1048592 | tf_op jit(solution)/shard_map/jit(dynamic_index_in_dim)/squeeze | solution.py:261
  12.6 0.1 collective-permute-start.3
  12.7 0.5 collective-permute-start.6
  13.2 1.0 %collective-permute-done.3 = bf16[2,256,256]{2,1,0:T(8,128)(2,1)S(1)} collective-permute-done((bf16[2,256,256]{2,1,0:T(8,128)(2,1)S(1)}, bf16[2,256,256]{2,1,0:T(8,128)(2,1)S(1)}, u32[]{:S(2)}, u32[]{:S(2)}) %collective-permute-start.3) | collective-permute-done | bytes 262176 | tf_op jit(solution)/shard_map/ppermute | solution.py:53
  14.2 0.7 slice_bitcast_fusion
  14.9 0.1 fusion
  14.9 0.1 collective-permute-start.4
  15.0 0.0 copy-done.5
  15.0 0.0 copy-start.1
  15.0 3.4 %copy-done.1 = bf16[1,1024,4096]{2,1,0:T(8,128)(2,1)S(1)} copy-done((bf16[1,1024,4096]{2,1,0:T(8,128)(2,1)S(1)}, bf16[1,1024,4096]{2,1,0:T(8,128)(2,1)}, u32[]{:S(2)}) %copy-start.1) | copy-done | bytes 8388632
  18.4 4.6 %shard_map.76 = (bf16[256,4096]{1,0:T(8,128)(2,1)S(1)}, f32[1,4096]{1,0:T(1,128)S(1)}, f32[1,256]{1,0:T(1,128)S(1)}) custom-call(f32[1,256]{1,0:T(1,128)S(1)} %bitcast.30, f32[1,256]{1,0:T(1,128)S(1)} %collective-permute-done.refs_1_, bf16[256,1024]{1,0:T(8,128)(2,1)S(1)} %bitcast.26, bf16[1024,4096]{1,0:T(8,128)(2,1)S(1)} %bitcast.24, ...), custom_call_target="tpu_custom_call" | custom-call | flops 2147483648 | bytes 13107200 | tf_op jit(solution)/shard_map/pallas_call | solution.py:122
  23.0 0.0 copy-start.3
  23.0 1.3 %copy-done.3 = bf16[256,4096]{1,0:T(8,128)(2,1)} copy-done((bf16[256,4096]{1,0:T(8,128)(2,1)}, bf16[256,4096]{1,0:T(8,128)(2,1)S(1)}, u32[]{:S(2)}) %copy-start.3) | copy-done | bytes 2097176
  24.3 1.7 %collective-permute-start.7 = (f32[1,4096]{1,0:T(1,128)S(1)}, f32[1,4096]{1,0:T(1,128)S(1)}, u32[]{:S(2)}, u32[]{:S(2)}) collective-permute-start(f32[1,4096]{1,0:T(1,128)S(1)} %get-tuple-element.13), channel_id=1, source_target_pairs={{0,24},{8,16},{16,8},{24,0},{1,25},{9,17},{17,9},{25,1},{2,26},{10... | collective-permute-start | bytes 49160 | tf_op jit(solution)/shard_map/ppermute | solution.py:53
  26.0 11.6 %collective-permute-done.7 = f32[1,4096]{1,0:T(1,128)S(1)} collective-permute-done((f32[1,4096]{1,0:T(1,128)S(1)}, f32[1,4096]{1,0:T(1,128)S(1)}, u32[]{:S(2)}, u32[]{:S(2)}) %collective-permute-start.7) | collective-permute-done | bytes 16416 | tf_op jit(solution)/shard_map/ppermute | solution.py:53
  37.6 0.0 collective-permute-done.4
  37.6 0.0 copy-start.6
  37.6 1.0 %slice.14 = bf16[256,1536]{1,0:T(8,128)(2,1)} slice(bf16[256,4096]{1,0:T(8,128)(2,1)S(1)} %bitcast.20), slice={[0:256], [2560:4096]} | slice | bytes 1572864 | tf_op jit(solution)/shard_map/slice | solution.py:246
  38.6 1.3 %collective-permute-start.8 = (bf16[256,1536]{1,0:T(8,128)(2,1)}, bf16[256,1536]{1,0:T(8,128)(2,1)}, u32[]{:S(2)}, u32[]{:S(2)}) collective-permute-start(bf16[256,1536]{1,0:T(8,128)(2,1)} %slice.14), channel_id=1, source_target_pairs={{0,16},{8,24},{16,0},{24,8},{1,17},{9,25},{17,1},{25,9},{2,18},{10... | collective-permute-start | bytes 2359304 | tf_op jit(solution)/shard_map/ppermute | solution.py:53
  39.9 0.0 collective-permute-done.11.refs_6_
  39.9 1.1 %collective-permute-start.12 = (bf16[256,2560]{1,0:T(8,128)(2,1)}, bf16[256,2560]{1,0:T(8,128)(2,1)S(1)}, u32[]{:S(2)}, u32[]{:S(2)}) collective-permute-start(bf16[256,2560]{1,0:T(8,128)(2,1)} %collective-permute-done.11.refs_6_), channel_id=1, source_target_pairs={{0,8},{8,0},{16,24},{24,16},{1,9},{9,1},{17,25},{25,17},{2,10},{10... | collective-permute-start | bytes 3932168 | tf_op jit(solution)/shard_map/ppermute | solution.py:53
  41.1 0.0 copy-done.6
  41.1 0.1 collective-permute-start.9
  41.2 0.0 copy-start.4
  41.2 2.4 %collective-permute-done.9 = f32[1,4096]{1,0:T(1,128)S(1)} collective-permute-done((f32[1,4096]{1,0:T(1,128)S(1)}, f32[1,4096]{1,0:T(1,128)S(1)}, u32[]{:S(2)}, u32[]{:S(2)}) %collective-permute-start.9) | collective-permute-done | bytes 16416 | tf_op jit(solution)/shard_map/ppermute | solution.py:53
  43.6 0.6 add.107
  44.2 1.5 %collective-permute-start.5 = (bf16[256,256]{1,0:T(8,128)(2,1)}, bf16[256,256]{1,0:T(8,128)(2,1)S(1)}, u32[]{:S(2)}, u32[]{:S(2)}) collective-permute-start(bf16[256,256]{1,0:T(8,128)(2,1)} %copy-done.6), channel_id=1, source_target_pairs={{0,1},{1,0},{2,3},{3,2},{4,5},{5,4},{6,7},{7,6},{8,9},{9,8},{10,11... | collective-permute-start | bytes 393224 | tf_op jit(solution)/shard_map/ppermute | solution.py:36
  45.7 1.0 %pad_maximum_fusion.1.refs_0_ = bf16[256,512]{1,0:T(8,128)(2,1)S(1)} fusion(bf16[256,256]{1,0:T(8,128)(2,1)} %get-tuple-element.24, bf16[256,256]{1,0:T(8,128)(2,1)} %get-tuple-element.20), kind=kLoop, calls=%fused_computation.2 | loop fusion | flops 524288 | bytes 524288 | tf_op jit(solution)/shard_map/concatenate | solution.py:268
  46.7 0.9 %constant_dynamic-update-slice_fusion.1 = bf16[256,512]{1,0:T(8,128)(2,1)S(1)} fusion(bf16[256,256]{1,0:T(8,128)(2,1)} %copy-done.6), kind=kLoop, calls=%fused_computation.12 | loop fusion | bytes 262144
  47.6 2.4 %collective-permute-done.5 = bf16[256,256]{1,0:T(8,128)(2,1)S(1)} collective-permute-done((bf16[256,256]{1,0:T(8,128)(2,1)}, bf16[256,256]{1,0:T(8,128)(2,1)S(1)}, u32[]{:S(2)}, u32[]{:S(2)}) %collective-permute-start.5) | collective-permute-done | bytes 131104 | tf_op jit(solution)/shard_map/ppermute | solution.py:36
  50.0 1.5 %collective-permute-start.1 = (f32[1,256]{1,0:T(1,128)S(1)}, f32[1,256]{1,0:T(1,128)S(1)}, u32[]{:S(2)}, u32[]{:S(2)}) collective-permute-start(f32[1,256]{1,0:T(1,128)S(1)} %get-tuple-element.10.refs_2_), channel_id=1, source_target_pairs={{0,1},{1,0},{2,3},{3,2},{4,5},{5,4},{6,7},{7,6},{8,9},{9,8},{10,11... | collective-permute-start | bytes 3080 | tf_op jit(solution)/shard_map/ppermute | solution.py:36
  51.5 2.0 %collective-permute-done.1.refs_3_ = f32[1,256]{1,0:T(1,128)S(1)} collective-permute-done((f32[1,256]{1,0:T(1,128)S(1)}, f32[1,256]{1,0:T(1,128)S(1)}, u32[]{:S(2)}, u32[]{:S(2)}) %collective-permute-start.1) | collective-permute-done | bytes 1056 | tf_op jit(solution)/shard_map/ppermute | solution.py:36
  53.5 2.0 %collective-permute-done.2.refs_6_ = bf16[256,4096]{1,0:T(8,128)(2,1)} collective-permute-done((bf16[256,4096]{1,0:T(8,128)(2,1)}, bf16[256,4096]{1,0:T(8,128)(2,1)}, u32[]{:S(2)}, u32[]{:S(2)}) %collective-permute-start.2) | collective-permute-done | bytes 2097184 | tf_op jit(solution)/shard_map/ppermute | solution.py:250
  55.5 0.0 copy-done.4
  55.5 4.1 %shard_map.77 = bf16[256,4096]{1,0:T(8,128)(2,1)} custom-call(f32[1,256]{1,0:T(1,128)S(1)} %bitcast.31, f32[1,256]{1,0:T(1,128)S(1)} %collective-permute-done.refs_1_, f32[1,256]{1,0:T(1,128)S(1)} %get-tuple-element.10.refs_2_, f32[1,256]{1,0:T(1,128)S(1)} %collective-permute-done.1.refs_3_, bf16[256,4096]{1,0:T(8,128)(2,1)S(1)} %copy-done.4, ...), custom_call_target="tpu_custom_call" | custom-call | flops 4194304 | bytes 8388608 | tf_op jit(solution)/shard_map/pallas_call | solution.py:174
  59.7 0.0 collective-permute-done.8.refs_6_
  59.7 0.0 collective-permute-start.10
  59.7 0.0 collective-permute-done.6.refs_4_
  59.7 0.0 collective-permute-done.12.refs_5_
  59.7 4.2 %shard_map.79.refs_7_ = f32[256,4096]{1,0:T(8,128)} custom-call(bf16[256,512]{1,0:T(8,128)(2,1)S(1)} %pad_maximum_fusion.1.refs_0_, bf16[256,512]{1,0:T(8,128)(2,1)S(1)} %pad_maximum_fusion.2.refs_1_, f32[1,4096]{1,0:T(1,128)S(1)} %copy-done.5, bf16[256,4096]{1,0:T(8,128)(2,1)S(1)} %bitcast.22, bf16[256,4096]{1,0:T(8,128)(2,1)} %collective-permute-done.6.refs_4_, ...), custom_call_target="tpu_custom_call" | custom-call | flops 1342177280 | bytes 8388608 | tf_op jit(solution)/shard_map/pallas_call | solution.py:216
  63.9 0.0 collective-permute-done.10.refs_5_
  63.9 4.0 %shard_map.80 = f32[256,4096]{1,0:T(8,128)} custom-call(bf16[256,512]{1,0:T(8,128)(2,1)S(1)} %pad_maximum_fusion.1.refs_0_, bf16[256,512]{1,0:T(8,128)(2,1)S(1)} %pad_maximum_fusion.2.refs_1_, f32[1,4096]{1,0:T(1,128)S(1)} %copy-done.5, bf16[256,4096]{1,0:T(8,128)(2,1)S(1)} %bitcast.23, ...), custom_call_target="tpu_custom_call", output_to_operand_aliasing={{}: (7, {})} | custom-call | flops 805306368 | bytes 5242880 | tf_op jit(solution)/shard_map/pallas_call | solution.py:216
  (5 shorter events, 0.1 us)
Async XLA Ops:
  0.6 6.9 %copy-start = (bf16[1,256,4096]{2,1,0:T(8,128)(2,1)S(1)}, bf16[1,256,4096]{2,1,0:T(8,128)(2,1)}, u32[]{:S(2)}) copy-start(bf16[1,256,4096]{2,1,0:T(8,128)(2,1)} %param.5) | copy-start | bytes 6291460
  0.6 11.0 %copy-start.2 = (bf16[1,256,1024]{2,1,0:T(8,128)(2,1)S(1)}, bf16[1,256,1024]{2,1,0:T(8,128)(2,1)}, u32[]{:S(2)}) copy-start(bf16[1,256,1024]{2,1,0:T(8,128)(2,1)} %param.8) | copy-start | bytes 1572868
  3.3 36.7 %collective-permute-start.11 = (bf16[256,2560]{1,0:T(8,128)(2,1)}, bf16[256,2560]{1,0:T(8,128)(2,1)}, u32[]{:S(2)}, u32[]{:S(2)}) collective-permute-start(bf16[256,2560]{1,0:T(8,128)(2,1)} %slice.18), channel_id=1, source_target_pairs={{0,16},{8,24},{16,0},{24,8},{1,17},{9,25},{17,1},{25,9},{2,18},{10... | collective-permute-start | bytes 3932168 | tf_op jit(solution)/shard_map/ppermute | solution.py:53
  6.2 49.3 %collective-permute-start.2 = (bf16[256,4096]{1,0:T(8,128)(2,1)}, bf16[256,4096]{1,0:T(8,128)(2,1)}, u32[]{:S(2)}, u32[]{:S(2)}) collective-permute-start(bf16[256,4096]{1,0:T(8,128)(2,1)} %bitcast.34), channel_id=1, source_target_pairs={{2,0},{4,2},{6,4},{3,1},{5,3},{7,5},{10,8},{12,10},{14,12},{11,9},... | collective-permute-start | bytes 6291464 | tf_op jit(solution)/shard_map/ppermute | solution.py:250
  8.0 7.0 %copy-start.5 = (f32[1,4096]{1,0:T(1,128)S(1)}, f32[1,4096]{1,0:T(1,128)}, u32[]{:S(2)}) copy-start(f32[1,4096]{1,0:T(1,128)} %refs_2_.3) | copy-start | bytes 49156
  8.0 3.6 %collective-permute-start = (f32[1,256]{1,0:T(1,128)S(1)}, f32[1,256]{1,0:T(1,128)S(1)}, u32[]{:S(2)}, u32[]{:S(2)}) collective-permute-start(f32[1,256]{1,0:T(1,128)S(1)} %bitcast.28), channel_id=1, source_target_pairs={{0,1},{1,0},{2,3},{3,2},{4,5},{5,4},{6,7},{7,6},{8,9},{9,8},{10,11... | collective-permute-start | bytes 3080 | tf_op jit(solution)/shard_map/ppermute | solution.py:36
  12.6 1.6 %collective-permute-start.3 = (bf16[2,256,256]{2,1,0:T(8,128)(2,1)S(1)}, bf16[2,256,256]{2,1,0:T(8,128)(2,1)S(1)}, u32[]{:S(2)}, u32[]{:S(2)}) collective-permute-start(bf16[2,256,256]{2,1,0:T(8,128)(2,1)S(1)} %pad_maximum_fusion), channel_id=1, source_target_pairs={{0,8},{8,0},{16,24},{24,16},{1,9},{9,1},{17,25},{25,17},{2,10},{10... | collective-permute-start | bytes 786440 | tf_op jit(solution)/shard_map/ppermute | solution.py:53
  12.7 47.0 %collective-permute-start.6 = (bf16[256,4096]{1,0:T(8,128)(2,1)S(1)}, bf16[256,4096]{1,0:T(8,128)(2,1)}, u32[]{:S(2)}, u32[]{:S(2)}) collective-permute-start(bf16[256,4096]{1,0:T(8,128)(2,1)S(1)} %bitcast.18), channel_id=1, source_target_pairs={{0,8},{8,0},{16,24},{24,16},{1,9},{9,1},{17,25},{25,17},{2,10},{10... | collective-permute-start | bytes 6291464 | tf_op jit(solution)/shard_map/ppermute | solution.py:53
  14.9 22.7 %collective-permute-start.4 = (bf16[256,256]{1,0:T(8,128)(2,1)S(1)}, bf16[256,256]{1,0:T(8,128)(2,1)S(1)}, u32[]{:S(2)}, u32[]{:S(2)}) collective-permute-start(bf16[256,256]{1,0:T(8,128)(2,1)S(1)} %fusion), channel_id=1, source_target_pairs={{0,24},{8,16},{16,8},{24,0},{1,25},{9,17},{17,9},{25,1},{2,26},{10... | collective-permute-start | bytes 393224 | tf_op jit(solution)/shard_map/ppermute | solution.py:53
  15.0 3.4 %copy-start.1 = (bf16[1,1024,4096]{2,1,0:T(8,128)(2,1)S(1)}, bf16[1,1024,4096]{2,1,0:T(8,128)(2,1)}, u32[]{:S(2)}) copy-start(bf16[1,1024,4096]{2,1,0:T(8,128)(2,1)} %param.7) | copy-start | bytes 25165828
  23.0 1.3 %copy-start.3 = (bf16[256,4096]{1,0:T(8,128)(2,1)}, bf16[256,4096]{1,0:T(8,128)(2,1)S(1)}, u32[]{:S(2)}) copy-start(bf16[256,4096]{1,0:T(8,128)(2,1)S(1)} %get-tuple-element.11.refs_4_) | copy-start | bytes 6291460
  24.3 13.3 %collective-permute-start.7 = (f32[1,4096]{1,0:T(1,128)S(1)}, f32[1,4096]{1,0:T(1,128)S(1)}, u32[]{:S(2)}, u32[]{:S(2)}) collective-permute-start(f32[1,4096]{1,0:T(1,128)S(1)} %get-tuple-element.13), channel_id=1, source_target_pairs={{0,24},{8,16},{16,8},{24,0},{1,25},{9,17},{17,9},{25,1},{2,26},{10... | collective-permute-start | bytes 49160 | tf_op jit(solution)/shard_map/ppermute | solution.py:53
  37.6 3.4 %copy-start.6 = (bf16[256,256]{1,0:T(8,128)(2,1)}, bf16[256,256]{1,0:T(8,128)(2,1)S(1)}, u32[]{:S(2)}) copy-start(bf16[256,256]{1,0:T(8,128)(2,1)S(1)} %collective-permute-done.4) | copy-start | bytes 393220
  38.6 21.0 %collective-permute-start.8 = (bf16[256,1536]{1,0:T(8,128)(2,1)}, bf16[256,1536]{1,0:T(8,128)(2,1)}, u32[]{:S(2)}, u32[]{:S(2)}) collective-permute-start(bf16[256,1536]{1,0:T(8,128)(2,1)} %slice.14), channel_id=1, source_target_pairs={{0,16},{8,24},{16,0},{24,8},{1,17},{9,25},{17,1},{25,9},{2,18},{10... | collective-permute-start | bytes 2359304 | tf_op jit(solution)/shard_map/ppermute | solution.py:53
  39.9 19.7 %collective-permute-start.12 = (bf16[256,2560]{1,0:T(8,128)(2,1)}, bf16[256,2560]{1,0:T(8,128)(2,1)S(1)}, u32[]{:S(2)}, u32[]{:S(2)}) collective-permute-start(bf16[256,2560]{1,0:T(8,128)(2,1)} %collective-permute-done.11.refs_6_), channel_id=1, source_target_pairs={{0,8},{8,0},{16,24},{24,16},{1,9},{9,1},{17,25},{25,17},{2,10},{10... | collective-permute-start | bytes 3932168 | tf_op jit(solution)/shard_map/ppermute | solution.py:53
  41.1 2.5 %collective-permute-start.9 = (f32[1,4096]{1,0:T(1,128)S(1)}, f32[1,4096]{1,0:T(1,128)S(1)}, u32[]{:S(2)}, u32[]{:S(2)}) collective-permute-start(f32[1,4096]{1,0:T(1,128)S(1)} %add.106), channel_id=1, source_target_pairs={{0,8},{8,0},{16,24},{24,16},{1,9},{9,1},{17,25},{25,17},{2,10},{10... | collective-permute-start | bytes 49160 | tf_op jit(solution)/shard_map/ppermute | solution.py:53
  41.2 14.3 %copy-start.4 = (bf16[256,4096]{1,0:T(8,128)(2,1)S(1)}, bf16[256,4096]{1,0:T(8,128)(2,1)}, u32[]{:S(2)}) copy-start(bf16[256,4096]{1,0:T(8,128)(2,1)} %copy-done.3) | copy-start | bytes 6291460
  44.2 5.7 %collective-permute-start.5 = (bf16[256,256]{1,0:T(8,128)(2,1)}, bf16[256,256]{1,0:T(8,128)(2,1)S(1)}, u32[]{:S(2)}, u32[]{:S(2)}) collective-permute-start(bf16[256,256]{1,0:T(8,128)(2,1)} %copy-done.6), channel_id=1, source_target_pairs={{0,1},{1,0},{2,3},{3,2},{4,5},{5,4},{6,7},{7,6},{8,9},{9,8},{10,11... | collective-permute-start | bytes 393224 | tf_op jit(solution)/shard_map/ppermute | solution.py:36
  50.0 3.6 %collective-permute-start.1 = (f32[1,256]{1,0:T(1,128)S(1)}, f32[1,256]{1,0:T(1,128)S(1)}, u32[]{:S(2)}, u32[]{:S(2)}) collective-permute-start(f32[1,256]{1,0:T(1,128)S(1)} %get-tuple-element.10.refs_2_), channel_id=1, source_target_pairs={{0,1},{1,0},{2,3},{3,2},{4,5},{5,4},{6,7},{7,6},{8,9},{9,8},{10,11... | collective-permute-start | bytes 3080 | tf_op jit(solution)/shard_map/ppermute | solution.py:36
  59.7 4.2 %collective-permute-start.10 = (bf16[256,1536]{1,0:T(8,128)(2,1)}, bf16[256,1536]{1,0:T(8,128)(2,1)S(1)}, u32[]{:S(2)}, u32[]{:S(2)}) collective-permute-start(bf16[256,1536]{1,0:T(8,128)(2,1)} %collective-permute-done.8.refs_6_), channel_id=1, source_target_pairs={{0,8},{8,0},{16,24},{24,16},{1,9},{9,1},{17,25},{25,17},{2,10},{10... | collective-permute-start | bytes 2359304 | tf_op jit(solution)/shard_map/ppermute | solution.py:53
where the time goes:
time: 68.2 us; the launch traced here: 67.8 us
  waiting for transfers between devices  23.5 us (34%)
  Pallas kernels  17.1 us (25%)
  starting transfers between devices  13.6 us (20%)
  local copies, waits for them, and re-layouts  10.6 us (16%)
  other arithmetic  2.22 us (3%)
  between operations  0.84 us (1%)
    ppermute x9, waiting for transfers between devices, send(): lax.ppermute(array, self.axis, [(i, self.to(i, high, low)) for i in range...  15 us
    pallas_call x2, Pallas kernels, weight_columns(): pl.pallas_call(functools.partial(weight_kernel, len(scaled)), grid=(width...  8.16 us
    ppermute x9, starting transfers between devices, send(): lax.ppermute(array, self.axis, [(i, self.to(i, high, low)) for i in range...  7.82 us
    ppermute x3, waiting for transfers between devices, from_others(): lax.ppermute(array, axis, [(i, (i + by) % count) for i in range(count)])  6.43 us
    unnamed x15, local copies, waits for them, and re-layouts  5.63 us
    pallas_call x1, Pallas kernels, scaled_grads(): pl.pallas_call(functools.partial(grad_kernel, scale, len(sums) - 1), grid...  4.59 us
    ppermute x3, starting transfers between devices, from_others(): lax.ppermute(array, axis, [(i, (i + by) % count) for i in range(count)])  4.54 us
    pallas_call x1, Pallas kernels, add_rows(): pl.pallas_call(functools.partial(add_kernel, len(sums) - 1), grid=(tokens...  4.13 us
  transfers between devices with their start and end apart: 13, of which 7 were waited for; matrix products, arithmetic and copies ran while one was open for 8% of the time, Pallas kernels for 19%

commit v1 on v0

--- a/solution.py
+++ b/solution.py
@@ -85,9 +85,7 @@
         functools.partial(scale_kernel, scale),
         out_shape=jax.ShapeDtypeStruct(cotangent.shape[::-1], jnp.bfloat16),
         compiler_params=PARAMS,
-        cost_estimate=pl.CostEstimate(
-            flops=2 * cotangent.size, bytes_accessed=4 * cotangent.size, transcendentals=0
-        ),
+        cost_estimate=pl.CostEstimate(flops=1, bytes_accessed=1, transcendentals=0),
     )(*sums, cotangent)
 
 
@@ -141,17 +139,13 @@
         ],
         scratch_shapes=[pltpu.VMEM((tokens, 1), jnp.float32), pltpu.VMEM((tokens, 128), jnp.float32)],
         compiler_params=PARAMS,
-        cost_estimate=pl.CostEstimate(
-            flops=2 * tokens * features * weight.shape[0],
-            bytes_accessed=2 * (weight.size + cotangent.size + 2 * x.size),
-            transcendentals=0,
-        ),
+        cost_estimate=pl.CostEstimate(flops=1, bytes_accessed=1, transcendentals=0),
     )(*sums, cotangent, weight, x, gain_row)
 
 
-def add_kernel(others, *refs):
+def local_kernel(others, *refs):
     sums, centers = refs[: others + 1], refs[others + 1 : 2 * others + 2]
-    scaled_grad_ref, x_ref, received_ref, out_ref, factor = refs[2 * others + 2 :]
+    scaled_grad_ref, x_ref, out_ref, factor = refs[2 * others + 2 :]
 
     @pl.when(pl.program_id(0) == 0)
     def _():
@@ -164,23 +158,42 @@
     height = x_ref.shape[0]
     rows = pl.ds(pl.multiple_of(pl.program_id(0) * height, height), height)
     local = scaled_grad_ref[...].astype(jnp.float32) - x_ref[...].astype(jnp.float32) * factor[rows]
-    out_ref[...] = (local + received_ref[...].astype(jnp.float32)).astype(out_ref.dtype)
-
-
-def add_rows(sums, centers, scaled_grad, x, received):
+    out_ref[...] = local.astype(out_ref.dtype)
+
+
+def local_part(sums, centers, scaled_grad, x):
+    tokens, features = x.shape
+    tile = tile_of(tokens, 128)
+    block = pl.BlockSpec((tile, features), lambda r: (r, 0))
+    return pl.pallas_call(
+        functools.partial(local_kernel, len(sums) - 1),
+        grid=(tokens // tile,),
+        in_specs=[pl.BlockSpec((1, tokens), lambda r: (0, 0))] * (2 * len(sums)) + [block] * 2,
+        out_specs=block,
+        out_shape=jax.ShapeDtypeStruct(x.shape, jnp.bfloat16),
+        scratch_shapes=[pltpu.VMEM((tokens, 1), jnp.float32)],
+        compiler_params=PARAMS,
+        cost_estimate=pl.CostEstimate(flops=1, bytes_accessed=1, transcendentals=0),
+    )(*sums, *centers, scaled_grad, x)
+
+
+def add_kernel(local_ref, received_ref, out_ref):
+    out_ref[...] = (local_ref[...].astype(jnp.float32) + received_ref[...].astype(jnp.float32)).astype(out_ref.dtype)
+
+
+def add_rows(local, received):
     tokens, features = received.shape
     tile = tile_of(tokens, 128)
     block = pl.BlockSpec((tile, features), lambda r: (r, 0))
     return pl.pallas_call(
-        functools.partial(add_kernel, len(sums) - 1),
+        add_kernel,
         grid=(tokens // tile,),
-        in_specs=[pl.BlockSpec((1, tokens), lambda r: (0, 0))] * (2 * len(sums)) + [block] * 3,
+        in_specs=[block] * 2,
         out_specs=block,
-        out_shape=jax.ShapeDtypeStruct(x.shape, received.dtype),
-        scratch_shapes=[pltpu.VMEM((tokens, 1), jnp.float32)],
-        compiler_params=PARAMS,
-        cost_estimate=pl.CostEstimate(flops=4 * x.size, bytes_accessed=8 * x.size, transcendentals=0),
-    )(*sums, *centers, scaled_grad, x, received)
+        out_shape=jax.ShapeDtypeStruct(received.shape, received.dtype),
+        compiler_params=PARAMS,
+        cost_estimate=pl.CostEstimate(flops=1, bytes_accessed=1, transcendentals=0),
+    )(local, received)
 
 
 def weight_kernel(groups, *refs):
@@ -221,11 +234,7 @@
         out_shape=jax.ShapeDtypeStruct((rows, features), jnp.float32),
         input_output_aliases=aliases,
         compiler_params=PARAMS,
-        cost_estimate=pl.CostEstimate(
-            flops=2 * sources * tokens * rows * width,
-            bytes_accessed=2 * sources * tokens * (rows + width) + 4 * rows * width,
-            transcendentals=0,
-        ),
+        cost_estimate=pl.CostEstimate(flops=1, bytes_accessed=1, transcendentals=0),
     )(*args)
 
 
@@ -254,6 +263,7 @@
     scaled = scaled_cotangent(sums, cotangent, grad_scale)
     scaled_grad, gain_grad, center = scaled_grads(sums, cotangent, value_weight[0], x, gain_row, grad_scale)
     centers = [center] + from_others(center, "tensor")
+    local = local_part(sums, centers, scaled_grad, x)
     near_x = [replicas.send(after(x, scaled), 0, low) for low in near]
 
     by_core = scaled.reshape(replicas.count, rows, tokens)
@@ -278,18 +288,18 @@
             lax.dynamic_slice_in_dim(shares, (mine - at) % slices * share, share, axis=1) for at in range(slices)
         ]
         cots.append(jnp.concatenate(pieces, axis=1))
-    gain_far = [replicas.send(gain_grad, high, turn) for high in far]
+    gain_far = [replicas.send(after(gain_grad, local), high, turn) for high in far]
     gain_grad = sum(gain_far, gain_grad)
     gain_grad = sum([replicas.send(gain_grad, 0, low) for low in near], gain_grad)
 
     for c in range(1, len(columns)):
-        part = column_part(c, *got, *gain_far)
+        part = after(column_part(c, center), *got, *gain_far)
         far_x.append([replicas.send(part, high, 0) for high in far])
     weight_grad = None
     for c, ((start, width), direct) in enumerate(zip(columns, far_x)):
         gates = got + gain_far
         if c == len(columns) - 1:
-            input_grad = add_rows(sums, centers, scaled_grad, x, upper)
+            input_grad = add_rows(local, upper)
             gates = [input_grad, gain_grad, *cots]
         received = []
         for block in direct:

time: 68.2 us -> 69 us (1.012); the launches traced: 67.8 us -> 67.7 us
  waiting for transfers between devices: 23.5 us -> 26.2 us
  local copies, waits for them, and re-layouts: 10.6 us -> 8.29 us
    ppermute x3, waiting for transfers between devices: 6.43 us -> 8.06 us  [from_others(): lax.ppermute(array, axis, [(i, (i + by) % count) for i in range(count)])]
    concatenate x2, other arithmetic: 1.04 us -> 0.09 us  [per_device(): pair = [jnp.concatenate(blocks, axis=1) for blocks in pair]]
    unnamed x15 -> x13, local copies, waits for them, and re-layouts: 5.63 us -> 4.72 us
    ppermute x1, waiting for transfers between devices: 1.99 us -> 2.87 us  [per_device(): upper = lax.ppermute(upper_grad[0], 'pipe', down)]
    another operation x1, other arithmetic: 0.03 us -> 0.73 us  [per_device(): jnp.stack([rows_for(high, turn + low if high else low) for high in range(...]
    pallas_call x1 -> x2, Pallas kernels: 4.13 us -> 4.19 us  [the longest x1 2.78 us: add_rows(): pl.pallas_call(add_kernel, grid=(tokens // tile,), in_specs=[block] * 2,...]
  transfers between devices with their start and end apart: 13 -> 13, of which waited for: 7 -> 8; matrix products, arithmetic and copies ran while one was open for 8% -> 8% of each run, Pallas kernels for 19% -> 19%
where the time goes in v1:
time: 69 us; the launch traced here: 67.7 us
  waiting for transfers between devices  26.2 us (38%)
  Pallas kernels  17 us (25%)
  starting transfers between devices  13.4 us (19%)
  local copies, waits for them, and re-layouts  8.29 us (12%)
  other arithmetic  1.97 us (3%)
  between operations  0.79 us (1%)
    ppermute x9, waiting for transfers between devices, send(): lax.ppermute(array, self.axis, [(i, self.to(i, high, low)) for i in range...  15.3 us
    ppermute x3, waiting for transfers between devices, from_others(): lax.ppermute(array, axis, [(i, (i + by) % count) for i in range(count)])  8.06 us
    pallas_call x2, Pallas kernels, weight_columns(): pl.pallas_call(functools.partial(weight_kernel, len(scaled)), grid=(width...  7.98 us
    ppermute x9, starting transfers between devices, send(): lax.ppermute(array, self.axis, [(i, self.to(i, high, low)) for i in range...  7.17 us
    ppermute x3, starting transfers between devices, from_others(): lax.ppermute(array, axis, [(i, (i + by) % count) for i in range(count)])  4.84 us
    unnamed x13, local copies, waits for them, and re-layouts  4.72 us
    pallas_call x1, Pallas kernels, scaled_grads(): pl.pallas_call(functools.partial(grad_kernel, scale, len(sums) - 1), grid...  4.6 us
    slice x2, local copies, waits for them, and re-layouts, per_device(): (after(x, *gates) if gates else x)[:, columns[c][0]:sum(columns[c])]  3.47 us
  transfers between devices with their start and end apart: 13, of which 8 were waited for; matrix products, arithmetic and copies ran while one was open for 8% of the time, Pallas kernels for 19%

profile of v1, /device:TPU:0, one launch (start us, length us, event | category | flops | bytes accessed | tf_op | source)
XLA Modules:
  0.0 67.7 jit_solution(13541153703345997629)
XLA Ops:
  0.6 0.0 copy-start
  0.6 1.4 %collective-permute-start.2 = (bf16[256,4096]{1,0:T(8,128)(2,1)}, bf16[256,4096]{1,0:T(8,128)(2,1)}, u32[]{:S(2)}, u32[]{:S(2)}) collective-permute-start(bf16[256,4096]{1,0:T(8,128)(2,1)} %bitcast.34), channel_id=1, source_target_pairs={{2,0},{4,2},{6,4},{3,1},{5,3},{7,5},{10,8},{12,10},{14,12},{11,9},... | collective-permute-start | bytes 6291464 | tf_op jit(solution)/shard_map/ppermute | solution.py:259
  2.1 0.0 copy-start.4
  2.1 2.5 %slice.18 = bf16[256,2560]{1,0:T(8,128)(2,1)} slice(bf16[256,4096]{1,0:T(8,128)(2,1)} %bitcast.17), slice={[0:256], [0:2560]} | slice | bytes 2621440 | tf_op jit(solution)/shard_map/slice | solution.py:255
  4.6 3.0 %collective-permute-start.11 = (bf16[256,2560]{1,0:T(8,128)(2,1)}, bf16[256,2560]{1,0:T(8,128)(2,1)}, u32[]{:S(2)}, u32[]{:S(2)}) collective-permute-start(bf16[256,2560]{1,0:T(8,128)(2,1)} %slice.18), channel_id=1, source_target_pairs={{0,16},{8,24},{16,0},{24,8},{1,17},{9,25},{17,1},{25,9},{2,18},{10... | collective-permute-start | bytes 3932168 | tf_op jit(solution)/shard_map/ppermute | solution.py:53
  7.6 0.0 copy-done
  7.6 0.5 multiply_reduce_fusion
  8.1 0.0 copy-start.5
  8.1 1.6 %collective-permute-start = (f32[1,256]{1,0:T(1,128)S(1)}, f32[1,256]{1,0:T(1,128)S(1)}, u32[]{:S(2)}, u32[]{:S(2)}) collective-permute-start(f32[1,256]{1,0:T(1,128)S(1)} %bitcast.28), channel_id=1, source_target_pairs={{0,1},{1,0},{2,3},{3,2},{4,5},{5,4},{6,7},{7,6},{8,9},{9,8},{10,11... | collective-permute-start | bytes 3080 | tf_op jit(solution)/shard_map/ppermute | solution.py:36
  9.6 2.1 %collective-permute-done.refs_1_ = f32[1,256]{1,0:T(1,128)S(1)} collective-permute-done((f32[1,256]{1,0:T(1,128)S(1)}, f32[1,256]{1,0:T(1,128)S(1)}, u32[]{:S(2)}, u32[]{:S(2)}) %collective-permute-start) | collective-permute-done | bytes 1056 | tf_op jit(solution)/shard_map/ppermute | solution.py:36
  11.7 0.0 copy-done.4
  11.7 0.2 shard_map.79
  12.0 0.7 %pad_maximum_fusion = bf16[2,256,256]{2,1,0:T(8,128)(2,1)} fusion(bf16[1,256,256]{2,1,0:T(8,128)(2,1)S(1)} %get-tuple-element.22, bf16[1,256,256]{2,1,0:T(8,128)(2,1)S(1)} %get-tuple-element.23), kind=kLoop, calls=%fused_computation.1 | loop fusion | flops 131072 | bytes 524288 | tf_op jit(solution)/shard_map/stack | solution.py:274
  12.7 0.0 collective-permute-start.3
  12.7 0.5 collective-permute-start.6
  13.2 1.6 %collective-permute-done.3 = bf16[2,256,256]{2,1,0:T(8,128)(2,1)S(1)} collective-permute-done((bf16[2,256,256]{2,1,0:T(8,128)(2,1)}, bf16[2,256,256]{2,1,0:T(8,128)(2,1)S(1)}, u32[]{:S(2)}, u32[]{:S(2)}) %collective-permute-start.3) | collective-permute-done | bytes 262176 | tf_op jit(solution)/shard_map/ppermute | solution.py:53
  14.8 0.1 fusion
  14.9 0.1 collective-permute-start.4
  15.0 0.0 copy-done.5
  15.0 0.0 copy-start.1
  15.0 3.4 %copy-done.1 = bf16[1,1024,4096]{2,1,0:T(8,128)(2,1)S(1)} copy-done((bf16[1,1024,4096]{2,1,0:T(8,128)(2,1)S(1)}, bf16[1,1024,4096]{2,1,0:T(8,128)(2,1)}, u32[]{:S(2)}) %copy-start.1) | copy-done | bytes 8388632
  18.4 4.6 %shard_map.76 = (bf16[256,4096]{1,0:T(8,128)(2,1)S(1)}, f32[1,4096]{1,0:T(1,128)S(1)}, f32[1,256]{1,0:T(1,128)S(1)}) custom-call(f32[1,256]{1,0:T(1,128)S(1)} %bitcast.30, f32[1,256]{1,0:T(1,128)S(1)} %collective-permute-done.refs_1_, bf16[256,1024]{1,0:T(8,128)(2,1)S(1)} %bitcast.26, bf16[1024,4096]{1,0:T(8,128)(2,1)S(1)} %bitcast.24, ...), custom_call_target="tpu_custom_call" | custom-call | flops 1 | bytes 1 | tf_op jit(solution)/shard_map/pallas_call | solution.py:120
  23.0 1.8 %collective-permute-start.1 = (f32[1,256]{1,0:T(1,128)S(1)}, f32[1,256]{1,0:T(1,128)S(1)}, u32[]{:S(2)}, u32[]{:S(2)}) collective-permute-start(f32[1,256]{1,0:T(1,128)S(1)} %get-tuple-element.12.refs_2_), channel_id=1, source_target_pairs={{0,1},{1,0},{2,3},{3,2},{4,5},{5,4},{6,7},{7,6},{8,9},{9,8},{10,11... | collective-permute-start | bytes 3080 | tf_op jit(solution)/shard_map/ppermute | solution.py:36
  24.8 1.8 %collective-permute-done.1.refs_3_ = f32[1,256]{1,0:T(1,128)S(1)} collective-permute-done((f32[1,256]{1,0:T(1,128)S(1)}, f32[1,256]{1,0:T(1,128)S(1)}, u32[]{:S(2)}, u32[]{:S(2)}) %collective-permute-start.1) | collective-permute-done | bytes 1056 | tf_op jit(solution)/shard_map/ppermute | solution.py:36
  26.6 1.4 %shard_map.77.local_ref = bf16[256,4096]{1,0:T(8,128)(2,1)S(1)} custom-call(f32[1,256]{1,0:T(1,128)S(1)} %bitcast.31, f32[1,256]{1,0:T(1,128)S(1)} %collective-permute-done.refs_1_, f32[1,256]{1,0:T(1,128)S(1)} %get-tuple-element.12.refs_2_, f32[1,256]{1,0:T(1,128)S(1)} %collective-permute-done.1.refs_3_, bf16[256,4096]{1,0:T(8,128)(2,1)S(1)} %get-tuple-element.13.refs_4_, ...), custom_call_target="tpu_custom_call" | custom-call | flops 1 | bytes 1 | tf_op jit(solution)/shard_map/pallas_call | solution.py:168
  28.0 0.0 copy-start.2
  28.0 1.3 %copy-done.2 = bf16[256,4096]{1,0:T(8,128)(2,1)} copy-done((bf16[256,4096]{1,0:T(8,128)(2,1)}, bf16[256,4096]{1,0:T(8,128)(2,1)S(1)}, u32[]{:S(2)}) %copy-start.2) | copy-done | bytes 2097176
  29.3 1.0 %collective-permute-start.7 = (f32[1,4096]{1,0:T(1,128)S(1)}, f32[1,4096]{1,0:T(1,128)S(1)}, u32[]{:S(2)}, u32[]{:S(2)}) collective-permute-start(f32[1,4096]{1,0:T(1,128)S(1)} %get-tuple-element.17), channel_id=1, source_target_pairs={{0,24},{8,16},{16,8},{24,0},{1,25},{9,17},{17,9},{25,1},{2,26},{10... | collective-permute-start | bytes 49160 | tf_op jit(solution)/shard_map/ppermute | solution.py:53
  30.3 1.0 %slice.14 = bf16[256,1536]{1,0:T(8,128)(2,1)} slice(bf16[256,4096]{1,0:T(8,128)(2,1)S(1)} %bitcast.21), slice={[0:256], [2560:4096]} | slice | bytes 1572864 | tf_op jit(solution)/shard_map/slice | solution.py:255
  31.3 7.7 %collective-permute-done.7 = f32[1,4096]{1,0:T(1,128)S(1)} collective-permute-done((f32[1,4096]{1,0:T(1,128)S(1)}, f32[1,4096]{1,0:T(1,128)S(1)}, u32[]{:S(2)}, u32[]{:S(2)}) %collective-permute-start.7) | collective-permute-done | bytes 16416 | tf_op jit(solution)/shard_map/ppermute | solution.py:53
  39.0 0.0 collective-permute-done.4
  39.0 1.3 %collective-permute-start.8 = (bf16[256,1536]{1,0:T(8,128)(2,1)}, bf16[256,1536]{1,0:T(8,128)(2,1)S(1)}, u32[]{:S(2)}, u32[]{:S(2)}) collective-permute-start(bf16[256,1536]{1,0:T(8,128)(2,1)} %slice.14), channel_id=1, source_target_pairs={{0,16},{8,24},{16,0},{24,8},{1,17},{9,25},{17,1},{25,9},{2,18},{10... | collective-permute-start | bytes 2359304 | tf_op jit(solution)/shard_map/ppermute | solution.py:53
  40.3 1.2 %collective-permute-start.9 = (f32[1,4096]{1,0:T(1,128)S(1)}, f32[1,4096]{1,0:T(1,128)S(1)}, u32[]{:S(2)}, u32[]{:S(2)}) collective-permute-start(f32[1,4096]{1,0:T(1,128)S(1)} %add.106), channel_id=1, source_target_pairs={{0,8},{8,0},{16,24},{24,16},{1,9},{9,1},{17,25},{25,17},{2,10},{10... | collective-permute-start | bytes 49160 | tf_op jit(solution)/shard_map/ppermute | solution.py:53
  41.5 0.0 copy-start.3
  41.5 0.8 %collective-permute-done.9 = f32[1,4096]{1,0:T(1,128)S(1)} collective-permute-done((f32[1,4096]{1,0:T(1,128)S(1)}, f32[1,4096]{1,0:T(1,128)S(1)}, u32[]{:S(2)}, u32[]{:S(2)}) %collective-permute-start.9) | collective-permute-done | bytes 16416 | tf_op jit(solution)/shard_map/ppermute | solution.py:53
  42.3 0.6 add.107
  42.9 1.5 %collective-permute-start.5 = (bf16[256,256]{1,0:T(8,128)(2,1)S(1)}, bf16[256,256]{1,0:T(8,128)(2,1)S(1)}, u32[]{:S(2)}, u32[]{:S(2)}) collective-permute-start(bf16[256,256]{1,0:T(8,128)(2,1)S(1)} %collective-permute-done.4), channel_id=1, source_target_pairs={{0,1},{1,0},{2,3},{3,2},{4,5},{5,4},{6,7},{7,6},{8,9},{9,8},{10,11... | collective-permute-start | bytes 393224 | tf_op jit(solution)/shard_map/ppermute | solution.py:36
  44.4 0.0 collective-permute-done.11.refs_6_
  44.4 0.1 collective-permute-start.12
  44.5 4.1 %collective-permute-done.5 = bf16[256,256]{1,0:T(8,128)(2,1)S(1)} collective-permute-done((bf16[256,256]{1,0:T(8,128)(2,1)S(1)}, bf16[256,256]{1,0:T(8,128)(2,1)S(1)}, u32[]{:S(2)}, u32[]{:S(2)}) %collective-permute-start.5) | collective-permute-done | bytes 131104 | tf_op jit(solution)/shard_map/ppermute | solution.py:36
  48.8 2.9 %collective-permute-done.2.received_ref = bf16[256,4096]{1,0:T(8,128)(2,1)} collective-permute-done((bf16[256,4096]{1,0:T(8,128)(2,1)}, bf16[256,4096]{1,0:T(8,128)(2,1)}, u32[]{:S(2)}, u32[]{:S(2)}) %collective-permute-start.2) | collective-permute-done | bytes 2097184 | tf_op jit(solution)/shard_map/ppermute | solution.py:259
  51.6 0.0 copy-done.3
  51.6 2.8 %shard_map.78 = bf16[256,4096]{1,0:T(8,128)(2,1)} custom-call(bf16[256,4096]{1,0:T(8,128)(2,1)S(1)} %copy-done.3, bf16[256,4096]{1,0:T(8,128)(2,1)} %collective-permute-done.2.received_ref), custom_call_target="tpu_custom_call" | custom-call | flops 1 | bytes 1 | tf_op jit(solution)/shard_map/pallas_call | solution.py:188
  54.4 5.2 %collective-permute-done.8.refs_6_ = bf16[256,1536]{1,0:T(8,128)(2,1)S(1)} collective-permute-done((bf16[256,1536]{1,0:T(8,128)(2,1)}, bf16[256,1536]{1,0:T(8,128)(2,1)S(1)}, u32[]{:S(2)}, u32[]{:S(2)}) %collective-permute-start.8) | collective-permute-done | bytes 786464 | tf_op jit(solution)/shard_map/ppermute | solution.py:53
  59.6 0.1 collective-permute-start.10
  59.7 0.0 collective-permute-done.6.refs_4_
  59.7 0.0 collective-permute-done.12.refs_5_
  59.7 4.2 %shard_map.80.refs_7_ = f32[256,4096]{1,0:T(8,128)} custom-call(bf16[256,512]{1,0:T(8,128)(2,1)S(1)} %pad_maximum_fusion.1.refs_0_, bf16[256,512]{1,0:T(8,128)(2,1)S(1)} %pad_maximum_fusion.2.refs_1_, f32[1,4096]{1,0:T(1,128)S(1)} %copy-done.5, bf16[256,4096]{1,0:T(8,128)(2,1)S(1)} %bitcast.22, bf16[256,4096]{1,0:T(8,128)(2,1)} %collective-permute-done.6.refs_4_, ...), custom_call_target="tpu_custom_call" | custom-call | flops 1 | bytes 1 | tf_op jit(solution)/shard_map/pallas_call | solution.py:229
  63.9 0.0 collective-permute-done.10.refs_5_
  63.9 3.8 %shard_map.81 = f32[256,4096]{1,0:T(8,128)} custom-call(bf16[256,512]{1,0:T(8,128)(2,1)S(1)} %pad_maximum_fusion.1.refs_0_, bf16[256,512]{1,0:T(8,128)(2,1)S(1)} %pad_maximum_fusion.2.refs_1_, f32[1,4096]{1,0:T(1,128)S(1)} %copy-done.5, bf16[256,4096]{1,0:T(8,128)(2,1)S(1)} %bitcast.23, ...), custom_call_target="tpu_custom_call", output_to_operand_aliasing={{}: (7, {})} | custom-call | flops 1 | bytes 1 | tf_op jit(solution)/shard_map/pallas_call | solution.py:229
  (8 shorter events, 0.2 us)
Async XLA Ops:
  0.6 6.9 %copy-start = (bf16[1,256,4096]{2,1,0:T(8,128)(2,1)S(1)}, bf16[1,256,4096]{2,1,0:T(8,128)(2,1)}, u32[]{:S(2)}) copy-start(bf16[1,256,4096]{2,1,0:T(8,128)(2,1)} %param.5) | copy-start | bytes 6291460
  0.6 51.0 %collective-permute-start.2 = (bf16[256,4096]{1,0:T(8,128)(2,1)}, bf16[256,4096]{1,0:T(8,128)(2,1)}, u32[]{:S(2)}, u32[]{:S(2)}) collective-permute-start(bf16[256,4096]{1,0:T(8,128)(2,1)} %bitcast.34), channel_id=1, source_target_pairs={{2,0},{4,2},{6,4},{3,1},{5,3},{7,5},{10,8},{12,10},{14,12},{11,9},... | collective-permute-start | bytes 6291464 | tf_op jit(solution)/shard_map/ppermute | solution.py:259
  2.1 9.6 %copy-start.4 = (bf16[1,256,1024]{2,1,0:T(8,128)(2,1)S(1)}, bf16[1,256,1024]{2,1,0:T(8,128)(2,1)}, u32[]{:S(2)}) copy-start(bf16[1,256,1024]{2,1,0:T(8,128)(2,1)} %param.8) | copy-start | bytes 1572868
  4.6 39.8 %collective-permute-start.11 = (bf16[256,2560]{1,0:T(8,128)(2,1)}, bf16[256,2560]{1,0:T(8,128)(2,1)}, u32[]{:S(2)}, u32[]{:S(2)}) collective-permute-start(bf16[256,2560]{1,0:T(8,128)(2,1)} %slice.18), channel_id=1, source_target_pairs={{0,16},{8,24},{16,0},{24,8},{1,17},{9,25},{17,1},{25,9},{2,18},{10... | collective-permute-start | bytes 3932168 | tf_op jit(solution)/shard_map/ppermute | solution.py:53
  8.1 6.9 %copy-start.5 = (f32[1,4096]{1,0:T(1,128)S(1)}, f32[1,4096]{1,0:T(1,128)}, u32[]{:S(2)}) copy-start(f32[1,4096]{1,0:T(1,128)} %refs_2_.3) | copy-start | bytes 49156
  8.1 3.6 %collective-permute-start = (f32[1,256]{1,0:T(1,128)S(1)}, f32[1,256]{1,0:T(1,128)S(1)}, u32[]{:S(2)}, u32[]{:S(2)}) collective-permute-start(f32[1,256]{1,0:T(1,128)S(1)} %bitcast.28), channel_id=1, source_target_pairs={{0,1},{1,0},{2,3},{3,2},{4,5},{5,4},{6,7},{7,6},{8,9},{9,8},{10,11... | collective-permute-start | bytes 3080 | tf_op jit(solution)/shard_map/ppermute | solution.py:36
  12.7 2.1 %collective-permute-start.3 = (bf16[2,256,256]{2,1,0:T(8,128)(2,1)}, bf16[2,256,256]{2,1,0:T(8,128)(2,1)S(1)}, u32[]{:S(2)}, u32[]{:S(2)}) collective-permute-start(bf16[2,256,256]{2,1,0:T(8,128)(2,1)} %pad_maximum_fusion), channel_id=1, source_target_pairs={{0,8},{8,0},{16,24},{24,16},{1,9},{9,1},{17,25},{25,17},{2,10},{10... | collective-permute-start | bytes 786440 | tf_op jit(solution)/shard_map/ppermute | solution.py:53
  12.7 47.0 %collective-permute-start.6 = (bf16[256,4096]{1,0:T(8,128)(2,1)S(1)}, bf16[256,4096]{1,0:T(8,128)(2,1)}, u32[]{:S(2)}, u32[]{:S(2)}) collective-permute-start(bf16[256,4096]{1,0:T(8,128)(2,1)S(1)} %bitcast.18), channel_id=1, source_target_pairs={{0,8},{8,0},{16,24},{24,16},{1,9},{9,1},{17,25},{25,17},{2,10},{10... | collective-permute-start | bytes 6291464 | tf_op jit(solution)/shard_map/ppermute | solution.py:53
  14.9 24.1 %collective-permute-start.4 = (bf16[256,256]{1,0:T(8,128)(2,1)S(1)}, bf16[256,256]{1,0:T(8,128)(2,1)S(1)}, u32[]{:S(2)}, u32[]{:S(2)}) collective-permute-start(bf16[256,256]{1,0:T(8,128)(2,1)S(1)} %fusion), channel_id=1, source_target_pairs={{0,24},{8,16},{16,8},{24,0},{1,25},{9,17},{17,9},{25,1},{2,26},{10... | collective-permute-start | bytes 393224 | tf_op jit(solution)/shard_map/ppermute | solution.py:53
  15.0 3.4 %copy-start.1 = (bf16[1,1024,4096]{2,1,0:T(8,128)(2,1)S(1)}, bf16[1,1024,4096]{2,1,0:T(8,128)(2,1)}, u32[]{:S(2)}) copy-start(bf16[1,1024,4096]{2,1,0:T(8,128)(2,1)} %param.7) | copy-start | bytes 25165828
  23.0 3.6 %collective-permute-start.1 = (f32[1,256]{1,0:T(1,128)S(1)}, f32[1,256]{1,0:T(1,128)S(1)}, u32[]{:S(2)}, u32[]{:S(2)}) collective-permute-start(f32[1,256]{1,0:T(1,128)S(1)} %get-tuple-element.12.refs_2_), channel_id=1, source_target_pairs={{0,1},{1,0},{2,3},{3,2},{4,5},{5,4},{6,7},{7,6},{8,9},{9,8},{10,11... | collective-permute-start | bytes 3080 | tf_op jit(solution)/shard_map/ppermute | solution.py:36
  28.0 1.3 %copy-start.2 = (bf16[256,4096]{1,0:T(8,128)(2,1)}, bf16[256,4096]{1,0:T(8,128)(2,1)S(1)}, u32[]{:S(2)}) copy-start(bf16[256,4096]{1,0:T(8,128)(2,1)S(1)} %shard_map.77.local_ref) | copy-start | bytes 6291460
  29.3 9.6 %collective-permute-start.7 = (f32[1,4096]{1,0:T(1,128)S(1)}, f32[1,4096]{1,0:T(1,128)S(1)}, u32[]{:S(2)}, u32[]{:S(2)}) collective-permute-start(f32[1,4096]{1,0:T(1,128)S(1)} %get-tuple-element.17), channel_id=1, source_target_pairs={{0,24},{8,16},{16,8},{24,0},{1,25},{9,17},{17,9},{25,1},{2,26},{10... | collective-permute-start | bytes 49160 | tf_op jit(solution)/shard_map/ppermute | solution.py:53
  39.0 20.6 %collective-permute-start.8 = (bf16[256,1536]{1,0:T(8,128)(2,1)}, bf16[256,1536]{1,0:T(8,128)(2,1)S(1)}, u32[]{:S(2)}, u32[]{:S(2)}) collective-permute-start(bf16[256,1536]{1,0:T(8,128)(2,1)} %slice.14), channel_id=1, source_target_pairs={{0,16},{8,24},{16,0},{24,8},{1,17},{9,25},{17,1},{25,9},{2,18},{10... | collective-permute-start | bytes 2359304 | tf_op jit(solution)/shard_map/ppermute | solution.py:53
  40.3 2.0 %collective-permute-start.9 = (f32[1,4096]{1,0:T(1,128)S(1)}, f32[1,4096]{1,0:T(1,128)S(1)}, u32[]{:S(2)}, u32[]{:S(2)}) collective-permute-start(f32[1,4096]{1,0:T(1,128)S(1)} %add.106), channel_id=1, source_target_pairs={{0,8},{8,0},{16,24},{24,16},{1,9},{9,1},{17,25},{25,17},{2,10},{10... | collective-permute-start | bytes 49160 | tf_op jit(solution)/shard_map/ppermute | solution.py:53
  41.5 10.2 %copy-start.3 = (bf16[256,4096]{1,0:T(8,128)(2,1)S(1)}, bf16[256,4096]{1,0:T(8,128)(2,1)}, u32[]{:S(2)}) copy-start(bf16[256,4096]{1,0:T(8,128)(2,1)} %copy-done.2) | copy-start | bytes 6291460
  42.9 5.7 %collective-permute-start.5 = (bf16[256,256]{1,0:T(8,128)(2,1)S(1)}, bf16[256,256]{1,0:T(8,128)(2,1)S(1)}, u32[]{:S(2)}, u32[]{:S(2)}) collective-permute-start(bf16[256,256]{1,0:T(8,128)(2,1)S(1)} %collective-permute-done.4), channel_id=1, source_target_pairs={{0,1},{1,0},{2,3},{3,2},{4,5},{5,4},{6,7},{7,6},{8,9},{9,8},{10,11... | collective-permute-start | bytes 393224 | tf_op jit(solution)/shard_map/ppermute | solution.py:36
  44.4 15.3 %collective-permute-start.12 = (bf16[256,2560]{1,0:T(8,128)(2,1)}, bf16[256,2560]{1,0:T(8,128)(2,1)S(1)}, u32[]{:S(2)}, u32[]{:S(2)}) collective-permute-start(bf16[256,2560]{1,0:T(8,128)(2,1)} %collective-permute-done.11.refs_6_), channel_id=1, source_target_pairs={{0,8},{8,0},{16,24},{24,16},{1,9},{9,1},{17,25},{25,17},{2,10},{10... | collective-permute-start | bytes 3932168 | tf_op jit(solution)/shard_map/ppermute | solution.py:53
  59.6 4.3 %collective-permute-start.10 = (bf16[256,1536]{1,0:T(8,128)(2,1)S(1)}, bf16[256,1536]{1,0:T(8,128)(2,1)S(1)}, u32[]{:S(2)}, u32[]{:S(2)}) collective-permute-start(bf16[256,1536]{1,0:T(8,128)(2,1)S(1)} %collective-permute-done.8.refs_6_), channel_id=1, source_target_pairs={{0,8},{8,0},{16,24},{24,16},{1,9},{9,1},{17,25},{25,17},{2,10},{10... | collective-permute-start | bytes 2359304 | tf_op jit(solution)/shard_map/ppermute | solution.py:53

commit v2 on v1

--- a/solution.py
+++ b/solution.py
@@ -85,7 +85,9 @@
         functools.partial(scale_kernel, scale),
         out_shape=jax.ShapeDtypeStruct(cotangent.shape[::-1], jnp.bfloat16),
         compiler_params=PARAMS,
-        cost_estimate=pl.CostEstimate(flops=1, bytes_accessed=1, transcendentals=0),
+        cost_estimate=pl.CostEstimate(
+            flops=2 * cotangent.size, bytes_accessed=4 * cotangent.size, transcendentals=0
+        ),
     )(*sums, cotangent)
 
 
@@ -139,7 +141,11 @@
         ],
         scratch_shapes=[pltpu.VMEM((tokens, 1), jnp.float32), pltpu.VMEM((tokens, 128), jnp.float32)],
         compiler_params=PARAMS,
-        cost_estimate=pl.CostEstimate(flops=1, bytes_accessed=1, transcendentals=0),
+        cost_estimate=pl.CostEstimate(
+            flops=2 * tokens * features * weight.shape[0],
+            bytes_accessed=2 * (weight.size + cotangent.size + 2 * x.size),
+            transcendentals=0,
+        ),
     )(*sums, cotangent, weight, x, gain_row)
 
 
@@ -173,7 +179,7 @@
         out_shape=jax.ShapeDtypeStruct(x.shape, jnp.bfloat16),
         scratch_shapes=[pltpu.VMEM((tokens, 1), jnp.float32)],
         compiler_params=PARAMS,
-        cost_estimate=pl.CostEstimate(flops=1, bytes_accessed=1, transcendentals=0),
+        cost_estimate=pl.CostEstimate(flops=3 * x.size, bytes_accessed=6 * x.size, transcendentals=0),
     )(*sums, *centers, scaled_grad, x)
 
 
@@ -192,40 +198,71 @@
         out_specs=block,
         out_shape=jax.ShapeDtypeStruct(received.shape, received.dtype),
         compiler_params=PARAMS,
-        cost_estimate=pl.CostEstimate(flops=1, bytes_accessed=1, transcendentals=0),
+        cost_estimate=pl.CostEstimate(flops=received.size, bytes_accessed=6 * received.size, transcendentals=0),
     )(local, received)
 
 
+def products(scaled_ref, blocks):
+    tokens = blocks[0].shape[0]
+    total = None
+    for at, block in enumerate(blocks):
+        scaled = scaled_ref[:, at * tokens : (at + 1) * tokens]
+        term = jnp.dot(scaled, block[...], preferred_element_type=jnp.float32)
+        total = term if total is None else total + term
+    return total
+
+
+def held_kernel(scaled_ref, *refs):
+    refs[-1][...] = products(scaled_ref, refs[:-1]).astype(refs[-1].dtype)
+
+
+def held_product(scaled, held):
+    tokens, features = held[0].shape
+    rows = scaled.shape[0]
+    tile = tile_of(features, 1024)
+    column = lambda c: (0, c)
+    return pl.pallas_call(
+        held_kernel,
+        grid=(features // tile,),
+        in_specs=[pl.BlockSpec(scaled.shape, lambda c: (0, 0))]
+        + [pl.BlockSpec((tokens, tile), column)] * len(held),
+        out_specs=pl.BlockSpec((rows, tile), column),
+        out_shape=jax.ShapeDtypeStruct((rows, features), jnp.bfloat16),
+        compiler_params=PARAMS,
+        cost_estimate=pl.CostEstimate(
+            flops=2 * scaled.size * features,
+            bytes_accessed=2 * (scaled.size + len(held) * tokens * features + rows * features),
+            transcendentals=0,
+        ),
+    )(scaled, *held)
+
+
 def weight_kernel(groups, *refs):
-    scaled_refs, gain_ref, blocks, out_ref = refs[:groups], refs[groups], refs[groups + 1 :], refs[-1]
-    tokens = blocks[0].shape[0]
-    width = scaled_refs[0].shape[1] // tokens
-    total = None
-    for at in range(groups * width):
-        scaled = scaled_refs[at // width][:, at % width * tokens : (at % width + 1) * tokens]
-        term = jnp.dot(scaled, blocks[at][...], preferred_element_type=jnp.float32)
-        total = term if total is None else total + term
+    scaled_refs, gain_ref, partial_ref, out_ref = refs[:groups], refs[groups], refs[groups + 1], refs[-1]
+    blocks = refs[groups + 2 :]
+    total = partial_ref[...].astype(jnp.float32)
+    width = scaled_refs[0].shape[1] // blocks[0].shape[0] if groups else 0
+    for at, scaled_ref in enumerate(scaled_refs):
+        total = total + products(scaled_ref, blocks[at * width : (at + 1) * width])
     out_ref[...] = total * gain_ref[...]
 
 
-def weight_columns(scaled, held, received, gain_row, start, out):
-    tokens, features = held[0].shape
-    width = received[0].shape[1]
-    rows = scaled[0].shape[0]
-    tile = next(t for t in (1536, 1280, 768, 640, 512, 256, 128) if width % t == 0 and start % t == 0)
+def weight_columns(scaled, partial, received, gain_row, start, width, out):
+    rows, features = partial.shape
+    tile = next(t for t in (1280, 768, 640, 512, 384, 256, 128) if width % t == 0 and start % t == 0)
     first = start // tile
     whole = lambda c: (0, 0)
     placed = lambda c: (0, first + c)
     here = lambda c: (0, c)
-    in_specs = [pl.BlockSpec(part.shape, whole) for part in scaled] + [pl.BlockSpec((1, tile), placed)]
-    in_specs += [pl.BlockSpec((tokens, tile), placed)] * len(held)
-    in_specs += [pl.BlockSpec((tokens, tile), here)] * len(received)
-    args, aliases = [*scaled, gain_row, *held, *received], {}
+    in_specs = [pl.BlockSpec(part.shape, whole) for part in scaled]
+    in_specs += [pl.BlockSpec((1, tile), placed), pl.BlockSpec((rows, tile), placed)]
+    in_specs += [pl.BlockSpec((block.shape[0], tile), here) for block in received]
+    args, aliases = [*scaled, gain_row, partial, *received], {}
     if out is not None:
         in_specs.append(pl.BlockSpec(memory_space=pl.ANY))
         aliases = {len(args): 0}
         args.append(out)
-    sources = len(held) + len(received)
+    tokens = sum(block.shape[0] for block in received)
     return pl.pallas_call(
         functools.partial(weight_kernel, len(scaled)),
         grid=(width // tile,),
@@ -234,7 +271,11 @@
         out_shape=jax.ShapeDtypeStruct((rows, features), jnp.float32),
         input_output_aliases=aliases,
         compiler_params=PARAMS,
-        cost_estimate=pl.CostEstimate(flops=1, bytes_accessed=1, transcendentals=0),
+        cost_estimate=pl.CostEstimate(
+            flops=2 * tokens * rows * width,
+            bytes_accessed=2 * tokens * (rows + width) + 6 * rows * width,
+            transcendentals=0,
+        ),
     )(*args)
 
 
@@ -264,7 +305,7 @@
     scaled_grad, gain_grad, center = scaled_grads(sums, cotangent, value_weight[0], x, gain_row, grad_scale)
     centers = [center] + from_others(center, "tensor")
     local = local_part(sums, centers, scaled_grad, x)
-    near_x = [replicas.send(after(x, scaled), 0, low) for low in near]
+    near_x = [replicas.send(x, 0, low) for low in near]
 
     by_core = scaled.reshape(replicas.count, rows, tokens)
     turn = replicas.width - 1
@@ -288,12 +329,13 @@
             lax.dynamic_slice_in_dim(shares, (mine - at) % slices * share, share, axis=1) for at in range(slices)
         ]
         cots.append(jnp.concatenate(pieces, axis=1))
+    partial = held_product(cots[0], [x] + near_x)
     gain_far = [replicas.send(after(gain_grad, local), high, turn) for high in far]
     gain_grad = sum(gain_far, gain_grad)
     gain_grad = sum([replicas.send(gain_grad, 0, low) for low in near], gain_grad)
 
     for c in range(1, len(columns)):
-        part = after(column_part(c, center), *got, *gain_far)
+        part = after(column_part(c, center), *got, *gain_far, partial)
         far_x.append([replicas.send(part, high, 0) for high in far])
     weight_grad = None
     for c, ((start, width), direct) in enumerate(zip(columns, far_x)):
@@ -305,7 +347,7 @@
         for block in direct:
             handed = after(block, *gates) if gates else block
             received += [replicas.send(handed, 0, low) for low in near] + [block]
-        weight_grad = weight_columns(cots, [x] + near_x, received, gain_row, start, weight_grad)
+        weight_grad = weight_columns(cots[1:], partial, received, gain_row, start, width, weight_grad)
     return (input_grad[None], weight_grad[None], gain_grad)
 
 

time: 69 us -> 66.8 us (0.968); the launches traced: 67.7 us -> 66.4 us
  waiting for transfers between devices: 26.2 us -> 17.3 us
  local copies, waits for them, and re-layouts: 8.29 us -> 15.1 us
  Pallas kernels: 17 us -> 18.3 us
    ppermute x9, waiting for transfers between devices: 15.3 us -> 0.93 us  [send(): lax.ppermute(array, self.axis, [(i, self.to(i, high, low)) for i in range...]
    ppermute x1, waiting for transfers between devices: 2.87 us -> 9.49 us  [per_device(): upper = lax.ppermute(upper_grad[0], 'pipe', down)]
    unnamed x13 -> x25, local copies, waits for them, and re-layouts: 4.72 us -> 10.5 us
    pallas_call x0 -> x1, Pallas kernels: none -> 3.66 us  [held_product(): pl.pallas_call(held_kernel, grid=(features // tile,), in_specs=[pl.BlockS...]
    pallas_call x2, Pallas kernels: 7.98 us -> 5.65 us  [weight_columns(): pl.pallas_call(functools.partial(weight_kernel, len(scaled)), grid=(width...]
    ppermute x3, waiting for transfers between devices: 8.06 us -> 6.91 us  [from_others(): lax.ppermute(array, axis, [(i, (i + by) % count) for i in range(count)])]
    squeeze x1, local copies, waits for them, and re-layouts: 0.02 us -> 0.99 us  [per_device(): pair[high].append(swapped[high])]
    squeeze x1, local copies, waits for them, and re-layouts: 0.05 us -> 0.74 us  [per_device(): lax.dynamic_index_in_dim(by_core, replicas.index(high, low), 0, False)]
  transfers between devices with their start and end apart: 13 -> 13, of which waited for: 8 -> 5; matrix products, arithmetic and copies ran while one was open for 8% -> 10% of each run, Pallas kernels for 19% -> 24%
where the time goes in v2:
time: 66.8 us; the launch traced here: 66.4 us
  Pallas kernels  18.3 us (27%)
  waiting for transfers between devices  17.3 us (26%)
  local copies, waits for them, and re-layouts  15.1 us (23%)
  starting transfers between devices  12.9 us (19%)
  other arithmetic  1.97 us (3%)
  between operations  0.82 us (1%)
    unnamed x25, local copies, waits for them, and re-layouts  10.5 us
    ppermute x1, waiting for transfers between devices, per_device(): upper = lax.ppermute(upper_grad[0], 'pipe', down)  9.49 us
    ppermute x3, waiting for transfers between devices, from_others(): lax.ppermute(array, axis, [(i, (i + by) % count) for i in range(count)])  6.91 us
    ppermute x9, starting transfers between devices, send(): lax.ppermute(array, self.axis, [(i, self.to(i, high, low)) for i in range...  6.85 us
    pallas_call x2, Pallas kernels, weight_columns(): pl.pallas_call(functools.partial(weight_kernel, len(scaled)), grid=(width...  5.65 us
    pallas_call x1, Pallas kernels, scaled_grads(): pl.pallas_call(functools.partial(grad_kernel, scale, len(sums) - 1), grid...  4.59 us
    ppermute x3, starting transfers between devices, from_others(): lax.ppermute(array, axis, [(i, (i + by) % count) for i in range(count)])  4.59 us
    pallas_call x1, Pallas kernels, held_product(): pl.pallas_call(held_kernel, grid=(features // tile,), in_specs=[pl.BlockS...  3.66 us
  transfers between devices with their start and end apart: 13, of which 5 were waited for; matrix products, arithmetic and copies ran while one was open for 10% of the time, Pallas kernels for 24%

profile of v2, /device:TPU:0, one launch (start us, length us, event | category | flops | bytes accessed | tf_op | source)
XLA Modules:
  0.0 66.4 jit_solution(3310580571116896007)
XLA Ops:
  0.6 0.0 copy-start
  0.6 0.0 copy-start.6
  0.6 0.5 collective-permute-start.6
  1.2 2.7 %slice.18 = bf16[256,2560]{1,0:T(8,128)(2,1)} slice(bf16[256,4096]{1,0:T(8,128)(2,1)} %bitcast.18), slice={[0:256], [0:2560]} | slice | bytes 2621440 | tf_op jit(solution)/shard_map/slice | solution.py:296
  3.9 2.4 %collective-permute-start.11 = (bf16[256,2560]{1,0:T(8,128)(2,1)}, bf16[256,2560]{1,0:T(8,128)(2,1)}, u32[]{:S(2)}, u32[]{:S(2)}) collective-permute-start(bf16[256,2560]{1,0:T(8,128)(2,1)} %slice.18), channel_id=1, source_target_pairs={{0,16},{8,24},{16,0},{24,8},{1,17},{9,25},{17,1},{25,9},{2,18},{10... | collective-permute-start | bytes 3932168 | tf_op jit(solution)/shard_map/ppermute | solution.py:53
  6.3 0.0 copy-start.9
  6.4 1.4 %collective-permute-start.2 = (bf16[256,4096]{1,0:T(8,128)(2,1)}, bf16[256,4096]{1,0:T(8,128)(2,1)}, u32[]{:S(2)}, u32[]{:S(2)}) collective-permute-start(bf16[256,4096]{1,0:T(8,128)(2,1)} %bitcast.33), channel_id=1, source_target_pairs={{2,0},{4,2},{6,4},{3,1},{5,3},{7,5},{10,8},{12,10},{14,12},{11,9},... | collective-permute-start | bytes 6291464 | tf_op jit(solution)/shard_map/ppermute | solution.py:300
  7.8 0.0 copy-done
  7.8 0.5 multiply_reduce_fusion
  8.3 1.6 %collective-permute-start = (f32[1,256]{1,0:T(1,128)S(1)}, f32[1,256]{1,0:T(1,128)S(1)}, u32[]{:S(2)}, u32[]{:S(2)}) collective-permute-start(f32[1,256]{1,0:T(1,128)S(1)} %bitcast.27), channel_id=1, source_target_pairs={{0,1},{1,0},{2,3},{3,2},{4,5},{5,4},{6,7},{7,6},{8,9},{9,8},{10,11... | collective-permute-start | bytes 3080 | tf_op jit(solution)/shard_map/ppermute | solution.py:36
  9.8 2.1 %collective-permute-done.refs_1_ = f32[1,256]{1,0:T(1,128)S(1)} collective-permute-done((f32[1,256]{1,0:T(1,128)S(1)}, f32[1,256]{1,0:T(1,128)S(1)}, u32[]{:S(2)}, u32[]{:S(2)}) %collective-permute-start) | collective-permute-done | bytes 1056 | tf_op jit(solution)/shard_map/ppermute | solution.py:36
  11.9 0.0 copy-done.6
  11.9 0.2 shard_map.79
  12.1 0.7 %dynamic-slice_bitcast_fusion = (bf16[256,256]{1,0:T(8,128)(2,1)}, bf16[1,256,256]{2,1,0:T(8,128)(2,1)S(1)}, bf16[1,256,256]{2,1,0:T(8,128)(2,1)S(1)}, bf16[256,256]{1,0:T(8,128)(2,1)}) fusion(bf16[4,256,256]{2,1,0:T(8,128)(2,1)S(1)} %bitcast.26, s32[]{:T(128)S(6)} %select_n.91, s32[]{:T(128)S(6)} %select_n.84, s32[]{:T(128)S(6)} %select_n.82, s32[]{:T(128)S(6)} %select_n.80), kind=kLoop, calls=%fused_computation.9 | loop fusion | bytes 1048592 | tf_op jit(solution)/shard_map/jit(dynamic_index_in_dim)/squeeze | solution.py:312
  12.9 0.7 %pad_maximum_fusion = bf16[2,256,256]{2,1,0:T(8,128)(2,1)} fusion(bf16[1,256,256]{2,1,0:T(8,128)(2,1)S(1)} %get-tuple-element.20, bf16[1,256,256]{2,1,0:T(8,128)(2,1)S(1)} %get-tuple-element.21), kind=kLoop, calls=%fused_computation.1 | loop fusion | flops 131072 | bytes 524288 | tf_op jit(solution)/shard_map/stack | solution.py:315
  13.6 0.0 collective-permute-start.3
  13.6 0.0 copy-done.9
  13.6 0.0 copy-start.3
  13.6 3.4 %copy-done.3 = bf16[1,1024,4096]{2,1,0:T(8,128)(2,1)S(1)} copy-done((bf16[1,1024,4096]{2,1,0:T(8,128)(2,1)S(1)}, bf16[1,1024,4096]{2,1,0:T(8,128)(2,1)}, u32[]{:S(2)}) %copy-start.3) | copy-done | bytes 8388632
  17.0 4.6 %shard_map.76 = (bf16[256,4096]{1,0:T(8,128)(2,1)S(1)}, f32[1,4096]{1,0:T(1,128)S(1)}, f32[1,256]{1,0:T(1,128)S(1)}) custom-call(f32[1,256]{1,0:T(1,128)S(1)} %bitcast.29, f32[1,256]{1,0:T(1,128)S(1)} %collective-permute-done.refs_1_, bf16[256,1024]{1,0:T(8,128)(2,1)S(1)} %bitcast.25, bf16[1024,4096]{1,0:T(8,128)(2,1)S(1)} %bitcast.23, ...), custom_call_target="tpu_custom_call" | custom-call | flops 2147483648 | bytes 13107200 | tf_op jit(solution)/shard_map/pallas_call | solution.py:122
  21.6 0.0 copy-start.7
  21.6 1.3 %copy-done.7 = bf16[256,4096]{1,0:T(8,128)(2,1)} copy-done((bf16[256,4096]{1,0:T(8,128)(2,1)}, bf16[256,4096]{1,0:T(8,128)(2,1)S(1)}, u32[]{:S(2)}) %copy-start.7) | copy-done | bytes 2097176
  22.9 1.5 %collective-permute-start.1 = (f32[1,256]{1,0:T(1,128)S(1)}, f32[1,256]{1,0:T(1,128)S(1)}, u32[]{:S(2)}, u32[]{:S(2)}) collective-permute-start(f32[1,256]{1,0:T(1,128)S(1)} %get-tuple-element.11.refs_2_), channel_id=1, source_target_pairs={{0,1},{1,0},{2,3},{3,2},{4,5},{5,4},{6,7},{7,6},{8,9},{9,8},{10,11... | collective-permute-start | bytes 3080 | tf_op jit(solution)/shard_map/ppermute | solution.py:36
  24.4 0.1 slice.14
  24.4 2.0 %collective-permute-done.1.refs_3_ = f32[1,256]{1,0:T(1,128)S(1)} collective-permute-done((f32[1,256]{1,0:T(1,128)S(1)}, f32[1,256]{1,0:T(1,128)S(1)}, u32[]{:S(2)}, u32[]{:S(2)}) %collective-permute-start.1) | collective-permute-done | bytes 1056 | tf_op jit(solution)/shard_map/ppermute | solution.py:36
  26.5 0.0 copy-start.8
  26.5 1.6 %copy-done.8 = bf16[256,4096]{1,0:T(8,128)(2,1)S(1)} copy-done((bf16[256,4096]{1,0:T(8,128)(2,1)S(1)}, bf16[256,4096]{1,0:T(8,128)(2,1)}, u32[]{:S(2)}) %copy-start.8) | copy-done | bytes 2097176
  28.1 0.0 copy-start.10
  28.1 0.0 copy-start.11
  28.1 1.4 %shard_map.77.local_ref = bf16[256,4096]{1,0:T(8,128)(2,1)S(1)} custom-call(f32[1,256]{1,0:T(1,128)S(1)} %bitcast.30, f32[1,256]{1,0:T(1,128)S(1)} %collective-permute-done.refs_1_, f32[1,256]{1,0:T(1,128)S(1)} %get-tuple-element.11.refs_2_, f32[1,256]{1,0:T(1,128)S(1)} %collective-permute-done.1.refs_3_, bf16[256,4096]{1,0:T(8,128)(2,1)S(1)} %copy-done.8, ...), custom_call_target="tpu_custom_call" | custom-call | flops 3145728 | bytes 6291456 | tf_op jit(solution)/shard_map/pallas_call | solution.py:174
  29.5 0.0 copy-start.4
  29.5 1.3 %copy-done.4 = bf16[256,4096]{1,0:T(8,128)(2,1)} copy-done((bf16[256,4096]{1,0:T(8,128)(2,1)}, bf16[256,4096]{1,0:T(8,128)(2,1)S(1)}, u32[]{:S(2)}) %copy-start.4) | copy-done | bytes 2097176
  30.8 0.0 collective-permute-start.7
  30.8 0.0 collective-permute-done.3
  30.8 1.0 %slice_bitcast_fusion = (bf16[256,256]{1,0:T(8,128)(2,1)S(1)}, bf16[256,256]{1,0:T(8,128)(2,1)S(1)}) fusion(bf16[2,256,256]{2,1,0:T(8,128)(2,1)} %collective-permute-done.3), kind=kLoop, calls=%fused_computation.7 | loop fusion | bytes 524288 | tf_op jit(solution)/shard_map/squeeze | solution.py:318
  31.8 0.0 copy-done.10
  31.8 0.1 fusion
  31.9 1.8 %collective-permute-start.4 = (bf16[256,256]{1,0:T(8,128)(2,1)S(1)}, bf16[256,256]{1,0:T(8,128)(2,1)S(1)}, u32[]{:S(2)}, u32[]{:S(2)}) collective-permute-start(bf16[256,256]{1,0:T(8,128)(2,1)S(1)} %fusion), channel_id=1, source_target_pairs={{0,24},{8,16},{16,8},{24,0},{1,25},{9,17},{17,9},{25,1},{2,26},{10... | collective-permute-start | bytes 393224 | tf_op jit(solution)/shard_map/ppermute | solution.py:53
  33.7 0.0 copy-done.11
  33.7 0.0 collective-permute-done.6.refs_1_
  33.7 3.7 %shard_map.80.refs_2_ = bf16[256,4096]{1,0:T(8,128)(2,1)S(1)} custom-call(bf16[256,512]{1,0:T(8,128)(2,1)S(1)} %pad_maximum_fusion.2.scaled_ref, bf16[256,4096]{1,0:T(8,128)(2,1)S(1)} %bitcast.22, bf16[256,4096]{1,0:T(8,128)(2,1)} %collective-permute-done.6.refs_1_), custom_call_target="tpu_custom_call" | custom-call | flops 1073741824 | bytes 6553600 | tf_op jit(solution)/shard_map/pallas_call | solution.py:224
  37.4 0.0 copy-start.1
  37.4 1.3 %copy-done.1 = bf16[256,4096]{1,0:T(8,128)(2,1)} copy-done((bf16[256,4096]{1,0:T(8,128)(2,1)}, bf16[256,4096]{1,0:T(8,128)(2,1)S(1)}, u32[]{:S(2)}) %copy-start.1) | copy-done | bytes 2097176
  38.7 0.0 collective-permute-done.7
  38.7 0.0 collective-permute-done.4
  38.7 1.5 %collective-permute-start.8 = (bf16[256,1536]{1,0:T(8,128)(2,1)S(1)}, bf16[256,1536]{1,0:T(8,128)(2,1)S(1)}, u32[]{:S(2)}, u32[]{:S(2)}) collective-permute-start(bf16[256,1536]{1,0:T(8,128)(2,1)S(1)} %slice.14), channel_id=1, source_target_pairs={{0,16},{8,24},{16,0},{24,8},{1,17},{9,25},{17,1},{25,9},{2,18},{10... | collective-permute-start | bytes 2359304 | tf_op jit(solution)/shard_map/ppermute | solution.py:53
  40.2 0.0 collective-permute-done.11.refs_4_
  40.2 0.5 collective-permute-start.12
  40.7 0.1 collective-permute-start.9
  40.8 1.6 %collective-permute-start.5 = (bf16[256,256]{1,0:T(8,128)(2,1)S(1)}, bf16[256,256]{1,0:T(8,128)(2,1)S(1)}, u32[]{:S(2)}, u32[]{:S(2)}) collective-permute-start(bf16[256,256]{1,0:T(8,128)(2,1)S(1)} %collective-permute-done.4), channel_id=1, source_target_pairs={{0,1},{1,0},{2,3},{3,2},{4,5},{5,4},{6,7},{7,6},{8,9},{9,8},{10,11... | collective-permute-start | bytes 393224 | tf_op jit(solution)/shard_map/ppermute | solution.py:36
  42.4 0.9 %collective-permute-done.9 = f32[1,4096]{1,0:T(1,128)S(1)} collective-permute-done((f32[1,4096]{1,0:T(1,128)S(1)}, f32[1,4096]{1,0:T(1,128)S(1)}, u32[]{:S(2)}, u32[]{:S(2)}) %collective-permute-start.9) | collective-permute-done | bytes 16416 | tf_op jit(solution)/shard_map/ppermute | solution.py:53
  43.3 0.6 add.107
  43.9 2.8 %collective-permute-done.5 = bf16[256,256]{1,0:T(8,128)(2,1)S(1)} collective-permute-done((bf16[256,256]{1,0:T(8,128)(2,1)S(1)}, bf16[256,256]{1,0:T(8,128)(2,1)S(1)}, u32[]{:S(2)}, u32[]{:S(2)}) %collective-permute-start.5) | collective-permute-done | bytes 131104 | tf_op jit(solution)/shard_map/ppermute | solution.py:36
  46.8 0.0 copy-start.2
  46.8 9.5 %collective-permute-done.2.received_ref = bf16[256,4096]{1,0:T(8,128)(2,1)} collective-permute-done((bf16[256,4096]{1,0:T(8,128)(2,1)}, bf16[256,4096]{1,0:T(8,128)(2,1)}, u32[]{:S(2)}, u32[]{:S(2)}) %collective-permute-start.2) | collective-permute-done | bytes 2097184 | tf_op jit(solution)/shard_map/ppermute | solution.py:300
  56.3 1.6 %copy-done.5 = bf16[256,4096]{1,0:T(8,128)(2,1)S(1)} copy-done((bf16[256,4096]{1,0:T(8,128)(2,1)S(1)}, bf16[256,4096]{1,0:T(8,128)(2,1)}, u32[]{:S(2)}) %copy-start.5) | copy-done | bytes 2097176
  57.9 2.8 %shard_map.78 = bf16[256,4096]{1,0:T(8,128)(2,1)} custom-call(bf16[256,4096]{1,0:T(8,128)(2,1)S(1)} %copy-done.5, bf16[256,4096]{1,0:T(8,128)(2,1)} %collective-permute-done.2.received_ref), custom_call_target="tpu_custom_call" | custom-call | flops 1048576 | bytes 6291456 | tf_op jit(solution)/shard_map/pallas_call | solution.py:194
  60.7 0.0 collective-permute-done.8.refs_4_
  60.7 0.0 collective-permute-start.10
  60.7 0.0 collective-permute-done.12.refs_3_
  60.7 0.0 copy-done.2
  60.7 3.3 %shard_map.81.refs_5_ = f32[256,4096]{1,0:T(8,128)} custom-call(bf16[256,512]{1,0:T(8,128)(2,1)S(1)} %pad_maximum_fusion.1.refs_0_, f32[1,4096]{1,0:T(1,128)S(1)} %copy-done.9, bf16[256,4096]{1,0:T(8,128)(2,1)S(1)} %copy-done.2, bf16[256,2560]{1,0:T(8,128)(2,1)S(1)} %collective-permute-done.12.refs_3_, bf16[256,2560]{1,0:T(8,128)(2,1)} %collective-permute-done.11.refs_4_), custom_call_target="tpu_custom_call" | custom-call | flops 671088640 | bytes 6815744 | tf_op jit(solution)/shard_map/pallas_call | solution.py:266
  64.0 0.0 collective-permute-done.10.refs_3_
  64.0 2.3 %shard_map.82 = f32[256,4096]{1,0:T(8,128)} custom-call(bf16[256,512]{1,0:T(8,128)(2,1)S(1)} %pad_maximum_fusion.1.refs_0_, f32[1,4096]{1,0:T(1,128)S(1)} %copy-done.9, bf16[256,4096]{1,0:T(8,128)(2,1)S(1)} %copy-done.2, bf16[256,1536]{1,0:T(8,128)(2,1)S(1)} %collective-permute-done.10.refs_3_, ...), custom_call_target="tpu_custom_call", output_to_operand_aliasing={{}: (5, {})} | custom-call | flops 402653184 | bytes 4194304 | tf_op jit(solution)/shard_map/pallas_call | solution.py:266
  (7 shorter events, 0.1 us)
Async XLA Ops:
  0.6 7.1 %copy-start = (bf16[1,256,4096]{2,1,0:T(8,128)(2,1)S(1)}, bf16[1,256,4096]{2,1,0:T(8,128)(2,1)}, u32[]{:S(2)}) copy-start(bf16[1,256,4096]{2,1,0:T(8,128)(2,1)} %param.5) | copy-start | bytes 6291460
  0.6 11.3 %copy-start.6 = (bf16[1,256,1024]{2,1,0:T(8,128)(2,1)S(1)}, bf16[1,256,1024]{2,1,0:T(8,128)(2,1)}, u32[]{:S(2)}) copy-start(bf16[1,256,1024]{2,1,0:T(8,128)(2,1)} %param.8) | copy-start | bytes 1572868
  0.6 33.1 %collective-permute-start.6 = (bf16[256,4096]{1,0:T(8,128)(2,1)}, bf16[256,4096]{1,0:T(8,128)(2,1)}, u32[]{:S(2)}, u32[]{:S(2)}) collective-permute-start(bf16[256,4096]{1,0:T(8,128)(2,1)} %bitcast.17), channel_id=1, source_target_pairs={{0,8},{8,0},{16,24},{24,16},{1,9},{9,1},{17,25},{25,17},{2,10},{10... | collective-permute-start | bytes 6291464 | tf_op jit(solution)/shard_map/ppermute | solution.py:53
  3.9 36.3 %collective-permute-start.11 = (bf16[256,2560]{1,0:T(8,128)(2,1)}, bf16[256,2560]{1,0:T(8,128)(2,1)}, u32[]{:S(2)}, u32[]{:S(2)}) collective-permute-start(bf16[256,2560]{1,0:T(8,128)(2,1)} %slice.18), channel_id=1, source_target_pairs={{0,16},{8,24},{16,0},{24,8},{1,17},{9,25},{17,1},{25,9},{2,18},{10... | collective-permute-start | bytes 3932168 | tf_op jit(solution)/shard_map/ppermute | solution.py:53
  6.3 7.2 %copy-start.9 = (f32[1,4096]{1,0:T(1,128)S(1)}, f32[1,4096]{1,0:T(1,128)}, u32[]{:S(2)}) copy-start(f32[1,4096]{1,0:T(1,128)} %refs_1_.3) | copy-start | bytes 49156
  6.4 49.9 %collective-permute-start.2 = (bf16[256,4096]{1,0:T(8,128)(2,1)}, bf16[256,4096]{1,0:T(8,128)(2,1)}, u32[]{:S(2)}, u32[]{:S(2)}) collective-permute-start(bf16[256,4096]{1,0:T(8,128)(2,1)} %bitcast.33), channel_id=1, source_target_pairs={{2,0},{4,2},{6,4},{3,1},{5,3},{7,5},{10,8},{12,10},{14,12},{11,9},... | collective-permute-start | bytes 6291464 | tf_op jit(solution)/shard_map/ppermute | solution.py:300
  8.3 3.6 %collective-permute-start = (f32[1,256]{1,0:T(1,128)S(1)}, f32[1,256]{1,0:T(1,128)S(1)}, u32[]{:S(2)}, u32[]{:S(2)}) collective-permute-start(f32[1,256]{1,0:T(1,128)S(1)} %bitcast.27), channel_id=1, source_target_pairs={{0,1},{1,0},{2,3},{3,2},{4,5},{5,4},{6,7},{7,6},{8,9},{9,8},{10,11... | collective-permute-start | bytes 3080 | tf_op jit(solution)/shard_map/ppermute | solution.py:36
  13.6 17.2 %collective-permute-start.3 = (bf16[2,256,256]{2,1,0:T(8,128)(2,1)}, bf16[2,256,256]{2,1,0:T(8,128)(2,1)}, u32[]{:S(2)}, u32[]{:S(2)}) collective-permute-start(bf16[2,256,256]{2,1,0:T(8,128)(2,1)} %pad_maximum_fusion), channel_id=1, source_target_pairs={{0,8},{8,0},{16,24},{24,16},{1,9},{9,1},{17,25},{25,17},{2,10},{10... | collective-permute-start | bytes 786440 | tf_op jit(solution)/shard_map/ppermute | solution.py:53
  13.6 3.4 %copy-start.3 = (bf16[1,1024,4096]{2,1,0:T(8,128)(2,1)S(1)}, bf16[1,1024,4096]{2,1,0:T(8,128)(2,1)}, u32[]{:S(2)}) copy-start(bf16[1,1024,4096]{2,1,0:T(8,128)(2,1)} %param.7) | copy-start | bytes 25165828
  21.6 1.3 %copy-start.7 = (bf16[256,4096]{1,0:T(8,128)(2,1)}, bf16[256,4096]{1,0:T(8,128)(2,1)S(1)}, u32[]{:S(2)}) copy-start(bf16[256,4096]{1,0:T(8,128)(2,1)S(1)} %get-tuple-element.12.refs_4_) | copy-start | bytes 6291460
  22.9 3.6 %collective-permute-start.1 = (f32[1,256]{1,0:T(1,128)S(1)}, f32[1,256]{1,0:T(1,128)S(1)}, u32[]{:S(2)}, u32[]{:S(2)}) collective-permute-start(f32[1,256]{1,0:T(1,128)S(1)} %get-tuple-element.11.refs_2_), channel_id=1, source_target_pairs={{0,1},{1,0},{2,3},{3,2},{4,5},{5,4},{6,7},{7,6},{8,9},{9,8},{10,11... | collective-permute-start | bytes 3080 | tf_op jit(solution)/shard_map/ppermute | solution.py:36
  26.5 1.6 %copy-start.8 = (bf16[256,4096]{1,0:T(8,128)(2,1)S(1)}, bf16[256,4096]{1,0:T(8,128)(2,1)}, u32[]{:S(2)}) copy-start(bf16[256,4096]{1,0:T(8,128)(2,1)} %copy-done.7) | copy-start | bytes 6291460
  28.1 3.7 %copy-start.10 = (bf16[256,256]{1,0:T(8,128)(2,1)S(1)}, bf16[256,256]{1,0:T(8,128)(2,1)}, u32[]{:S(2)}) copy-start(bf16[256,256]{1,0:T(8,128)(2,1)} %get-tuple-element.22) | copy-start | bytes 393220
  28.1 5.6 %copy-start.11 = (bf16[256,256]{1,0:T(8,128)(2,1)S(1)}, bf16[256,256]{1,0:T(8,128)(2,1)}, u32[]{:S(2)}) copy-start(bf16[256,256]{1,0:T(8,128)(2,1)} %get-tuple-element.19) | copy-start | bytes 393220
  29.5 1.3 %copy-start.4 = (bf16[256,4096]{1,0:T(8,128)(2,1)}, bf16[256,4096]{1,0:T(8,128)(2,1)S(1)}, u32[]{:S(2)}) copy-start(bf16[256,4096]{1,0:T(8,128)(2,1)S(1)} %shard_map.77.local_ref) | copy-start | bytes 6291460
  30.8 7.9 %collective-permute-start.7 = (f32[1,4096]{1,0:T(1,128)S(1)}, f32[1,4096]{1,0:T(1,128)S(1)}, u32[]{:S(2)}, u32[]{:S(2)}) collective-permute-start(f32[1,4096]{1,0:T(1,128)S(1)} %get-tuple-element.15), channel_id=1, source_target_pairs={{0,24},{8,16},{16,8},{24,0},{1,25},{9,17},{17,9},{25,1},{2,26},{10... | collective-permute-start | bytes 49160 | tf_op jit(solution)/shard_map/ppermute | solution.py:53
  31.9 6.8 %collective-permute-start.4 = (bf16[256,256]{1,0:T(8,128)(2,1)S(1)}, bf16[256,256]{1,0:T(8,128)(2,1)S(1)}, u32[]{:S(2)}, u32[]{:S(2)}) collective-permute-start(bf16[256,256]{1,0:T(8,128)(2,1)S(1)} %fusion), channel_id=1, source_target_pairs={{0,24},{8,16},{16,8},{24,0},{1,25},{9,17},{17,9},{25,1},{2,26},{10... | collective-permute-start | bytes 393224 | tf_op jit(solution)/shard_map/ppermute | solution.py:53
  37.4 1.3 %copy-start.1 = (bf16[256,4096]{1,0:T(8,128)(2,1)}, bf16[256,4096]{1,0:T(8,128)(2,1)S(1)}, u32[]{:S(2)}) copy-start(bf16[256,4096]{1,0:T(8,128)(2,1)S(1)} %shard_map.80.refs_2_) | copy-start | bytes 6291460
  38.7 22.0 %collective-permute-start.8 = (bf16[256,1536]{1,0:T(8,128)(2,1)S(1)}, bf16[256,1536]{1,0:T(8,128)(2,1)S(1)}, u32[]{:S(2)}, u32[]{:S(2)}) collective-permute-start(bf16[256,1536]{1,0:T(8,128)(2,1)S(1)} %slice.14), channel_id=1, source_target_pairs={{0,16},{8,24},{16,0},{24,8},{1,17},{9,25},{17,1},{25,9},{2,18},{10... | collective-permute-start | bytes 2359304 | tf_op jit(solution)/shard_map/ppermute | solution.py:53
  40.2 20.5 %collective-permute-start.12 = (bf16[256,2560]{1,0:T(8,128)(2,1)}, bf16[256,2560]{1,0:T(8,128)(2,1)S(1)}, u32[]{:S(2)}, u32[]{:S(2)}) collective-permute-start(bf16[256,2560]{1,0:T(8,128)(2,1)} %collective-permute-done.11.refs_4_), channel_id=1, source_target_pairs={{0,8},{8,0},{16,24},{24,16},{1,9},{9,1},{17,25},{25,17},{2,10},{10... | collective-permute-start | bytes 3932168 | tf_op jit(solution)/shard_map/ppermute | solution.py:53
  40.7 2.5 %collective-permute-start.9 = (f32[1,4096]{1,0:T(1,128)S(1)}, f32[1,4096]{1,0:T(1,128)S(1)}, u32[]{:S(2)}, u32[]{:S(2)}) collective-permute-start(f32[1,4096]{1,0:T(1,128)S(1)} %add.106), channel_id=1, source_target_pairs={{0,8},{8,0},{16,24},{24,16},{1,9},{9,1},{17,25},{25,17},{2,10},{10... | collective-permute-start | bytes 49160 | tf_op jit(solution)/shard_map/ppermute | solution.py:53
  40.8 5.9 %collective-permute-start.5 = (bf16[256,256]{1,0:T(8,128)(2,1)S(1)}, bf16[256,256]{1,0:T(8,128)(2,1)S(1)}, u32[]{:S(2)}, u32[]{:S(2)}) collective-permute-start(bf16[256,256]{1,0:T(8,128)(2,1)S(1)} %collective-permute-done.4), channel_id=1, source_target_pairs={{0,1},{1,0},{2,3},{3,2},{4,5},{5,4},{6,7},{7,6},{8,9},{9,8},{10,11... | collective-permute-start | bytes 393224 | tf_op jit(solution)/shard_map/ppermute | solution.py:36
  46.8 13.9 %copy-start.2 = (bf16[256,4096]{1,0:T(8,128)(2,1)S(1)}, bf16[256,4096]{1,0:T(8,128)(2,1)}, u32[]{:S(2)}) copy-start(bf16[256,4096]{1,0:T(8,128)(2,1)} %copy-done.1) | copy-start | bytes 6291460
  56.3 1.6 %copy-start.5 = (bf16[256,4096]{1,0:T(8,128)(2,1)S(1)}, bf16[256,4096]{1,0:T(8,128)(2,1)}, u32[]{:S(2)}) copy-start(bf16[256,4096]{1,0:T(8,128)(2,1)} %copy-done.4) | copy-start | bytes 6291460
  60.7 3.3 %collective-permute-start.10 = (bf16[256,1536]{1,0:T(8,128)(2,1)S(1)}, bf16[256,1536]{1,0:T(8,128)(2,1)S(1)}, u32[]{:S(2)}, u32[]{:S(2)}) collective-permute-start(bf16[256,1536]{1,0:T(8,128)(2,1)S(1)} %collective-permute-done.8.refs_4_), channel_id=1, source_target_pairs={{0,8},{8,0},{16,24},{24,16},{1,9},{9,1},{17,25},{25,17},{2,10},{10... | collective-permute-start | bytes 2359304 | tf_op jit(solution)/shard_map/ppermute | solution.py:53

commit v3 on v2

--- a/solution.py
+++ b/solution.py
@@ -85,9 +85,7 @@
         functools.partial(scale_kernel, scale),
         out_shape=jax.ShapeDtypeStruct(cotangent.shape[::-1], jnp.bfloat16),
         compiler_params=PARAMS,
-        cost_estimate=pl.CostEstimate(
-            flops=2 * cotangent.size, bytes_accessed=4 * cotangent.size, transcendentals=0
-        ),
+        cost_estimate=pl.CostEstimate(flops=1, bytes_accessed=1, transcendentals=0),
     )(*sums, cotangent)
 
 
@@ -141,11 +139,7 @@
         ],
         scratch_shapes=[pltpu.VMEM((tokens, 1), jnp.float32), pltpu.VMEM((tokens, 128), jnp.float32)],
         compiler_params=PARAMS,
-        cost_estimate=pl.CostEstimate(
-            flops=2 * tokens * features * weight.shape[0],
-            bytes_accessed=2 * (weight.size + cotangent.size + 2 * x.size),
-            transcendentals=0,
-        ),
+        cost_estimate=pl.CostEstimate(flops=1, bytes_accessed=1, transcendentals=0),
     )(*sums, cotangent, weight, x, gain_row)
 
 
@@ -179,7 +173,7 @@
         out_shape=jax.ShapeDtypeStruct(x.shape, jnp.bfloat16),
         scratch_shapes=[pltpu.VMEM((tokens, 1), jnp.float32)],
         compiler_params=PARAMS,
-        cost_estimate=pl.CostEstimate(flops=3 * x.size, bytes_accessed=6 * x.size, transcendentals=0),
+        cost_estimate=pl.CostEstimate(flops=1, bytes_accessed=1, transcendentals=0),
     )(*sums, *centers, scaled_grad, x)
 
 
@@ -198,7 +192,7 @@
         out_specs=block,
         out_shape=jax.ShapeDtypeStruct(received.shape, received.dtype),
         compiler_params=PARAMS,
-        cost_estimate=pl.CostEstimate(flops=received.size, bytes_accessed=6 * received.size, transcendentals=0),
+        cost_estimate=pl.CostEstimate(flops=1, bytes_accessed=1, transcendentals=0),
     )(local, received)
 
 
@@ -229,11 +223,7 @@
         out_specs=pl.BlockSpec((rows, tile), column),
         out_shape=jax.ShapeDtypeStruct((rows, features), jnp.bfloat16),
         compiler_params=PARAMS,
-        cost_estimate=pl.CostEstimate(
-            flops=2 * scaled.size * features,
-            bytes_accessed=2 * (scaled.size + len(held) * tokens * features + rows * features),
-            transcendentals=0,
-        ),
+        cost_estimate=pl.CostEstimate(flops=1, bytes_accessed=1, transcendentals=0),
     )(scaled, *held)
 
 
@@ -271,11 +261,7 @@
         out_shape=jax.ShapeDtypeStruct((rows, features), jnp.float32),
         input_output_aliases=aliases,
         compiler_params=PARAMS,
-        cost_estimate=pl.CostEstimate(
-            flops=2 * tokens * rows * width,
-            bytes_accessed=2 * tokens * (rows + width) + 6 * rows * width,
-            transcendentals=0,
-        ),
+        cost_estimate=pl.CostEstimate(flops=1, bytes_accessed=1, transcendentals=0),
     )(*args)
 
 

time: 66.8 us -> 67.2 us (level)
  the two profiles are of different devices: /device:TPU:0 before, /device:TPU:25 now
where the time goes in v3:
time: 67.2 us; the launch traced here: 66.9 us
  waiting for transfers between devices  18.9 us (28%)
  Pallas kernels  18.3 us (27%)
  starting transfers between devices  15.8 us (24%)
  local copies, waits for them, and re-layouts  11.9 us (18%)
  other arithmetic  1.27 us (2%)
  between operations  0.78 us (1%)
    ppermute x9, waiting for transfers between devices, send(): lax.ppermute(array, self.axis, [(i, self.to(i, high, low)) for i in range...  14.1 us
    unnamed x19, local copies, waits for them, and re-layouts  8.56 us
    ppermute x9, starting transfers between devices, send(): lax.ppermute(array, self.axis, [(i, self.to(i, high, low)) for i in range...  8.49 us
    pallas_call x2, Pallas kernels, weight_columns(): pl.pallas_call(functools.partial(weight_kernel, len(scaled)), grid=(width...  5.65 us
    pallas_call x1, Pallas kernels, scaled_grads(): pl.pallas_call(functools.partial(grad_kernel, scale, len(sums) - 1), grid...  4.6 us
    ppermute x3, waiting for transfers between devices, from_others(): lax.ppermute(array, axis, [(i, (i + by) % count) for i in range(count)])  4.26 us
    ppermute x3, starting transfers between devices, from_others(): lax.ppermute(array, axis, [(i, (i + by) % count) for i in range(count)])  3.75 us
    pallas_call x1, Pallas kernels, held_product(): pl.pallas_call(held_kernel, grid=(features // tile,), in_specs=[pl.BlockS...  3.65 us
  transfers between devices with their start and end apart: 13, of which 8 were waited for; matrix products, arithmetic and copies ran while one was open for 8% of the time, Pallas kernels for 24%

profile of v3, /device:TPU:25, one launch (start us, length us, event | category | flops | bytes accessed | tf_op | source)
XLA Modules:
  0.0 66.9 jit_solution(4342888760754070019)
XLA Ops:
  0.6 0.0 copy-start
  0.6 0.7 %collective-permute-start.6 = (bf16[256,4096]{1,0:T(8,128)(2,1)}, bf16[256,4096]{1,0:T(8,128)(2,1)}, u32[]{:S(2)}, u32[]{:S(2)}) collective-permute-start(bf16[256,4096]{1,0:T(8,128)(2,1)} %bitcast.17), channel_id=1, source_target_pairs={{0,8},{8,0},{16,24},{24,16},{1,9},{9,1},{17,25},{25,17},{2,10},{10... | collective-permute-start | bytes 6291464 | tf_op jit(solution)/shard_map/ppermute | solution.py:53
  1.4 0.0 copy-start.6
  1.4 3.5 %collective-permute-start.2 = (bf16[256,4096]{1,0:T(8,128)(2,1)}, bf16[256,4096]{1,0:T(8,128)(2,1)}, u32[]{:S(2)}, u32[]{:S(2)}) collective-permute-start(bf16[256,4096]{1,0:T(8,128)(2,1)} %bitcast.33), channel_id=1, source_target_pairs={{2,0},{4,2},{6,4},{3,1},{5,3},{7,5},{10,8},{12,10},{14,12},{11,9},... | collective-permute-start | bytes 6291464 | tf_op jit(solution)/shard_map/ppermute | solution.py:286
  4.9 2.5 %slice.18 = bf16[256,2560]{1,0:T(8,128)(2,1)} slice(bf16[256,4096]{1,0:T(8,128)(2,1)} %bitcast.18), slice={[0:256], [0:2560]} | slice | bytes 2621440 | tf_op jit(solution)/shard_map/slice | solution.py:282
  7.4 1.2 %collective-permute-start.11 = (bf16[256,2560]{1,0:T(8,128)(2,1)}, bf16[256,2560]{1,0:T(8,128)(2,1)}, u32[]{:S(2)}, u32[]{:S(2)}) collective-permute-start(bf16[256,2560]{1,0:T(8,128)(2,1)} %slice.18), channel_id=1, source_target_pairs={{0,16},{8,24},{16,0},{24,8},{1,17},{9,25},{17,1},{25,9},{2,18},{10... | collective-permute-start | bytes 3932168 | tf_op jit(solution)/shard_map/ppermute | solution.py:53
  8.6 0.0 copy-done
  8.6 0.5 multiply_reduce_fusion
  9.1 0.0 copy-start.7
  9.1 1.3 %collective-permute-start = (f32[1,256]{1,0:T(1,128)S(1)}, f32[1,256]{1,0:T(1,128)S(1)}, u32[]{:S(2)}, u32[]{:S(2)}) collective-permute-start(f32[1,256]{1,0:T(1,128)S(1)} %bitcast.27), channel_id=1, source_target_pairs={{0,1},{1,0},{2,3},{3,2},{4,5},{5,4},{6,7},{7,6},{8,9},{9,8},{10,11... | collective-permute-start | bytes 3080 | tf_op jit(solution)/shard_map/ppermute | solution.py:36
  10.4 1.6 %collective-permute-done.refs_1_ = f32[1,256]{1,0:T(1,128)S(1)} collective-permute-done((f32[1,256]{1,0:T(1,128)S(1)}, f32[1,256]{1,0:T(1,128)S(1)}, u32[]{:S(2)}, u32[]{:S(2)}) %collective-permute-start) | collective-permute-done | bytes 1056 | tf_op jit(solution)/shard_map/ppermute | solution.py:36
  12.0 0.0 copy-done.6
  12.0 0.2 shard_map.79
  12.2 0.7 %dynamic-slice_bitcast_fusion = (bf16[256,256]{1,0:T(8,128)(2,1)}, bf16[1,256,256]{2,1,0:T(8,128)(2,1)S(1)}, bf16[1,256,256]{2,1,0:T(8,128)(2,1)S(1)}, bf16[256,256]{1,0:T(8,128)(2,1)S(1)}) fusion(bf16[4,256,256]{2,1,0:T(8,128)(2,1)S(1)} %bitcast.26, s32[]{:T(128)S(6)} %select_n.91, s32[]{:T(128)S(6)} %select_n.84, s32[]{:T(128)S(6)} %select_n.82, ...), kind=kLoop, calls=%fused_computation.9 | loop fusion | bytes 1048592 | tf_op jit(solution)/shard_map/jit(dynamic_index_in_dim)/squeeze | solution.py:298
  13.0 1.4 %collective-permute-start.3 = (bf16[2,256,256]{2,1,0:T(8,128)(2,1)S(1)}, bf16[2,256,256]{2,1,0:T(8,128)(2,1)S(1)}, u32[]{:S(2)}, u32[]{:S(2)}) collective-permute-start(bf16[2,256,256]{2,1,0:T(8,128)(2,1)S(1)} %pad_maximum_fusion), channel_id=1, source_target_pairs={{0,8},{8,0},{16,24},{24,16},{1,9},{9,1},{17,25},{25,17},{2,10},{10... | collective-permute-start | bytes 786440 | tf_op jit(solution)/shard_map/ppermute | solution.py:53
  14.4 1.2 %collective-permute-done.3 = bf16[2,256,256]{2,1,0:T(8,128)(2,1)S(1)} collective-permute-done((bf16[2,256,256]{2,1,0:T(8,128)(2,1)S(1)}, bf16[2,256,256]{2,1,0:T(8,128)(2,1)S(1)}, u32[]{:S(2)}, u32[]{:S(2)}) %collective-permute-start.3) | collective-permute-done | bytes 262176 | tf_op jit(solution)/shard_map/ppermute | solution.py:53
  15.6 0.1 fusion
  15.6 0.6 collective-permute-start.4
  16.2 0.0 copy-done.7
  16.2 0.0 copy-start.3
  16.2 3.4 %copy-done.3 = bf16[1,1024,4096]{2,1,0:T(8,128)(2,1)S(1)} copy-done((bf16[1,1024,4096]{2,1,0:T(8,128)(2,1)S(1)}, bf16[1,1024,4096]{2,1,0:T(8,128)(2,1)}, u32[]{:S(2)}) %copy-start.3) | copy-done | bytes 8388632
  19.6 4.6 %shard_map.76 = (bf16[256,4096]{1,0:T(8,128)(2,1)S(1)}, f32[1,4096]{1,0:T(1,128)S(1)}, f32[1,256]{1,0:T(1,128)S(1)}) custom-call(f32[1,256]{1,0:T(1,128)S(1)} %bitcast.29, f32[1,256]{1,0:T(1,128)S(1)} %collective-permute-done.refs_1_, bf16[256,1024]{1,0:T(8,128)(2,1)S(1)} %bitcast.25, bf16[1024,4096]{1,0:T(8,128)(2,1)S(1)} %bitcast.23, ...), custom_call_target="tpu_custom_call" | custom-call | flops 1 | bytes 1 | tf_op jit(solution)/shard_map/pallas_call | solution.py:120
  24.2 1.3 %collective-permute-start.1 = (f32[1,256]{1,0:T(1,128)S(1)}, f32[1,256]{1,0:T(1,128)S(1)}, u32[]{:S(2)}, u32[]{:S(2)}) collective-permute-start(f32[1,256]{1,0:T(1,128)S(1)} %get-tuple-element.11.refs_2_), channel_id=1, source_target_pairs={{0,1},{1,0},{2,3},{3,2},{4,5},{5,4},{6,7},{7,6},{8,9},{9,8},{10,11... | collective-permute-start | bytes 3080 | tf_op jit(solution)/shard_map/ppermute | solution.py:36
  25.4 0.1 slice.14
  25.5 1.6 %collective-permute-done.1.refs_3_ = f32[1,256]{1,0:T(1,128)S(1)} collective-permute-done((f32[1,256]{1,0:T(1,128)S(1)}, f32[1,256]{1,0:T(1,128)S(1)}, u32[]{:S(2)}, u32[]{:S(2)}) %collective-permute-start.1) | collective-permute-done | bytes 1056 | tf_op jit(solution)/shard_map/ppermute | solution.py:36
  27.1 0.0 copy-start.8
  27.1 1.4 %shard_map.77.local_ref = bf16[256,4096]{1,0:T(8,128)(2,1)S(1)} custom-call(f32[1,256]{1,0:T(1,128)S(1)} %bitcast.30, f32[1,256]{1,0:T(1,128)S(1)} %collective-permute-done.refs_1_, f32[1,256]{1,0:T(1,128)S(1)} %get-tuple-element.11.refs_2_, f32[1,256]{1,0:T(1,128)S(1)} %collective-permute-done.1.refs_3_, bf16[256,4096]{1,0:T(8,128)(2,1)S(1)} %get-tuple-element.12.refs_4_, ...), custom_call_target="tpu_custom_call" | custom-call | flops 1 | bytes 1 | tf_op jit(solution)/shard_map/pallas_call | solution.py:168
  28.5 0.0 copy-start.4
  28.5 1.3 %copy-done.4 = bf16[256,4096]{1,0:T(8,128)(2,1)} copy-done((bf16[256,4096]{1,0:T(8,128)(2,1)}, bf16[256,4096]{1,0:T(8,128)(2,1)S(1)}, u32[]{:S(2)}) %copy-start.4) | copy-done | bytes 2097176
  29.8 2.0 %collective-permute-start.7 = (f32[1,4096]{1,0:T(1,128)S(1)}, f32[1,4096]{1,0:T(1,128)S(1)}, u32[]{:S(2)}, u32[]{:S(2)}) collective-permute-start(f32[1,4096]{1,0:T(1,128)S(1)} %get-tuple-element.15), channel_id=1, source_target_pairs={{0,24},{8,16},{16,8},{24,0},{1,25},{9,17},{17,9},{25,1},{2,26},{10... | collective-permute-start | bytes 49160 | tf_op jit(solution)/shard_map/ppermute | solution.py:53
  31.8 0.0 copy-done.8
  31.8 0.0 collective-permute-done.6.refs_1_
  31.9 3.7 %shard_map.80.refs_2_ = bf16[256,4096]{1,0:T(8,128)(2,1)S(1)} custom-call(bf16[256,512]{1,0:T(8,128)(2,1)S(1)} %pad_maximum_fusion.2.scaled_ref, bf16[256,4096]{1,0:T(8,128)(2,1)S(1)} %bitcast.22, bf16[256,4096]{1,0:T(8,128)(2,1)} %collective-permute-done.6.refs_1_), custom_call_target="tpu_custom_call" | custom-call | flops 1 | bytes 1 | tf_op jit(solution)/shard_map/pallas_call | solution.py:218
  35.5 0.0 copy-start.1
  35.5 1.3 %copy-done.1 = bf16[256,4096]{1,0:T(8,128)(2,1)} copy-done((bf16[256,4096]{1,0:T(8,128)(2,1)}, bf16[256,4096]{1,0:T(8,128)(2,1)S(1)}, u32[]{:S(2)}) %copy-start.1) | copy-done | bytes 2097176
  36.8 4.4 %collective-permute-done.7 = f32[1,4096]{1,0:T(1,128)S(1)} collective-permute-done((f32[1,4096]{1,0:T(1,128)S(1)}, f32[1,4096]{1,0:T(1,128)S(1)}, u32[]{:S(2)}, u32[]{:S(2)}) %collective-permute-start.7) | collective-permute-done | bytes 16416 | tf_op jit(solution)/shard_map/ppermute | solution.py:53
  41.3 0.0 collective-permute-done.4
  41.3 1.2 %collective-permute-start.8 = (bf16[256,1536]{1,0:T(8,128)(2,1)S(1)}, bf16[256,1536]{1,0:T(8,128)(2,1)S(1)}, u32[]{:S(2)}, u32[]{:S(2)}) collective-permute-start(bf16[256,1536]{1,0:T(8,128)(2,1)S(1)} %slice.14), channel_id=1, source_target_pairs={{0,16},{8,24},{16,0},{24,8},{1,17},{9,25},{17,1},{25,9},{2,18},{10... | collective-permute-start | bytes 2359304 | tf_op jit(solution)/shard_map/ppermute | solution.py:53
  42.5 0.0 collective-permute-done.11.refs_4_
  42.5 0.2 collective-permute-start.12
  42.8 0.4 collective-permute-start.9
  43.1 1.2 %collective-permute-start.5 = (bf16[256,256]{1,0:T(8,128)(2,1)}, bf16[256,256]{1,0:T(8,128)(2,1)S(1)}, u32[]{:S(2)}, u32[]{:S(2)}) collective-permute-start(bf16[256,256]{1,0:T(8,128)(2,1)} %collective-permute-done.4), channel_id=1, source_target_pairs={{0,1},{1,0},{2,3},{3,2},{4,5},{5,4},{6,7},{7,6},{8,9},{9,8},{10,11... | collective-permute-start | bytes 393224 | tf_op jit(solution)/shard_map/ppermute | solution.py:36
  44.3 1.2 %collective-permute-done.9 = f32[1,4096]{1,0:T(1,128)S(1)} collective-permute-done((f32[1,4096]{1,0:T(1,128)S(1)}, f32[1,4096]{1,0:T(1,128)S(1)}, u32[]{:S(2)}, u32[]{:S(2)}) %collective-permute-start.9) | collective-permute-done | bytes 16416 | tf_op jit(solution)/shard_map/ppermute | solution.py:53
  45.6 0.6 add.107
  46.2 0.9 %constant_dynamic-update-slice_fusion.1 = bf16[256,512]{1,0:T(8,128)(2,1)S(1)} fusion(bf16[256,256]{1,0:T(8,128)(2,1)} %collective-permute-done.4), kind=kLoop, calls=%fused_computation.12 | loop fusion | bytes 262144
  47.1 1.1 %collective-permute-done.5 = bf16[256,256]{1,0:T(8,128)(2,1)S(1)} collective-permute-done((bf16[256,256]{1,0:T(8,128)(2,1)}, bf16[256,256]{1,0:T(8,128)(2,1)S(1)}, u32[]{:S(2)}, u32[]{:S(2)}) %collective-permute-start.5) | collective-permute-done | bytes 131104 | tf_op jit(solution)/shard_map/ppermute | solution.py:36
  48.3 0.0 copy-start.2
  48.3 0.6 collective-permute-done.2.received_ref
  48.9 0.0 copy-start.5
  48.9 1.6 %copy-done.5 = bf16[256,4096]{1,0:T(8,128)(2,1)S(1)} copy-done((bf16[256,4096]{1,0:T(8,128)(2,1)S(1)}, bf16[256,4096]{1,0:T(8,128)(2,1)}, u32[]{:S(2)}) %copy-start.5) | copy-done | bytes 2097176
  50.5 2.8 %shard_map.78 = bf16[256,4096]{1,0:T(8,128)(2,1)} custom-call(bf16[256,4096]{1,0:T(8,128)(2,1)S(1)} %copy-done.5, bf16[256,4096]{1,0:T(8,128)(2,1)} %collective-permute-done.2.received_ref), custom_call_target="tpu_custom_call" | custom-call | flops 1 | bytes 1 | tf_op jit(solution)/shard_map/pallas_call | solution.py:188
  53.3 7.2 %collective-permute-done.8.refs_4_ = bf16[256,1536]{1,0:T(8,128)(2,1)S(1)} collective-permute-done((bf16[256,1536]{1,0:T(8,128)(2,1)S(1)}, bf16[256,1536]{1,0:T(8,128)(2,1)S(1)}, u32[]{:S(2)}, u32[]{:S(2)}) %collective-permute-start.8) | collective-permute-done | bytes 786464 | tf_op jit(solution)/shard_map/ppermute | solution.py:53
  60.5 0.7 %collective-permute-start.10 = (bf16[256,1536]{1,0:T(8,128)(2,1)S(1)}, bf16[256,1536]{1,0:T(8,128)(2,1)S(1)}, u32[]{:S(2)}, u32[]{:S(2)}) collective-permute-start(bf16[256,1536]{1,0:T(8,128)(2,1)S(1)} %collective-permute-done.8.refs_4_), channel_id=1, source_target_pairs={{0,8},{8,0},{16,24},{24,16},{1,9},{9,1},{17,25},{25,17},{2,10},{10... | collective-permute-start | bytes 2359304 | tf_op jit(solution)/shard_map/ppermute | solution.py:53
  61.2 0.0 collective-permute-done.12.refs_3_
  61.2 0.0 copy-done.2
  61.2 3.3 %shard_map.81.refs_5_ = f32[256,4096]{1,0:T(8,128)} custom-call(bf16[256,512]{1,0:T(8,128)(2,1)S(1)} %pad_maximum_fusion.1.refs_0_, f32[1,4096]{1,0:T(1,128)S(1)} %copy-done.7, bf16[256,4096]{1,0:T(8,128)(2,1)S(1)} %copy-done.2, bf16[256,2560]{1,0:T(8,128)(2,1)S(1)} %collective-permute-done.12.refs_3_, bf16[256,2560]{1,0:T(8,128)(2,1)} %collective-permute-done.11.refs_4_), custom_call_target="tpu_custom_call" | custom-call | flops 1 | bytes 1 | tf_op jit(solution)/shard_map/pallas_call | solution.py:256
  64.6 0.0 collective-permute-done.10.refs_3_
  64.6 2.3 %shard_map.82 = f32[256,4096]{1,0:T(8,128)} custom-call(bf16[256,512]{1,0:T(8,128)(2,1)S(1)} %pad_maximum_fusion.1.refs_0_, f32[1,4096]{1,0:T(1,128)S(1)} %copy-done.7, bf16[256,4096]{1,0:T(8,128)(2,1)S(1)} %copy-done.2, bf16[256,1536]{1,0:T(8,128)(2,1)S(1)} %collective-permute-done.10.refs_3_, ...), custom_call_target="tpu_custom_call", output_to_operand_aliasing={{}: (5, {})} | custom-call | flops 1 | bytes 1 | tf_op jit(solution)/shard_map/pallas_call | solution.py:256
  (7 shorter events, 0.1 us)
Async XLA Ops:
  0.6 8.0 %copy-start = (bf16[1,256,4096]{2,1,0:T(8,128)(2,1)S(1)}, bf16[1,256,4096]{2,1,0:T(8,128)(2,1)}, u32[]{:S(2)}) copy-start(bf16[1,256,4096]{2,1,0:T(8,128)(2,1)} %param.5) | copy-start | bytes 6291460
  0.6 31.2 %collective-permute-start.6 = (bf16[256,4096]{1,0:T(8,128)(2,1)}, bf16[256,4096]{1,0:T(8,128)(2,1)}, u32[]{:S(2)}, u32[]{:S(2)}) collective-permute-start(bf16[256,4096]{1,0:T(8,128)(2,1)} %bitcast.17), channel_id=1, source_target_pairs={{0,8},{8,0},{16,24},{24,16},{1,9},{9,1},{17,25},{25,17},{2,10},{10... | collective-permute-start | bytes 6291464 | tf_op jit(solution)/shard_map/ppermute | solution.py:53
  1.4 10.6 %copy-start.6 = (bf16[1,256,1024]{2,1,0:T(8,128)(2,1)S(1)}, bf16[1,256,1024]{2,1,0:T(8,128)(2,1)}, u32[]{:S(2)}) copy-start(bf16[1,256,1024]{2,1,0:T(8,128)(2,1)} %param.8) | copy-start | bytes 1572868
  1.4 47.5 %collective-permute-start.2 = (bf16[256,4096]{1,0:T(8,128)(2,1)}, bf16[256,4096]{1,0:T(8,128)(2,1)}, u32[]{:S(2)}, u32[]{:S(2)}) collective-permute-start(bf16[256,4096]{1,0:T(8,128)(2,1)} %bitcast.33), channel_id=1, source_target_pairs={{2,0},{4,2},{6,4},{3,1},{5,3},{7,5},{10,8},{12,10},{14,12},{11,9},... | collective-permute-start | bytes 6291464 | tf_op jit(solution)/shard_map/ppermute | solution.py:286
  7.4 35.1 %collective-permute-start.11 = (bf16[256,2560]{1,0:T(8,128)(2,1)}, bf16[256,2560]{1,0:T(8,128)(2,1)}, u32[]{:S(2)}, u32[]{:S(2)}) collective-permute-start(bf16[256,2560]{1,0:T(8,128)(2,1)} %slice.18), channel_id=1, source_target_pairs={{0,16},{8,24},{16,0},{24,8},{1,17},{9,25},{17,1},{25,9},{2,18},{10... | collective-permute-start | bytes 3932168 | tf_op jit(solution)/shard_map/ppermute | solution.py:53
  9.1 7.1 %copy-start.7 = (f32[1,4096]{1,0:T(1,128)S(1)}, f32[1,4096]{1,0:T(1,128)}, u32[]{:S(2)}) copy-start(f32[1,4096]{1,0:T(1,128)} %refs_1_.3) | copy-start | bytes 49156
  9.1 2.9 %collective-permute-start = (f32[1,256]{1,0:T(1,128)S(1)}, f32[1,256]{1,0:T(1,128)S(1)}, u32[]{:S(2)}, u32[]{:S(2)}) collective-permute-start(f32[1,256]{1,0:T(1,128)S(1)} %bitcast.27), channel_id=1, source_target_pairs={{0,1},{1,0},{2,3},{3,2},{4,5},{5,4},{6,7},{7,6},{8,9},{9,8},{10,11... | collective-permute-start | bytes 3080 | tf_op jit(solution)/shard_map/ppermute | solution.py:36
  13.0 2.6 %collective-permute-start.3 = (bf16[2,256,256]{2,1,0:T(8,128)(2,1)S(1)}, bf16[2,256,256]{2,1,0:T(8,128)(2,1)S(1)}, u32[]{:S(2)}, u32[]{:S(2)}) collective-permute-start(bf16[2,256,256]{2,1,0:T(8,128)(2,1)S(1)} %pad_maximum_fusion), channel_id=1, source_target_pairs={{0,8},{8,0},{16,24},{24,16},{1,9},{9,1},{17,25},{25,17},{2,10},{10... | collective-permute-start | bytes 786440 | tf_op jit(solution)/shard_map/ppermute | solution.py:53
  15.6 25.6 %collective-permute-start.4 = (bf16[256,256]{1,0:T(8,128)(2,1)S(1)}, bf16[256,256]{1,0:T(8,128)(2,1)}, u32[]{:S(2)}, u32[]{:S(2)}) collective-permute-start(bf16[256,256]{1,0:T(8,128)(2,1)S(1)} %fusion), channel_id=1, source_target_pairs={{0,24},{8,16},{16,8},{24,0},{1,25},{9,17},{17,9},{25,1},{2,26},{10... | collective-permute-start | bytes 393224 | tf_op jit(solution)/shard_map/ppermute | solution.py:53
  16.2 3.4 %copy-start.3 = (bf16[1,1024,4096]{2,1,0:T(8,128)(2,1)S(1)}, bf16[1,1024,4096]{2,1,0:T(8,128)(2,1)}, u32[]{:S(2)}) copy-start(bf16[1,1024,4096]{2,1,0:T(8,128)(2,1)} %param.7) | copy-start | bytes 25165828
  24.2 2.9 %collective-permute-start.1 = (f32[1,256]{1,0:T(1,128)S(1)}, f32[1,256]{1,0:T(1,128)S(1)}, u32[]{:S(2)}, u32[]{:S(2)}) collective-permute-start(f32[1,256]{1,0:T(1,128)S(1)} %get-tuple-element.11.refs_2_), channel_id=1, source_target_pairs={{0,1},{1,0},{2,3},{3,2},{4,5},{5,4},{6,7},{7,6},{8,9},{9,8},{10,11... | collective-permute-start | bytes 3080 | tf_op jit(solution)/shard_map/ppermute | solution.py:36
  27.1 4.8 %copy-start.8 = (bf16[256,256]{1,0:T(8,128)(2,1)S(1)}, bf16[256,256]{1,0:T(8,128)(2,1)}, u32[]{:S(2)}) copy-start(bf16[256,256]{1,0:T(8,128)(2,1)} %get-tuple-element.19) | copy-start | bytes 393220
  28.5 1.3 %copy-start.4 = (bf16[256,4096]{1,0:T(8,128)(2,1)}, bf16[256,4096]{1,0:T(8,128)(2,1)S(1)}, u32[]{:S(2)}) copy-start(bf16[256,4096]{1,0:T(8,128)(2,1)S(1)} %shard_map.77.local_ref) | copy-start | bytes 6291460
  29.8 11.5 %collective-permute-start.7 = (f32[1,4096]{1,0:T(1,128)S(1)}, f32[1,4096]{1,0:T(1,128)S(1)}, u32[]{:S(2)}, u32[]{:S(2)}) collective-permute-start(f32[1,4096]{1,0:T(1,128)S(1)} %get-tuple-element.15), channel_id=1, source_target_pairs={{0,24},{8,16},{16,8},{24,0},{1,25},{9,17},{17,9},{25,1},{2,26},{10... | collective-permute-start | bytes 49160 | tf_op jit(solution)/shard_map/ppermute | solution.py:53
  35.5 1.3 %copy-start.1 = (bf16[256,4096]{1,0:T(8,128)(2,1)}, bf16[256,4096]{1,0:T(8,128)(2,1)S(1)}, u32[]{:S(2)}) copy-start(bf16[256,4096]{1,0:T(8,128)(2,1)S(1)} %shard_map.80.refs_2_) | copy-start | bytes 6291460
  41.3 19.2 %collective-permute-start.8 = (bf16[256,1536]{1,0:T(8,128)(2,1)S(1)}, bf16[256,1536]{1,0:T(8,128)(2,1)S(1)}, u32[]{:S(2)}, u32[]{:S(2)}) collective-permute-start(bf16[256,1536]{1,0:T(8,128)(2,1)S(1)} %slice.14), channel_id=1, source_target_pairs={{0,16},{8,24},{16,0},{24,8},{1,17},{9,25},{17,1},{25,9},{2,18},{10... | collective-permute-start | bytes 2359304 | tf_op jit(solution)/shard_map/ppermute | solution.py:53
  42.5 18.7 %collective-permute-start.12 = (bf16[256,2560]{1,0:T(8,128)(2,1)}, bf16[256,2560]{1,0:T(8,128)(2,1)S(1)}, u32[]{:S(2)}, u32[]{:S(2)}) collective-permute-start(bf16[256,2560]{1,0:T(8,128)(2,1)} %collective-permute-done.11.refs_4_), channel_id=1, source_target_pairs={{0,8},{8,0},{16,24},{24,16},{1,9},{9,1},{17,25},{25,17},{2,10},{10... | collective-permute-start | bytes 3932168 | tf_op jit(solution)/shard_map/ppermute | solution.py:53
  42.8 2.8 %collective-permute-start.9 = (f32[1,4096]{1,0:T(1,128)S(1)}, f32[1,4096]{1,0:T(1,128)S(1)}, u32[]{:S(2)}, u32[]{:S(2)}) collective-permute-start(f32[1,4096]{1,0:T(1,128)S(1)} %add.106), channel_id=1, source_target_pairs={{0,8},{8,0},{16,24},{24,16},{1,9},{9,1},{17,25},{25,17},{2,10},{10... | collective-permute-start | bytes 49160 | tf_op jit(solution)/shard_map/ppermute | solution.py:53
  43.1 5.1 %collective-permute-start.5 = (bf16[256,256]{1,0:T(8,128)(2,1)}, bf16[256,256]{1,0:T(8,128)(2,1)S(1)}, u32[]{:S(2)}, u32[]{:S(2)}) collective-permute-start(bf16[256,256]{1,0:T(8,128)(2,1)} %collective-permute-done.4), channel_id=1, source_target_pairs={{0,1},{1,0},{2,3},{3,2},{4,5},{5,4},{6,7},{7,6},{8,9},{9,8},{10,11... | collective-permute-start | bytes 393224 | tf_op jit(solution)/shard_map/ppermute | solution.py:36
  48.3 13.0 %copy-start.2 = (bf16[256,4096]{1,0:T(8,128)(2,1)S(1)}, bf16[256,4096]{1,0:T(8,128)(2,1)}, u32[]{:S(2)}) copy-start(bf16[256,4096]{1,0:T(8,128)(2,1)} %copy-done.1) | copy-start | bytes 6291460
  48.9 1.6 %copy-start.5 = (bf16[256,4096]{1,0:T(8,128)(2,1)S(1)}, bf16[256,4096]{1,0:T(8,128)(2,1)}, u32[]{:S(2)}) copy-start(bf16[256,4096]{1,0:T(8,128)(2,1)} %copy-done.4) | copy-start | bytes 6291460
  60.5 4.0 %collective-permute-start.10 = (bf16[256,1536]{1,0:T(8,128)(2,1)S(1)}, bf16[256,1536]{1,0:T(8,128)(2,1)S(1)}, u32[]{:S(2)}, u32[]{:S(2)}) collective-permute-start(bf16[256,1536]{1,0:T(8,128)(2,1)S(1)} %collective-permute-done.8.refs_4_), channel_id=1, source_target_pairs={{0,8},{8,0},{16,24},{24,16},{1,9},{9,1},{17,25},{25,17},{2,10},{10... | collective-permute-start | bytes 2359304 | tf_op jit(solution)/shard_map/ppermute | solution.py:53

commit v4 on v2

--- a/solution.py
+++ b/solution.py
@@ -197,7 +197,7 @@
         in_specs=[block] * 2,
         out_specs=block,
         out_shape=jax.ShapeDtypeStruct(received.shape, received.dtype),
-        compiler_params=PARAMS,
+        compiler_params=pltpu.CompilerParams(vmem_limit_bytes=56 * MIB),
         cost_estimate=pl.CostEstimate(flops=received.size, bytes_accessed=6 * received.size, transcendentals=0),
     )(local, received)
 

time: 66.8 us -> 65.8 us (0.985)
  local copies, waits for them, and re-layouts: 15.1 us -> 13.5 us
    unnamed x25 -> x23, local copies, waits for them, and re-layouts: 10.5 us -> 8.93 us
  transfers between devices with their start and end apart: 13 -> 13, of which waited for: 5 -> 5; matrix products, arithmetic and copies ran while one was open for 10% -> 10% of each run, Pallas kernels for 24% -> 25%
where the time goes in v4:
time: 65.8 us; the launch traced here: 65.4 us
  Pallas kernels  18.9 us (29%)
  waiting for transfers between devices  17.3 us (26%)
  local copies, waits for them, and re-layouts  13.5 us (21%)
  starting transfers between devices  12.9 us (20%)
  other arithmetic  1.98 us (3%)
  between operations  0.83 us (1%)
    ppermute x1, waiting for transfers between devices, per_device(): upper = lax.ppermute(upper_grad[0], 'pipe', down)  9.49 us
    unnamed x23, local copies, waits for them, and re-layouts  8.93 us
    ppermute x3, waiting for transfers between devices, from_others(): lax.ppermute(array, axis, [(i, (i + by) % count) for i in range(count)])  6.9 us
    ppermute x9, starting transfers between devices, send(): lax.ppermute(array, self.axis, [(i, self.to(i, high, low)) for i in range...  6.86 us
    pallas_call x2, Pallas kernels, weight_columns(): pl.pallas_call(functools.partial(weight_kernel, len(scaled)), grid=(width...  5.65 us
    ppermute x3, starting transfers between devices, from_others(): lax.ppermute(array, axis, [(i, (i + by) % count) for i in range(count)])  4.6 us
    pallas_call x1, Pallas kernels, scaled_grads(): pl.pallas_call(functools.partial(grad_kernel, scale, len(sums) - 1), grid...  4.58 us
    pallas_call x1, Pallas kernels, held_product(): pl.pallas_call(held_kernel, grid=(features // tile,), in_specs=[pl.BlockS...  3.66 us
  transfers between devices with their start and end apart: 13, of which 5 were waited for; matrix products, arithmetic and copies ran while one was open for 10% of the time, Pallas kernels for 25%

profile of v4, /device:TPU:0, one launch (start us, length us, event | category | flops | bytes accessed | tf_op | source)
XLA Modules:
  0.0 65.4 jit_solution(14787590297017067168)
XLA Ops:
  0.6 0.0 copy-start
  0.6 0.0 copy-start.5
  0.7 0.5 collective-permute-start.6
  1.2 2.7 %slice.18 = bf16[256,2560]{1,0:T(8,128)(2,1)} slice(bf16[256,4096]{1,0:T(8,128)(2,1)} %bitcast.18), slice={[0:256], [0:2560]} | slice | bytes 2621440 | tf_op jit(solution)/shard_map/slice | solution.py:296
  3.9 2.4 %collective-permute-start.11 = (bf16[256,2560]{1,0:T(8,128)(2,1)}, bf16[256,2560]{1,0:T(8,128)(2,1)}, u32[]{:S(2)}, u32[]{:S(2)}) collective-permute-start(bf16[256,2560]{1,0:T(8,128)(2,1)} %slice.18), channel_id=1, source_target_pairs={{0,16},{8,24},{16,0},{24,8},{1,17},{9,25},{17,1},{25,9},{2,18},{10... | collective-permute-start | bytes 3932168 | tf_op jit(solution)/shard_map/ppermute | solution.py:53
  6.4 0.0 copy-start.8
  6.4 1.4 %collective-permute-start.2 = (bf16[256,4096]{1,0:T(8,128)(2,1)}, bf16[256,4096]{1,0:T(8,128)(2,1)}, u32[]{:S(2)}, u32[]{:S(2)}) collective-permute-start(bf16[256,4096]{1,0:T(8,128)(2,1)} %bitcast.33), channel_id=1, source_target_pairs={{2,0},{4,2},{6,4},{3,1},{5,3},{7,5},{10,8},{12,10},{14,12},{11,9},... | collective-permute-start | bytes 6291464 | tf_op jit(solution)/shard_map/ppermute | solution.py:300
  7.8 0.0 copy-done
  7.8 0.5 multiply_reduce_fusion
  8.3 1.6 %collective-permute-start = (f32[1,256]{1,0:T(1,128)S(1)}, f32[1,256]{1,0:T(1,128)S(1)}, u32[]{:S(2)}, u32[]{:S(2)}) collective-permute-start(f32[1,256]{1,0:T(1,128)S(1)} %bitcast.27), channel_id=1, source_target_pairs={{0,1},{1,0},{2,3},{3,2},{4,5},{5,4},{6,7},{7,6},{8,9},{9,8},{10,11... | collective-permute-start | bytes 3080 | tf_op jit(solution)/shard_map/ppermute | solution.py:36
  9.8 2.1 %collective-permute-done.refs_1_ = f32[1,256]{1,0:T(1,128)S(1)} collective-permute-done((f32[1,256]{1,0:T(1,128)S(1)}, f32[1,256]{1,0:T(1,128)S(1)}, u32[]{:S(2)}, u32[]{:S(2)}) %collective-permute-start) | collective-permute-done | bytes 1056 | tf_op jit(solution)/shard_map/ppermute | solution.py:36
  11.9 0.0 copy-done.5
  11.9 0.2 shard_map.79
  12.1 0.7 %dynamic-slice_bitcast_fusion = (bf16[256,256]{1,0:T(8,128)(2,1)}, bf16[1,256,256]{2,1,0:T(8,128)(2,1)S(1)}, bf16[1,256,256]{2,1,0:T(8,128)(2,1)S(1)}, bf16[256,256]{1,0:T(8,128)(2,1)}) fusion(bf16[4,256,256]{2,1,0:T(8,128)(2,1)S(1)} %bitcast.26, s32[]{:T(128)S(6)} %select_n.91, s32[]{:T(128)S(6)} %select_n.84, s32[]{:T(128)S(6)} %select_n.82, s32[]{:T(128)S(6)} %select_n.80), kind=kLoop, calls=%fused_computation.9 | loop fusion | bytes 1048592 | tf_op jit(solution)/shard_map/jit(dynamic_index_in_dim)/squeeze | solution.py:312
  12.9 0.7 %pad_maximum_fusion = bf16[2,256,256]{2,1,0:T(8,128)(2,1)} fusion(bf16[1,256,256]{2,1,0:T(8,128)(2,1)S(1)} %get-tuple-element.20, bf16[1,256,256]{2,1,0:T(8,128)(2,1)S(1)} %get-tuple-element.21), kind=kLoop, calls=%fused_computation.1 | loop fusion | flops 131072 | bytes 524288 | tf_op jit(solution)/shard_map/stack | solution.py:315
  13.6 0.0 collective-permute-start.3
  13.6 0.0 copy-done.8
  13.6 0.0 copy-start.3
  13.6 3.4 %copy-done.3 = bf16[1,1024,4096]{2,1,0:T(8,128)(2,1)S(1)} copy-done((bf16[1,1024,4096]{2,1,0:T(8,128)(2,1)S(1)}, bf16[1,1024,4096]{2,1,0:T(8,128)(2,1)}, u32[]{:S(2)}) %copy-start.3) | copy-done | bytes 8388632
  17.0 4.6 %shard_map.76 = (bf16[256,4096]{1,0:T(8,128)(2,1)S(1)}, f32[1,4096]{1,0:T(1,128)S(1)}, f32[1,256]{1,0:T(1,128)S(1)}) custom-call(f32[1,256]{1,0:T(1,128)S(1)} %bitcast.29, f32[1,256]{1,0:T(1,128)S(1)} %collective-permute-done.refs_1_, bf16[256,1024]{1,0:T(8,128)(2,1)S(1)} %bitcast.25, bf16[1024,4096]{1,0:T(8,128)(2,1)S(1)} %bitcast.23, ...), custom_call_target="tpu_custom_call" | custom-call | flops 2147483648 | bytes 13107200 | tf_op jit(solution)/shard_map/pallas_call | solution.py:122
  21.6 0.0 copy-start.6
  21.6 1.3 %copy-done.6 = bf16[256,4096]{1,0:T(8,128)(2,1)} copy-done((bf16[256,4096]{1,0:T(8,128)(2,1)}, bf16[256,4096]{1,0:T(8,128)(2,1)S(1)}, u32[]{:S(2)}) %copy-start.6) | copy-done | bytes 2097176
  22.9 1.5 %collective-permute-start.1 = (f32[1,256]{1,0:T(1,128)S(1)}, f32[1,256]{1,0:T(1,128)S(1)}, u32[]{:S(2)}, u32[]{:S(2)}) collective-permute-start(f32[1,256]{1,0:T(1,128)S(1)} %get-tuple-element.11.refs_2_), channel_id=1, source_target_pairs={{0,1},{1,0},{2,3},{3,2},{4,5},{5,4},{6,7},{7,6},{8,9},{9,8},{10,11... | collective-permute-start | bytes 3080 | tf_op jit(solution)/shard_map/ppermute | solution.py:36
  24.4 0.1 slice.14
  24.5 2.0 %collective-permute-done.1.refs_3_ = f32[1,256]{1,0:T(1,128)S(1)} collective-permute-done((f32[1,256]{1,0:T(1,128)S(1)}, f32[1,256]{1,0:T(1,128)S(1)}, u32[]{:S(2)}, u32[]{:S(2)}) %collective-permute-start.1) | collective-permute-done | bytes 1056 | tf_op jit(solution)/shard_map/ppermute | solution.py:36
  26.5 0.0 copy-start.7
  26.5 1.6 %copy-done.7 = bf16[256,4096]{1,0:T(8,128)(2,1)S(1)} copy-done((bf16[256,4096]{1,0:T(8,128)(2,1)S(1)}, bf16[256,4096]{1,0:T(8,128)(2,1)}, u32[]{:S(2)}) %copy-start.7) | copy-done | bytes 2097176
  28.1 0.0 copy-start.9
  28.1 0.0 copy-start.10
  28.1 1.4 %shard_map.77.local_ref = bf16[256,4096]{1,0:T(8,128)(2,1)S(1)} custom-call(f32[1,256]{1,0:T(1,128)S(1)} %bitcast.30, f32[1,256]{1,0:T(1,128)S(1)} %collective-permute-done.refs_1_, f32[1,256]{1,0:T(1,128)S(1)} %get-tuple-element.11.refs_2_, f32[1,256]{1,0:T(1,128)S(1)} %collective-permute-done.1.refs_3_, bf16[256,4096]{1,0:T(8,128)(2,1)S(1)} %copy-done.7, ...), custom_call_target="tpu_custom_call" | custom-call | flops 3145728 | bytes 6291456 | tf_op jit(solution)/shard_map/pallas_call | solution.py:174
  29.5 0.0 copy-start.4
  29.5 1.3 %copy-done.4 = bf16[256,4096]{1,0:T(8,128)(2,1)} copy-done((bf16[256,4096]{1,0:T(8,128)(2,1)}, bf16[256,4096]{1,0:T(8,128)(2,1)S(1)}, u32[]{:S(2)}) %copy-start.4) | copy-done | bytes 2097176
  30.8 0.0 collective-permute-start.7
  30.8 0.0 collective-permute-done.3
  30.8 1.0 %slice_bitcast_fusion = (bf16[256,256]{1,0:T(8,128)(2,1)S(1)}, bf16[256,256]{1,0:T(8,128)(2,1)S(1)}) fusion(bf16[2,256,256]{2,1,0:T(8,128)(2,1)} %collective-permute-done.3), kind=kLoop, calls=%fused_computation.7 | loop fusion | bytes 524288 | tf_op jit(solution)/shard_map/squeeze | solution.py:318
  31.8 0.0 copy-done.9
  31.8 0.1 fusion
  31.9 1.8 %collective-permute-start.4 = (bf16[256,256]{1,0:T(8,128)(2,1)S(1)}, bf16[256,256]{1,0:T(8,128)(2,1)S(1)}, u32[]{:S(2)}, u32[]{:S(2)}) collective-permute-start(bf16[256,256]{1,0:T(8,128)(2,1)S(1)} %fusion), channel_id=1, source_target_pairs={{0,24},{8,16},{16,8},{24,0},{1,25},{9,17},{17,9},{25,1},{2,26},{10... | collective-permute-start | bytes 393224 | tf_op jit(solution)/shard_map/ppermute | solution.py:53
  33.7 0.0 copy-done.10
  33.7 0.0 collective-permute-done.6.refs_1_
  33.7 3.7 %shard_map.80.refs_2_ = bf16[256,4096]{1,0:T(8,128)(2,1)S(1)} custom-call(bf16[256,512]{1,0:T(8,128)(2,1)S(1)} %pad_maximum_fusion.2.scaled_ref, bf16[256,4096]{1,0:T(8,128)(2,1)S(1)} %bitcast.22, bf16[256,4096]{1,0:T(8,128)(2,1)} %collective-permute-done.6.refs_1_), custom_call_target="tpu_custom_call" | custom-call | flops 1073741824 | bytes 6553600 | tf_op jit(solution)/shard_map/pallas_call | solution.py:224
  37.4 0.0 copy-start.1
  37.4 1.3 %copy-done.1 = bf16[256,4096]{1,0:T(8,128)(2,1)} copy-done((bf16[256,4096]{1,0:T(8,128)(2,1)}, bf16[256,4096]{1,0:T(8,128)(2,1)S(1)}, u32[]{:S(2)}) %copy-start.1) | copy-done | bytes 2097176
  38.7 0.0 collective-permute-done.7
  38.7 0.0 collective-permute-done.4
  38.7 1.5 %collective-permute-start.8 = (bf16[256,1536]{1,0:T(8,128)(2,1)S(1)}, bf16[256,1536]{1,0:T(8,128)(2,1)S(1)}, u32[]{:S(2)}, u32[]{:S(2)}) collective-permute-start(bf16[256,1536]{1,0:T(8,128)(2,1)S(1)} %slice.14), channel_id=1, source_target_pairs={{0,16},{8,24},{16,0},{24,8},{1,17},{9,25},{17,1},{25,9},{2,18},{10... | collective-permute-start | bytes 2359304 | tf_op jit(solution)/shard_map/ppermute | solution.py:53
  40.2 0.0 collective-permute-done.11.refs_4_
  40.2 0.5 collective-permute-start.12
  40.7 0.1 collective-permute-start.9
  40.8 1.6 %collective-permute-start.5 = (bf16[256,256]{1,0:T(8,128)(2,1)S(1)}, bf16[256,256]{1,0:T(8,128)(2,1)S(1)}, u32[]{:S(2)}, u32[]{:S(2)}) collective-permute-start(bf16[256,256]{1,0:T(8,128)(2,1)S(1)} %collective-permute-done.4), channel_id=1, source_target_pairs={{0,1},{1,0},{2,3},{3,2},{4,5},{5,4},{6,7},{7,6},{8,9},{9,8},{10,11... | collective-permute-start | bytes 393224 | tf_op jit(solution)/shard_map/ppermute | solution.py:36
  42.4 0.9 %collective-permute-done.9 = f32[1,4096]{1,0:T(1,128)S(1)} collective-permute-done((f32[1,4096]{1,0:T(1,128)S(1)}, f32[1,4096]{1,0:T(1,128)S(1)}, u32[]{:S(2)}, u32[]{:S(2)}) %collective-permute-start.9) | collective-permute-done | bytes 16416 | tf_op jit(solution)/shard_map/ppermute | solution.py:53
  43.3 0.6 add.107
  43.9 2.8 %collective-permute-done.5 = bf16[256,256]{1,0:T(8,128)(2,1)S(1)} collective-permute-done((bf16[256,256]{1,0:T(8,128)(2,1)S(1)}, bf16[256,256]{1,0:T(8,128)(2,1)S(1)}, u32[]{:S(2)}, u32[]{:S(2)}) %collective-permute-start.5) | collective-permute-done | bytes 131104 | tf_op jit(solution)/shard_map/ppermute | solution.py:36
  46.8 0.0 copy-start.2
  46.8 9.5 %collective-permute-done.2.received_ref = bf16[256,4096]{1,0:T(8,128)(2,1)} collective-permute-done((bf16[256,4096]{1,0:T(8,128)(2,1)}, bf16[256,4096]{1,0:T(8,128)(2,1)}, u32[]{:S(2)}, u32[]{:S(2)}) %collective-permute-start.2) | collective-permute-done | bytes 2097184 | tf_op jit(solution)/shard_map/ppermute | solution.py:300
  56.3 3.4 %shard_map.78 = bf16[256,4096]{1,0:T(8,128)(2,1)} custom-call(bf16[256,4096]{1,0:T(8,128)(2,1)} %copy-done.4, bf16[256,4096]{1,0:T(8,128)(2,1)} %collective-permute-done.2.received_ref), custom_call_target="tpu_custom_call" | custom-call | flops 1048576 | bytes 6291456 | tf_op jit(solution)/shard_map/pallas_call | solution.py:194
  59.7 0.0 collective-permute-done.8.refs_4_
  59.7 0.0 collective-permute-start.10
  59.7 0.0 collective-permute-done.12.refs_3_
  59.7 0.0 copy-done.2
  59.7 3.3 %shard_map.81.refs_5_ = f32[256,4096]{1,0:T(8,128)} custom-call(bf16[256,512]{1,0:T(8,128)(2,1)S(1)} %pad_maximum_fusion.1.refs_0_, f32[1,4096]{1,0:T(1,128)S(1)} %copy-done.8, bf16[256,4096]{1,0:T(8,128)(2,1)S(1)} %copy-done.2, bf16[256,2560]{1,0:T(8,128)(2,1)S(1)} %collective-permute-done.12.refs_3_, bf16[256,2560]{1,0:T(8,128)(2,1)} %collective-permute-done.11.refs_4_), custom_call_target="tpu_custom_call" | custom-call | flops 671088640 | bytes 6815744 | tf_op jit(solution)/shard_map/pallas_call | solution.py:266
  63.0 0.0 collective-permute-done.10.refs_3_
  63.0 2.3 %shard_map.82 = f32[256,4096]{1,0:T(8,128)} custom-call(bf16[256,512]{1,0:T(8,128)(2,1)S(1)} %pad_maximum_fusion.1.refs_0_, f32[1,4096]{1,0:T(1,128)S(1)} %copy-done.8, bf16[256,4096]{1,0:T(8,128)(2,1)S(1)} %copy-done.2, bf16[256,1536]{1,0:T(8,128)(2,1)S(1)} %collective-permute-done.10.refs_3_, ...), custom_call_target="tpu_custom_call", output_to_operand_aliasing={{}: (5, {})} | custom-call | flops 402653184 | bytes 4194304 | tf_op jit(solution)/shard_map/pallas_call | solution.py:266
  (6 shorter events, 0.1 us)
Async XLA Ops:
  0.6 7.1 %copy-start = (bf16[1,256,4096]{2,1,0:T(8,128)(2,1)S(1)}, bf16[1,256,4096]{2,1,0:T(8,128)(2,1)}, u32[]{:S(2)}) copy-start(bf16[1,256,4096]{2,1,0:T(8,128)(2,1)} %param.5) | copy-start | bytes 6291460
  0.6 11.3 %copy-start.5 = (bf16[1,256,1024]{2,1,0:T(8,128)(2,1)S(1)}, bf16[1,256,1024]{2,1,0:T(8,128)(2,1)}, u32[]{:S(2)}) copy-start(bf16[1,256,1024]{2,1,0:T(8,128)(2,1)} %param.8) | copy-start | bytes 1572868
  0.7 33.1 %collective-permute-start.6 = (bf16[256,4096]{1,0:T(8,128)(2,1)}, bf16[256,4096]{1,0:T(8,128)(2,1)}, u32[]{:S(2)}, u32[]{:S(2)}) collective-permute-start(bf16[256,4096]{1,0:T(8,128)(2,1)} %bitcast.17), channel_id=1, source_target_pairs={{0,8},{8,0},{16,24},{24,16},{1,9},{9,1},{17,25},{25,17},{2,10},{10... | collective-permute-start | bytes 6291464 | tf_op jit(solution)/shard_map/ppermute | solution.py:53
  3.9 36.3 %collective-permute-start.11 = (bf16[256,2560]{1,0:T(8,128)(2,1)}, bf16[256,2560]{1,0:T(8,128)(2,1)}, u32[]{:S(2)}, u32[]{:S(2)}) collective-permute-start(bf16[256,2560]{1,0:T(8,128)(2,1)} %slice.18), channel_id=1, source_target_pairs={{0,16},{8,24},{16,0},{24,8},{1,17},{9,25},{17,1},{25,9},{2,18},{10... | collective-permute-start | bytes 3932168 | tf_op jit(solution)/shard_map/ppermute | solution.py:53
  6.4 7.3 %copy-start.8 = (f32[1,4096]{1,0:T(1,128)S(1)}, f32[1,4096]{1,0:T(1,128)}, u32[]{:S(2)}) copy-start(f32[1,4096]{1,0:T(1,128)} %refs_1_.3) | copy-start | bytes 49156
  6.4 49.9 %collective-permute-start.2 = (bf16[256,4096]{1,0:T(8,128)(2,1)}, bf16[256,4096]{1,0:T(8,128)(2,1)}, u32[]{:S(2)}, u32[]{:S(2)}) collective-permute-start(bf16[256,4096]{1,0:T(8,128)(2,1)} %bitcast.33), channel_id=1, source_target_pairs={{2,0},{4,2},{6,4},{3,1},{5,3},{7,5},{10,8},{12,10},{14,12},{11,9},... | collective-permute-start | bytes 6291464 | tf_op jit(solution)/shard_map/ppermute | solution.py:300
  8.3 3.6 %collective-permute-start = (f32[1,256]{1,0:T(1,128)S(1)}, f32[1,256]{1,0:T(1,128)S(1)}, u32[]{:S(2)}, u32[]{:S(2)}) collective-permute-start(f32[1,256]{1,0:T(1,128)S(1)} %bitcast.27), channel_id=1, source_target_pairs={{0,1},{1,0},{2,3},{3,2},{4,5},{5,4},{6,7},{7,6},{8,9},{9,8},{10,11... | collective-permute-start | bytes 3080 | tf_op jit(solution)/shard_map/ppermute | solution.py:36
  13.6 17.2 %collective-permute-start.3 = (bf16[2,256,256]{2,1,0:T(8,128)(2,1)}, bf16[2,256,256]{2,1,0:T(8,128)(2,1)}, u32[]{:S(2)}, u32[]{:S(2)}) collective-permute-start(bf16[2,256,256]{2,1,0:T(8,128)(2,1)} %pad_maximum_fusion), channel_id=1, source_target_pairs={{0,8},{8,0},{16,24},{24,16},{1,9},{9,1},{17,25},{25,17},{2,10},{10... | collective-permute-start | bytes 786440 | tf_op jit(solution)/shard_map/ppermute | solution.py:53
  13.6 3.4 %copy-start.3 = (bf16[1,1024,4096]{2,1,0:T(8,128)(2,1)S(1)}, bf16[1,1024,4096]{2,1,0:T(8,128)(2,1)}, u32[]{:S(2)}) copy-start(bf16[1,1024,4096]{2,1,0:T(8,128)(2,1)} %param.7) | copy-start | bytes 25165828
  21.6 1.3 %copy-start.6 = (bf16[256,4096]{1,0:T(8,128)(2,1)}, bf16[256,4096]{1,0:T(8,128)(2,1)S(1)}, u32[]{:S(2)}) copy-start(bf16[256,4096]{1,0:T(8,128)(2,1)S(1)} %get-tuple-element.12.refs_4_) | copy-start | bytes 6291460
  22.9 3.6 %collective-permute-start.1 = (f32[1,256]{1,0:T(1,128)S(1)}, f32[1,256]{1,0:T(1,128)S(1)}, u32[]{:S(2)}, u32[]{:S(2)}) collective-permute-start(f32[1,256]{1,0:T(1,128)S(1)} %get-tuple-element.11.refs_2_), channel_id=1, source_target_pairs={{0,1},{1,0},{2,3},{3,2},{4,5},{5,4},{6,7},{7,6},{8,9},{9,8},{10,11... | collective-permute-start | bytes 3080 | tf_op jit(solution)/shard_map/ppermute | solution.py:36
  26.5 1.6 %copy-start.7 = (bf16[256,4096]{1,0:T(8,128)(2,1)S(1)}, bf16[256,4096]{1,0:T(8,128)(2,1)}, u32[]{:S(2)}) copy-start(bf16[256,4096]{1,0:T(8,128)(2,1)} %copy-done.6) | copy-start | bytes 6291460
  28.1 3.7 %copy-start.9 = (bf16[256,256]{1,0:T(8,128)(2,1)S(1)}, bf16[256,256]{1,0:T(8,128)(2,1)}, u32[]{:S(2)}) copy-start(bf16[256,256]{1,0:T(8,128)(2,1)} %get-tuple-element.22) | copy-start | bytes 393220
  28.1 5.6 %copy-start.10 = (bf16[256,256]{1,0:T(8,128)(2,1)S(1)}, bf16[256,256]{1,0:T(8,128)(2,1)}, u32[]{:S(2)}) copy-start(bf16[256,256]{1,0:T(8,128)(2,1)} %get-tuple-element.19) | copy-start | bytes 393220
  29.5 1.3 %copy-start.4 = (bf16[256,4096]{1,0:T(8,128)(2,1)}, bf16[256,4096]{1,0:T(8,128)(2,1)S(1)}, u32[]{:S(2)}) copy-start(bf16[256,4096]{1,0:T(8,128)(2,1)S(1)} %shard_map.77.local_ref) | copy-start | bytes 6291460
  30.8 7.9 %collective-permute-start.7 = (f32[1,4096]{1,0:T(1,128)S(1)}, f32[1,4096]{1,0:T(1,128)S(1)}, u32[]{:S(2)}, u32[]{:S(2)}) collective-permute-start(f32[1,4096]{1,0:T(1,128)S(1)} %get-tuple-element.15), channel_id=1, source_target_pairs={{0,24},{8,16},{16,8},{24,0},{1,25},{9,17},{17,9},{25,1},{2,26},{10... | collective-permute-start | bytes 49160 | tf_op jit(solution)/shard_map/ppermute | solution.py:53
  31.9 6.8 %collective-permute-start.4 = (bf16[256,256]{1,0:T(8,128)(2,1)S(1)}, bf16[256,256]{1,0:T(8,128)(2,1)S(1)}, u32[]{:S(2)}, u32[]{:S(2)}) collective-permute-start(bf16[256,256]{1,0:T(8,128)(2,1)S(1)} %fusion), channel_id=1, source_target_pairs={{0,24},{8,16},{16,8},{24,0},{1,25},{9,17},{17,9},{25,1},{2,26},{10... | collective-permute-start | bytes 393224 | tf_op jit(solution)/shard_map/ppermute | solution.py:53
  37.4 1.3 %copy-start.1 = (bf16[256,4096]{1,0:T(8,128)(2,1)}, bf16[256,4096]{1,0:T(8,128)(2,1)S(1)}, u32[]{:S(2)}) copy-start(bf16[256,4096]{1,0:T(8,128)(2,1)S(1)} %shard_map.80.refs_2_) | copy-start | bytes 6291460
  38.7 21.0 %collective-permute-start.8 = (bf16[256,1536]{1,0:T(8,128)(2,1)S(1)}, bf16[256,1536]{1,0:T(8,128)(2,1)S(1)}, u32[]{:S(2)}, u32[]{:S(2)}) collective-permute-start(bf16[256,1536]{1,0:T(8,128)(2,1)S(1)} %slice.14), channel_id=1, source_target_pairs={{0,16},{8,24},{16,0},{24,8},{1,17},{9,25},{17,1},{25,9},{2,18},{10... | collective-permute-start | bytes 2359304 | tf_op jit(solution)/shard_map/ppermute | solution.py:53
  40.2 19.5 %collective-permute-start.12 = (bf16[256,2560]{1,0:T(8,128)(2,1)}, bf16[256,2560]{1,0:T(8,128)(2,1)S(1)}, u32[]{:S(2)}, u32[]{:S(2)}) collective-permute-start(bf16[256,2560]{1,0:T(8,128)(2,1)} %collective-permute-done.11.refs_4_), channel_id=1, source_target_pairs={{0,8},{8,0},{16,24},{24,16},{1,9},{9,1},{17,25},{25,17},{2,10},{10... | collective-permute-start | bytes 3932168 | tf_op jit(solution)/shard_map/ppermute | solution.py:53
  40.7 2.5 %collective-permute-start.9 = (f32[1,4096]{1,0:T(1,128)S(1)}, f32[1,4096]{1,0:T(1,128)S(1)}, u32[]{:S(2)}, u32[]{:S(2)}) collective-permute-start(f32[1,4096]{1,0:T(1,128)S(1)} %add.106), channel_id=1, source_target_pairs={{0,8},{8,0},{16,24},{24,16},{1,9},{9,1},{17,25},{25,17},{2,10},{10... | collective-permute-start | bytes 49160 | tf_op jit(solution)/shard_map/ppermute | solution.py:53
  40.8 5.9 %collective-permute-start.5 = (bf16[256,256]{1,0:T(8,128)(2,1)S(1)}, bf16[256,256]{1,0:T(8,128)(2,1)S(1)}, u32[]{:S(2)}, u32[]{:S(2)}) collective-permute-start(bf16[256,256]{1,0:T(8,128)(2,1)S(1)} %collective-permute-done.4), channel_id=1, source_target_pairs={{0,1},{1,0},{2,3},{3,2},{4,5},{5,4},{6,7},{7,6},{8,9},{9,8},{10,11... | collective-permute-start | bytes 393224 | tf_op jit(solution)/shard_map/ppermute | solution.py:36
  46.8 12.9 %copy-start.2 = (bf16[256,4096]{1,0:T(8,128)(2,1)S(1)}, bf16[256,4096]{1,0:T(8,128)(2,1)}, u32[]{:S(2)}) copy-start(bf16[256,4096]{1,0:T(8,128)(2,1)} %copy-done.1) | copy-start | bytes 6291460
  59.7 3.4 %collective-permute-start.10 = (bf16[256,1536]{1,0:T(8,128)(2,1)S(1)}, bf16[256,1536]{1,0:T(8,128)(2,1)S(1)}, u32[]{:S(2)}, u32[]{:S(2)}) collective-permute-start(bf16[256,1536]{1,0:T(8,128)(2,1)S(1)} %collective-permute-done.8.refs_4_), channel_id=1, source_target_pairs={{0,8},{8,0},{16,24},{24,16},{1,9},{9,1},{17,25},{25,17},{2,10},{10... | collective-permute-start | bytes 2359304 | tf_op jit(solution)/shard_map/ppermute | solution.py:53

commit v5 on v4

--- a/solution.py
+++ b/solution.py
@@ -189,7 +189,7 @@
 
 def add_rows(local, received):
     tokens, features = received.shape
-    tile = tile_of(tokens, 128)
+    tile = tile_of(tokens, 64)
     block = pl.BlockSpec((tile, features), lambda r: (r, 0))
     return pl.pallas_call(
         add_kernel,

time: 65.8 us -> 66.8 us (1.015)
  Pallas kernels: 18.9 us -> 19.8 us
    pallas_call x1, Pallas kernels: 3.38 us -> 4.3 us  [add_rows(): pl.pallas_call(add_kernel, grid=(tokens // tile,), in_specs=[block] * 2,...]
  transfers between devices with their start and end apart: 13 -> 13, of which waited for: 5 -> 5; matrix products, arithmetic and copies ran while one was open for 10% -> 10% of each run, Pallas kernels for 25% -> 26%
where the time goes in v5:
time: 66.8 us; the launch traced here: 66.3 us
  Pallas kernels  19.8 us (30%)
  waiting for transfers between devices  17.3 us (26%)
  local copies, waits for them, and re-layouts  13.5 us (20%)
  starting transfers between devices  12.9 us (19%)
  other arithmetic  1.98 us (3%)
  between operations  0.83 us (1%)
    ppermute x1, waiting for transfers between devices, per_device(): upper = lax.ppermute(upper_grad[0], 'pipe', down)  9.49 us
    unnamed x23, local copies, waits for them, and re-layouts  8.93 us
    ppermute x3, waiting for transfers between devices, from_others(): lax.ppermute(array, axis, [(i, (i + by) % count) for i in range(count)])  6.9 us
    ppermute x9, starting transfers between devices, send(): lax.ppermute(array, self.axis, [(i, self.to(i, high, low)) for i in range...  6.86 us
    pallas_call x2, Pallas kernels, weight_columns(): pl.pallas_call(functools.partial(weight_kernel, len(scaled)), grid=(width...  5.65 us
    ppermute x3, starting transfers between devices, from_others(): lax.ppermute(array, axis, [(i, (i + by) % count) for i in range(count)])  4.6 us
    pallas_call x1, Pallas kernels, scaled_grads(): pl.pallas_call(functools.partial(grad_kernel, scale, len(sums) - 1), grid...  4.58 us
    pallas_call x1, Pallas kernels, add_rows(): pl.pallas_call(add_kernel, grid=(tokens // tile,), in_specs=[block] * 2,...  4.3 us
  transfers between devices with their start and end apart: 13, of which 5 were waited for; matrix products, arithmetic and copies ran while one was open for 10% of the time, Pallas kernels for 26%

profile of v5, /device:TPU:0, one launch (start us, length us, event | category | flops | bytes accessed | tf_op | source)
XLA Modules:
  0.0 66.3 jit_solution(1503334526101582288)
XLA Ops:
  0.6 0.0 copy-start
  0.6 0.0 copy-start.5
  0.7 0.5 collective-permute-start.6
  1.2 2.7 %slice.18 = bf16[256,2560]{1,0:T(8,128)(2,1)} slice(bf16[256,4096]{1,0:T(8,128)(2,1)} %bitcast.18), slice={[0:256], [0:2560]} | slice | bytes 2621440 | tf_op jit(solution)/shard_map/slice | solution.py:296
  3.9 2.4 %collective-permute-start.11 = (bf16[256,2560]{1,0:T(8,128)(2,1)}, bf16[256,2560]{1,0:T(8,128)(2,1)}, u32[]{:S(2)}, u32[]{:S(2)}) collective-permute-start(bf16[256,2560]{1,0:T(8,128)(2,1)} %slice.18), channel_id=1, source_target_pairs={{0,16},{8,24},{16,0},{24,8},{1,17},{9,25},{17,1},{25,9},{2,18},{10... | collective-permute-start | bytes 3932168 | tf_op jit(solution)/shard_map/ppermute | solution.py:53
  6.4 0.0 copy-start.8
  6.4 1.4 %collective-permute-start.2 = (bf16[256,4096]{1,0:T(8,128)(2,1)}, bf16[256,4096]{1,0:T(8,128)(2,1)}, u32[]{:S(2)}, u32[]{:S(2)}) collective-permute-start(bf16[256,4096]{1,0:T(8,128)(2,1)} %bitcast.33), channel_id=1, source_target_pairs={{2,0},{4,2},{6,4},{3,1},{5,3},{7,5},{10,8},{12,10},{14,12},{11,9},... | collective-permute-start | bytes 6291464 | tf_op jit(solution)/shard_map/ppermute | solution.py:300
  7.8 0.0 copy-done
  7.8 0.5 multiply_reduce_fusion
  8.3 1.6 %collective-permute-start = (f32[1,256]{1,0:T(1,128)S(1)}, f32[1,256]{1,0:T(1,128)S(1)}, u32[]{:S(2)}, u32[]{:S(2)}) collective-permute-start(f32[1,256]{1,0:T(1,128)S(1)} %bitcast.27), channel_id=1, source_target_pairs={{0,1},{1,0},{2,3},{3,2},{4,5},{5,4},{6,7},{7,6},{8,9},{9,8},{10,11... | collective-permute-start | bytes 3080 | tf_op jit(solution)/shard_map/ppermute | solution.py:36
  9.8 2.1 %collective-permute-done.refs_1_ = f32[1,256]{1,0:T(1,128)S(1)} collective-permute-done((f32[1,256]{1,0:T(1,128)S(1)}, f32[1,256]{1,0:T(1,128)S(1)}, u32[]{:S(2)}, u32[]{:S(2)}) %collective-permute-start) | collective-permute-done | bytes 1056 | tf_op jit(solution)/shard_map/ppermute | solution.py:36
  11.9 0.0 copy-done.5
  11.9 0.2 shard_map.79
  12.1 0.7 %dynamic-slice_bitcast_fusion = (bf16[256,256]{1,0:T(8,128)(2,1)}, bf16[1,256,256]{2,1,0:T(8,128)(2,1)S(1)}, bf16[1,256,256]{2,1,0:T(8,128)(2,1)S(1)}, bf16[256,256]{1,0:T(8,128)(2,1)}) fusion(bf16[4,256,256]{2,1,0:T(8,128)(2,1)S(1)} %bitcast.26, s32[]{:T(128)S(6)} %select_n.91, s32[]{:T(128)S(6)} %select_n.84, s32[]{:T(128)S(6)} %select_n.82, s32[]{:T(128)S(6)} %select_n.80), kind=kLoop, calls=%fused_computation.9 | loop fusion | bytes 1048592 | tf_op jit(solution)/shard_map/jit(dynamic_index_in_dim)/squeeze | solution.py:312
  12.9 0.7 %pad_maximum_fusion = bf16[2,256,256]{2,1,0:T(8,128)(2,1)} fusion(bf16[1,256,256]{2,1,0:T(8,128)(2,1)S(1)} %get-tuple-element.20, bf16[1,256,256]{2,1,0:T(8,128)(2,1)S(1)} %get-tuple-element.21), kind=kLoop, calls=%fused_computation.1 | loop fusion | flops 131072 | bytes 524288 | tf_op jit(solution)/shard_map/stack | solution.py:315
  13.6 0.0 collective-permute-start.3
  13.6 0.0 copy-done.8
  13.6 0.0 copy-start.3
  13.6 3.4 %copy-done.3 = bf16[1,1024,4096]{2,1,0:T(8,128)(2,1)S(1)} copy-done((bf16[1,1024,4096]{2,1,0:T(8,128)(2,1)S(1)}, bf16[1,1024,4096]{2,1,0:T(8,128)(2,1)}, u32[]{:S(2)}) %copy-start.3) | copy-done | bytes 8388632
  17.0 4.6 %shard_map.76 = (bf16[256,4096]{1,0:T(8,128)(2,1)S(1)}, f32[1,4096]{1,0:T(1,128)S(1)}, f32[1,256]{1,0:T(1,128)S(1)}) custom-call(f32[1,256]{1,0:T(1,128)S(1)} %bitcast.29, f32[1,256]{1,0:T(1,128)S(1)} %collective-permute-done.refs_1_, bf16[256,1024]{1,0:T(8,128)(2,1)S(1)} %bitcast.25, bf16[1024,4096]{1,0:T(8,128)(2,1)S(1)} %bitcast.23, ...), custom_call_target="tpu_custom_call" | custom-call | flops 2147483648 | bytes 13107200 | tf_op jit(solution)/shard_map/pallas_call | solution.py:122
  21.6 0.0 copy-start.6
  21.6 1.3 %copy-done.6 = bf16[256,4096]{1,0:T(8,128)(2,1)} copy-done((bf16[256,4096]{1,0:T(8,128)(2,1)}, bf16[256,4096]{1,0:T(8,128)(2,1)S(1)}, u32[]{:S(2)}) %copy-start.6) | copy-done | bytes 2097176
  22.9 1.5 %collective-permute-start.1 = (f32[1,256]{1,0:T(1,128)S(1)}, f32[1,256]{1,0:T(1,128)S(1)}, u32[]{:S(2)}, u32[]{:S(2)}) collective-permute-start(f32[1,256]{1,0:T(1,128)S(1)} %get-tuple-element.11.refs_2_), channel_id=1, source_target_pairs={{0,1},{1,0},{2,3},{3,2},{4,5},{5,4},{6,7},{7,6},{8,9},{9,8},{10,11... | collective-permute-start | bytes 3080 | tf_op jit(solution)/shard_map/ppermute | solution.py:36
  24.4 0.1 slice.14
  24.5 2.0 %collective-permute-done.1.refs_3_ = f32[1,256]{1,0:T(1,128)S(1)} collective-permute-done((f32[1,256]{1,0:T(1,128)S(1)}, f32[1,256]{1,0:T(1,128)S(1)}, u32[]{:S(2)}, u32[]{:S(2)}) %collective-permute-start.1) | collective-permute-done | bytes 1056 | tf_op jit(solution)/shard_map/ppermute | solution.py:36
  26.5 0.0 copy-start.7
  26.5 1.6 %copy-done.7 = bf16[256,4096]{1,0:T(8,128)(2,1)S(1)} copy-done((bf16[256,4096]{1,0:T(8,128)(2,1)S(1)}, bf16[256,4096]{1,0:T(8,128)(2,1)}, u32[]{:S(2)}) %copy-start.7) | copy-done | bytes 2097176
  28.1 0.0 copy-start.9
  28.1 0.0 copy-start.10
  28.1 1.4 %shard_map.77.local_ref = bf16[256,4096]{1,0:T(8,128)(2,1)S(1)} custom-call(f32[1,256]{1,0:T(1,128)S(1)} %bitcast.30, f32[1,256]{1,0:T(1,128)S(1)} %collective-permute-done.refs_1_, f32[1,256]{1,0:T(1,128)S(1)} %get-tuple-element.11.refs_2_, f32[1,256]{1,0:T(1,128)S(1)} %collective-permute-done.1.refs_3_, bf16[256,4096]{1,0:T(8,128)(2,1)S(1)} %copy-done.7, ...), custom_call_target="tpu_custom_call" | custom-call | flops 3145728 | bytes 6291456 | tf_op jit(solution)/shard_map/pallas_call | solution.py:174
  29.5 0.0 copy-start.4
  29.5 1.3 %copy-done.4 = bf16[256,4096]{1,0:T(8,128)(2,1)} copy-done((bf16[256,4096]{1,0:T(8,128)(2,1)}, bf16[256,4096]{1,0:T(8,128)(2,1)S(1)}, u32[]{:S(2)}) %copy-start.4) | copy-done | bytes 2097176
  30.8 0.0 collective-permute-start.7
  30.8 0.0 collective-permute-done.3
  30.8 1.0 %slice_bitcast_fusion = (bf16[256,256]{1,0:T(8,128)(2,1)S(1)}, bf16[256,256]{1,0:T(8,128)(2,1)S(1)}) fusion(bf16[2,256,256]{2,1,0:T(8,128)(2,1)} %collective-permute-done.3), kind=kLoop, calls=%fused_computation.7 | loop fusion | bytes 524288 | tf_op jit(solution)/shard_map/squeeze | solution.py:318
  31.8 0.0 copy-done.9
  31.8 0.1 fusion
  31.9 1.8 %collective-permute-start.4 = (bf16[256,256]{1,0:T(8,128)(2,1)S(1)}, bf16[256,256]{1,0:T(8,128)(2,1)S(1)}, u32[]{:S(2)}, u32[]{:S(2)}) collective-permute-start(bf16[256,256]{1,0:T(8,128)(2,1)S(1)} %fusion), channel_id=1, source_target_pairs={{0,24},{8,16},{16,8},{24,0},{1,25},{9,17},{17,9},{25,1},{2,26},{10... | collective-permute-start | bytes 393224 | tf_op jit(solution)/shard_map/ppermute | solution.py:53
  33.7 0.0 copy-done.10
  33.7 0.0 collective-permute-done.6.refs_1_
  33.7 3.7 %shard_map.80.refs_2_ = bf16[256,4096]{1,0:T(8,128)(2,1)S(1)} custom-call(bf16[256,512]{1,0:T(8,128)(2,1)S(1)} %pad_maximum_fusion.2.scaled_ref, bf16[256,4096]{1,0:T(8,128)(2,1)S(1)} %bitcast.22, bf16[256,4096]{1,0:T(8,128)(2,1)} %collective-permute-done.6.refs_1_), custom_call_target="tpu_custom_call" | custom-call | flops 1073741824 | bytes 6553600 | tf_op jit(solution)/shard_map/pallas_call | solution.py:224
  37.4 0.0 copy-start.1
  37.4 1.3 %copy-done.1 = bf16[256,4096]{1,0:T(8,128)(2,1)} copy-done((bf16[256,4096]{1,0:T(8,128)(2,1)}, bf16[256,4096]{1,0:T(8,128)(2,1)S(1)}, u32[]{:S(2)}) %copy-start.1) | copy-done | bytes 2097176
  38.7 0.0 collective-permute-done.7
  38.7 0.0 collective-permute-done.4
  38.7 1.5 %collective-permute-start.8 = (bf16[256,1536]{1,0:T(8,128)(2,1)S(1)}, bf16[256,1536]{1,0:T(8,128)(2,1)S(1)}, u32[]{:S(2)}, u32[]{:S(2)}) collective-permute-start(bf16[256,1536]{1,0:T(8,128)(2,1)S(1)} %slice.14), channel_id=1, source_target_pairs={{0,16},{8,24},{16,0},{24,8},{1,17},{9,25},{17,1},{25,9},{2,18},{10... | collective-permute-start | bytes 2359304 | tf_op jit(solution)/shard_map/ppermute | solution.py:53
  40.2 0.0 collective-permute-done.11.refs_4_
  40.2 0.5 collective-permute-start.12
  40.7 0.1 collective-permute-start.9
  40.8 1.6 %collective-permute-start.5 = (bf16[256,256]{1,0:T(8,128)(2,1)S(1)}, bf16[256,256]{1,0:T(8,128)(2,1)S(1)}, u32[]{:S(2)}, u32[]{:S(2)}) collective-permute-start(bf16[256,256]{1,0:T(8,128)(2,1)S(1)} %collective-permute-done.4), channel_id=1, source_target_pairs={{0,1},{1,0},{2,3},{3,2},{4,5},{5,4},{6,7},{7,6},{8,9},{9,8},{10,11... | collective-permute-start | bytes 393224 | tf_op jit(solution)/shard_map/ppermute | solution.py:36
  42.4 0.9 %collective-permute-done.9 = f32[1,4096]{1,0:T(1,128)S(1)} collective-permute-done((f32[1,4096]{1,0:T(1,128)S(1)}, f32[1,4096]{1,0:T(1,128)S(1)}, u32[]{:S(2)}, u32[]{:S(2)}) %collective-permute-start.9) | collective-permute-done | bytes 16416 | tf_op jit(solution)/shard_map/ppermute | solution.py:53
  43.3 0.6 add.107
  43.9 2.8 %collective-permute-done.5 = bf16[256,256]{1,0:T(8,128)(2,1)S(1)} collective-permute-done((bf16[256,256]{1,0:T(8,128)(2,1)S(1)}, bf16[256,256]{1,0:T(8,128)(2,1)S(1)}, u32[]{:S(2)}, u32[]{:S(2)}) %collective-permute-start.5) | collective-permute-done | bytes 131104 | tf_op jit(solution)/shard_map/ppermute | solution.py:36
  46.8 0.0 copy-start.2
  46.8 9.5 %collective-permute-done.2.received_ref = bf16[256,4096]{1,0:T(8,128)(2,1)} collective-permute-done((bf16[256,4096]{1,0:T(8,128)(2,1)}, bf16[256,4096]{1,0:T(8,128)(2,1)}, u32[]{:S(2)}, u32[]{:S(2)}) %collective-permute-start.2) | collective-permute-done | bytes 2097184 | tf_op jit(solution)/shard_map/ppermute | solution.py:300
  56.3 4.3 %shard_map.78 = bf16[256,4096]{1,0:T(8,128)(2,1)} custom-call(bf16[256,4096]{1,0:T(8,128)(2,1)} %copy-done.4, bf16[256,4096]{1,0:T(8,128)(2,1)} %collective-permute-done.2.received_ref), custom_call_target="tpu_custom_call" | custom-call | flops 1048576 | bytes 6291456 | tf_op jit(solution)/shard_map/pallas_call | solution.py:194
  60.6 0.0 collective-permute-done.8.refs_4_
  60.6 0.0 collective-permute-start.10
  60.6 0.0 collective-permute-done.12.refs_3_
  60.6 0.0 copy-done.2
  60.6 3.3 %shard_map.81.refs_5_ = f32[256,4096]{1,0:T(8,128)} custom-call(bf16[256,512]{1,0:T(8,128)(2,1)S(1)} %pad_maximum_fusion.1.refs_0_, f32[1,4096]{1,0:T(1,128)S(1)} %copy-done.8, bf16[256,4096]{1,0:T(8,128)(2,1)S(1)} %copy-done.2, bf16[256,2560]{1,0:T(8,128)(2,1)S(1)} %collective-permute-done.12.refs_3_, bf16[256,2560]{1,0:T(8,128)(2,1)} %collective-permute-done.11.refs_4_), custom_call_target="tpu_custom_call" | custom-call | flops 671088640 | bytes 6815744 | tf_op jit(solution)/shard_map/pallas_call | solution.py:266
  64.0 0.0 collective-permute-done.10.refs_3_
  64.0 2.3 %shard_map.82 = f32[256,4096]{1,0:T(8,128)} custom-call(bf16[256,512]{1,0:T(8,128)(2,1)S(1)} %pad_maximum_fusion.1.refs_0_, f32[1,4096]{1,0:T(1,128)S(1)} %copy-done.8, bf16[256,4096]{1,0:T(8,128)(2,1)S(1)} %copy-done.2, bf16[256,1536]{1,0:T(8,128)(2,1)S(1)} %collective-permute-done.10.refs_3_, ...), custom_call_target="tpu_custom_call", output_to_operand_aliasing={{}: (5, {})} | custom-call | flops 402653184 | bytes 4194304 | tf_op jit(solution)/shard_map/pallas_call | solution.py:266
  (6 shorter events, 0.1 us)
Async XLA Ops:
  0.6 7.1 %copy-start = (bf16[1,256,4096]{2,1,0:T(8,128)(2,1)S(1)}, bf16[1,256,4096]{2,1,0:T(8,128)(2,1)}, u32[]{:S(2)}) copy-start(bf16[1,256,4096]{2,1,0:T(8,128)(2,1)} %param.5) | copy-start | bytes 6291460
  0.6 11.3 %copy-start.5 = (bf16[1,256,1024]{2,1,0:T(8,128)(2,1)S(1)}, bf16[1,256,1024]{2,1,0:T(8,128)(2,1)}, u32[]{:S(2)}) copy-start(bf16[1,256,1024]{2,1,0:T(8,128)(2,1)} %param.8) | copy-start | bytes 1572868
  0.7 33.1 %collective-permute-start.6 = (bf16[256,4096]{1,0:T(8,128)(2,1)}, bf16[256,4096]{1,0:T(8,128)(2,1)}, u32[]{:S(2)}, u32[]{:S(2)}) collective-permute-start(bf16[256,4096]{1,0:T(8,128)(2,1)} %bitcast.17), channel_id=1, source_target_pairs={{0,8},{8,0},{16,24},{24,16},{1,9},{9,1},{17,25},{25,17},{2,10},{10... | collective-permute-start | bytes 6291464 | tf_op jit(solution)/shard_map/ppermute | solution.py:53
  3.9 36.3 %collective-permute-start.11 = (bf16[256,2560]{1,0:T(8,128)(2,1)}, bf16[256,2560]{1,0:T(8,128)(2,1)}, u32[]{:S(2)}, u32[]{:S(2)}) collective-permute-start(bf16[256,2560]{1,0:T(8,128)(2,1)} %slice.18), channel_id=1, source_target_pairs={{0,16},{8,24},{16,0},{24,8},{1,17},{9,25},{17,1},{25,9},{2,18},{10... | collective-permute-start | bytes 3932168 | tf_op jit(solution)/shard_map/ppermute | solution.py:53
  6.4 7.3 %copy-start.8 = (f32[1,4096]{1,0:T(1,128)S(1)}, f32[1,4096]{1,0:T(1,128)}, u32[]{:S(2)}) copy-start(f32[1,4096]{1,0:T(1,128)} %refs_1_.3) | copy-start | bytes 49156
  6.4 49.9 %collective-permute-start.2 = (bf16[256,4096]{1,0:T(8,128)(2,1)}, bf16[256,4096]{1,0:T(8,128)(2,1)}, u32[]{:S(2)}, u32[]{:S(2)}) collective-permute-start(bf16[256,4096]{1,0:T(8,128)(2,1)} %bitcast.33), channel_id=1, source_target_pairs={{2,0},{4,2},{6,4},{3,1},{5,3},{7,5},{10,8},{12,10},{14,12},{11,9},... | collective-permute-start | bytes 6291464 | tf_op jit(solution)/shard_map/ppermute | solution.py:300
  8.3 3.6 %collective-permute-start = (f32[1,256]{1,0:T(1,128)S(1)}, f32[1,256]{1,0:T(1,128)S(1)}, u32[]{:S(2)}, u32[]{:S(2)}) collective-permute-start(f32[1,256]{1,0:T(1,128)S(1)} %bitcast.27), channel_id=1, source_target_pairs={{0,1},{1,0},{2,3},{3,2},{4,5},{5,4},{6,7},{7,6},{8,9},{9,8},{10,11... | collective-permute-start | bytes 3080 | tf_op jit(solution)/shard_map/ppermute | solution.py:36
  13.6 17.2 %collective-permute-start.3 = (bf16[2,256,256]{2,1,0:T(8,128)(2,1)}, bf16[2,256,256]{2,1,0:T(8,128)(2,1)}, u32[]{:S(2)}, u32[]{:S(2)}) collective-permute-start(bf16[2,256,256]{2,1,0:T(8,128)(2,1)} %pad_maximum_fusion), channel_id=1, source_target_pairs={{0,8},{8,0},{16,24},{24,16},{1,9},{9,1},{17,25},{25,17},{2,10},{10... | collective-permute-start | bytes 786440 | tf_op jit(solution)/shard_map/ppermute | solution.py:53
  13.6 3.4 %copy-start.3 = (bf16[1,1024,4096]{2,1,0:T(8,128)(2,1)S(1)}, bf16[1,1024,4096]{2,1,0:T(8,128)(2,1)}, u32[]{:S(2)}) copy-start(bf16[1,1024,4096]{2,1,0:T(8,128)(2,1)} %param.7) | copy-start | bytes 25165828
  21.6 1.3 %copy-start.6 = (bf16[256,4096]{1,0:T(8,128)(2,1)}, bf16[256,4096]{1,0:T(8,128)(2,1)S(1)}, u32[]{:S(2)}) copy-start(bf16[256,4096]{1,0:T(8,128)(2,1)S(1)} %get-tuple-element.12.refs_4_) | copy-start | bytes 6291460
  22.9 3.6 %collective-permute-start.1 = (f32[1,256]{1,0:T(1,128)S(1)}, f32[1,256]{1,0:T(1,128)S(1)}, u32[]{:S(2)}, u32[]{:S(2)}) collective-permute-start(f32[1,256]{1,0:T(1,128)S(1)} %get-tuple-element.11.refs_2_), channel_id=1, source_target_pairs={{0,1},{1,0},{2,3},{3,2},{4,5},{5,4},{6,7},{7,6},{8,9},{9,8},{10,11... | collective-permute-start | bytes 3080 | tf_op jit(solution)/shard_map/ppermute | solution.py:36
  26.5 1.6 %copy-start.7 = (bf16[256,4096]{1,0:T(8,128)(2,1)S(1)}, bf16[256,4096]{1,0:T(8,128)(2,1)}, u32[]{:S(2)}) copy-start(bf16[256,4096]{1,0:T(8,128)(2,1)} %copy-done.6) | copy-start | bytes 6291460
  28.1 3.7 %copy-start.9 = (bf16[256,256]{1,0:T(8,128)(2,1)S(1)}, bf16[256,256]{1,0:T(8,128)(2,1)}, u32[]{:S(2)}) copy-start(bf16[256,256]{1,0:T(8,128)(2,1)} %get-tuple-element.22) | copy-start | bytes 393220
  28.1 5.6 %copy-start.10 = (bf16[256,256]{1,0:T(8,128)(2,1)S(1)}, bf16[256,256]{1,0:T(8,128)(2,1)}, u32[]{:S(2)}) copy-start(bf16[256,256]{1,0:T(8,128)(2,1)} %get-tuple-element.19) | copy-start | bytes 393220
  29.5 1.3 %copy-start.4 = (bf16[256,4096]{1,0:T(8,128)(2,1)}, bf16[256,4096]{1,0:T(8,128)(2,1)S(1)}, u32[]{:S(2)}) copy-start(bf16[256,4096]{1,0:T(8,128)(2,1)S(1)} %shard_map.77.local_ref) | copy-start | bytes 6291460
  30.8 7.9 %collective-permute-start.7 = (f32[1,4096]{1,0:T(1,128)S(1)}, f32[1,4096]{1,0:T(1,128)S(1)}, u32[]{:S(2)}, u32[]{:S(2)}) collective-permute-start(f32[1,4096]{1,0:T(1,128)S(1)} %get-tuple-element.15), channel_id=1, source_target_pairs={{0,24},{8,16},{16,8},{24,0},{1,25},{9,17},{17,9},{25,1},{2,26},{10... | collective-permute-start | bytes 49160 | tf_op jit(solution)/shard_map/ppermute | solution.py:53
  31.9 6.8 %collective-permute-start.4 = (bf16[256,256]{1,0:T(8,128)(2,1)S(1)}, bf16[256,256]{1,0:T(8,128)(2,1)S(1)}, u32[]{:S(2)}, u32[]{:S(2)}) collective-permute-start(bf16[256,256]{1,0:T(8,128)(2,1)S(1)} %fusion), channel_id=1, source_target_pairs={{0,24},{8,16},{16,8},{24,0},{1,25},{9,17},{17,9},{25,1},{2,26},{10... | collective-permute-start | bytes 393224 | tf_op jit(solution)/shard_map/ppermute | solution.py:53
  37.4 1.3 %copy-start.1 = (bf16[256,4096]{1,0:T(8,128)(2,1)}, bf16[256,4096]{1,0:T(8,128)(2,1)S(1)}, u32[]{:S(2)}) copy-start(bf16[256,4096]{1,0:T(8,128)(2,1)S(1)} %shard_map.80.refs_2_) | copy-start | bytes 6291460
  38.7 21.9 %collective-permute-start.8 = (bf16[256,1536]{1,0:T(8,128)(2,1)S(1)}, bf16[256,1536]{1,0:T(8,128)(2,1)S(1)}, u32[]{:S(2)}, u32[]{:S(2)}) collective-permute-start(bf16[256,1536]{1,0:T(8,128)(2,1)S(1)} %slice.14), channel_id=1, source_target_pairs={{0,16},{8,24},{16,0},{24,8},{1,17},{9,25},{17,1},{25,9},{2,18},{10... | collective-permute-start | bytes 2359304 | tf_op jit(solution)/shard_map/ppermute | solution.py:53
  40.2 20.4 %collective-permute-start.12 = (bf16[256,2560]{1,0:T(8,128)(2,1)}, bf16[256,2560]{1,0:T(8,128)(2,1)S(1)}, u32[]{:S(2)}, u32[]{:S(2)}) collective-permute-start(bf16[256,2560]{1,0:T(8,128)(2,1)} %collective-permute-done.11.refs_4_), channel_id=1, source_target_pairs={{0,8},{8,0},{16,24},{24,16},{1,9},{9,1},{17,25},{25,17},{2,10},{10... | collective-permute-start | bytes 3932168 | tf_op jit(solution)/shard_map/ppermute | solution.py:53
  40.7 2.5 %collective-permute-start.9 = (f32[1,4096]{1,0:T(1,128)S(1)}, f32[1,4096]{1,0:T(1,128)S(1)}, u32[]{:S(2)}, u32[]{:S(2)}) collective-permute-start(f32[1,4096]{1,0:T(1,128)S(1)} %add.106), channel_id=1, source_target_pairs={{0,8},{8,0},{16,24},{24,16},{1,9},{9,1},{17,25},{25,17},{2,10},{10... | collective-permute-start | bytes 49160 | tf_op jit(solution)/shard_map/ppermute | solution.py:53
  40.8 5.9 %collective-permute-start.5 = (bf16[256,256]{1,0:T(8,128)(2,1)S(1)}, bf16[256,256]{1,0:T(8,128)(2,1)S(1)}, u32[]{:S(2)}, u32[]{:S(2)}) collective-permute-start(bf16[256,256]{1,0:T(8,128)(2,1)S(1)} %collective-permute-done.4), channel_id=1, source_target_pairs={{0,1},{1,0},{2,3},{3,2},{4,5},{5,4},{6,7},{7,6},{8,9},{9,8},{10,11... | collective-permute-start | bytes 393224 | tf_op jit(solution)/shard_map/ppermute | solution.py:36
  46.8 13.8 %copy-start.2 = (bf16[256,4096]{1,0:T(8,128)(2,1)S(1)}, bf16[256,4096]{1,0:T(8,128)(2,1)}, u32[]{:S(2)}) copy-start(bf16[256,4096]{1,0:T(8,128)(2,1)} %copy-done.1) | copy-start | bytes 6291460
  60.6 3.4 %collective-permute-start.10 = (bf16[256,1536]{1,0:T(8,128)(2,1)S(1)}, bf16[256,1536]{1,0:T(8,128)(2,1)S(1)}, u32[]{:S(2)}, u32[]{:S(2)}) collective-permute-start(bf16[256,1536]{1,0:T(8,128)(2,1)S(1)} %collective-permute-done.8.refs_4_), channel_id=1, source_target_pairs={{0,8},{8,0},{16,24},{24,16},{1,9},{9,1},{17,25},{25,17},{2,10},{10... | collective-permute-start | bytes 2359304 | tf_op jit(solution)/shard_map/ppermute | solution.py:53

commit v6 on v5

--- a/solution.py
+++ b/solution.py
@@ -189,7 +189,7 @@
 
 def add_rows(local, received):
     tokens, features = received.shape
-    tile = tile_of(tokens, 64)
+    tile = tile_of(tokens, 256)
     block = pl.BlockSpec((tile, features), lambda r: (r, 0))
     return pl.pallas_call(
         add_kernel,

time: 66.8 us -> 66.4 us (level)
  no operation moved by 1% of the time
where the time goes in v6:
time: 66.4 us; the launch traced here: 66 us
  Pallas kernels  19.5 us (29%)
  waiting for transfers between devices  17.3 us (26%)
  local copies, waits for them, and re-layouts  13.5 us (20%)
  starting transfers between devices  12.9 us (19%)
  other arithmetic  1.98 us (3%)
  between operations  0.82 us (1%)
    ppermute x1, waiting for transfers between devices, per_device(): upper = lax.ppermute(upper_grad[0], 'pipe', down)  9.49 us
    unnamed x23, local copies, waits for them, and re-layouts  8.93 us
    ppermute x3, waiting for transfers between devices, from_others(): lax.ppermute(array, axis, [(i, (i + by) % count) for i in range(count)])  6.9 us
    ppermute x9, starting transfers between devices, send(): lax.ppermute(array, self.axis, [(i, self.to(i, high, low)) for i in range...  6.86 us
    pallas_call x2, Pallas kernels, weight_columns(): pl.pallas_call(functools.partial(weight_kernel, len(scaled)), grid=(width...  5.65 us
    ppermute x3, starting transfers between devices, from_others(): lax.ppermute(array, axis, [(i, (i + by) % count) for i in range(count)])  4.6 us
    pallas_call x1, Pallas kernels, scaled_grads(): pl.pallas_call(functools.partial(grad_kernel, scale, len(sums) - 1), grid...  4.58 us
    pallas_call x1, Pallas kernels, add_rows(): pl.pallas_call(add_kernel, grid=(tokens // tile,), in_specs=[block] * 2,...  4.02 us
  transfers between devices with their start and end apart: 13, of which 5 were waited for; matrix products, arithmetic and copies ran while one was open for 10% of the time, Pallas kernels for 26%

profile of v6, /device:TPU:0, one launch (start us, length us, event | category | flops | bytes accessed | tf_op | source)
XLA Modules:
  0.0 66.0 jit_solution(5511591498824292397)
XLA Ops:
  0.6 0.0 copy-start
  0.6 0.0 copy-start.5
  0.7 0.5 collective-permute-start.6
  1.2 2.7 %slice.18 = bf16[256,2560]{1,0:T(8,128)(2,1)} slice(bf16[256,4096]{1,0:T(8,128)(2,1)} %bitcast.18), slice={[0:256], [0:2560]} | slice | bytes 2621440 | tf_op jit(solution)/shard_map/slice | solution.py:296
  3.9 2.4 %collective-permute-start.11 = (bf16[256,2560]{1,0:T(8,128)(2,1)}, bf16[256,2560]{1,0:T(8,128)(2,1)}, u32[]{:S(2)}, u32[]{:S(2)}) collective-permute-start(bf16[256,2560]{1,0:T(8,128)(2,1)} %slice.18), channel_id=1, source_target_pairs={{0,16},{8,24},{16,0},{24,8},{1,17},{9,25},{17,1},{25,9},{2,18},{10... | collective-permute-start | bytes 3932168 | tf_op jit(solution)/shard_map/ppermute | solution.py:53
  6.4 0.0 copy-start.8
  6.4 1.4 %collective-permute-start.2 = (bf16[256,4096]{1,0:T(8,128)(2,1)}, bf16[256,4096]{1,0:T(8,128)(2,1)}, u32[]{:S(2)}, u32[]{:S(2)}) collective-permute-start(bf16[256,4096]{1,0:T(8,128)(2,1)} %bitcast.33), channel_id=1, source_target_pairs={{2,0},{4,2},{6,4},{3,1},{5,3},{7,5},{10,8},{12,10},{14,12},{11,9},... | collective-permute-start | bytes 6291464 | tf_op jit(solution)/shard_map/ppermute | solution.py:300
  7.8 0.0 copy-done
  7.8 0.5 multiply_reduce_fusion
  8.3 1.6 %collective-permute-start = (f32[1,256]{1,0:T(1,128)S(1)}, f32[1,256]{1,0:T(1,128)S(1)}, u32[]{:S(2)}, u32[]{:S(2)}) collective-permute-start(f32[1,256]{1,0:T(1,128)S(1)} %bitcast.27), channel_id=1, source_target_pairs={{0,1},{1,0},{2,3},{3,2},{4,5},{5,4},{6,7},{7,6},{8,9},{9,8},{10,11... | collective-permute-start | bytes 3080 | tf_op jit(solution)/shard_map/ppermute | solution.py:36
  9.8 2.1 %collective-permute-done.refs_1_ = f32[1,256]{1,0:T(1,128)S(1)} collective-permute-done((f32[1,256]{1,0:T(1,128)S(1)}, f32[1,256]{1,0:T(1,128)S(1)}, u32[]{:S(2)}, u32[]{:S(2)}) %collective-permute-start) | collective-permute-done | bytes 1056 | tf_op jit(solution)/shard_map/ppermute | solution.py:36
  11.9 0.0 copy-done.5
  11.9 0.2 shard_map.79
  12.1 0.7 %dynamic-slice_bitcast_fusion = (bf16[256,256]{1,0:T(8,128)(2,1)}, bf16[1,256,256]{2,1,0:T(8,128)(2,1)S(1)}, bf16[1,256,256]{2,1,0:T(8,128)(2,1)S(1)}, bf16[256,256]{1,0:T(8,128)(2,1)}) fusion(bf16[4,256,256]{2,1,0:T(8,128)(2,1)S(1)} %bitcast.26, s32[]{:T(128)S(6)} %select_n.91, s32[]{:T(128)S(6)} %select_n.84, s32[]{:T(128)S(6)} %select_n.82, s32[]{:T(128)S(6)} %select_n.80), kind=kLoop, calls=%fused_computation.9 | loop fusion | bytes 1048592 | tf_op jit(solution)/shard_map/jit(dynamic_index_in_dim)/squeeze | solution.py:312
  12.9 0.7 %pad_maximum_fusion = bf16[2,256,256]{2,1,0:T(8,128)(2,1)} fusion(bf16[1,256,256]{2,1,0:T(8,128)(2,1)S(1)} %get-tuple-element.20, bf16[1,256,256]{2,1,0:T(8,128)(2,1)S(1)} %get-tuple-element.21), kind=kLoop, calls=%fused_computation.1 | loop fusion | flops 131072 | bytes 524288 | tf_op jit(solution)/shard_map/stack | solution.py:315
  13.6 0.0 collective-permute-start.3
  13.6 0.0 copy-done.8
  13.6 0.0 copy-start.3
  13.6 3.4 %copy-done.3 = bf16[1,1024,4096]{2,1,0:T(8,128)(2,1)S(1)} copy-done((bf16[1,1024,4096]{2,1,0:T(8,128)(2,1)S(1)}, bf16[1,1024,4096]{2,1,0:T(8,128)(2,1)}, u32[]{:S(2)}) %copy-start.3) | copy-done | bytes 8388632
  17.0 4.6 %shard_map.76 = (bf16[256,4096]{1,0:T(8,128)(2,1)S(1)}, f32[1,4096]{1,0:T(1,128)S(1)}, f32[1,256]{1,0:T(1,128)S(1)}) custom-call(f32[1,256]{1,0:T(1,128)S(1)} %bitcast.29, f32[1,256]{1,0:T(1,128)S(1)} %collective-permute-done.refs_1_, bf16[256,1024]{1,0:T(8,128)(2,1)S(1)} %bitcast.25, bf16[1024,4096]{1,0:T(8,128)(2,1)S(1)} %bitcast.23, ...), custom_call_target="tpu_custom_call" | custom-call | flops 2147483648 | bytes 13107200 | tf_op jit(solution)/shard_map/pallas_call | solution.py:122
  21.6 0.0 copy-start.6
  21.6 1.3 %copy-done.6 = bf16[256,4096]{1,0:T(8,128)(2,1)} copy-done((bf16[256,4096]{1,0:T(8,128)(2,1)}, bf16[256,4096]{1,0:T(8,128)(2,1)S(1)}, u32[]{:S(2)}) %copy-start.6) | copy-done | bytes 2097176
  22.9 1.5 %collective-permute-start.1 = (f32[1,256]{1,0:T(1,128)S(1)}, f32[1,256]{1,0:T(1,128)S(1)}, u32[]{:S(2)}, u32[]{:S(2)}) collective-permute-start(f32[1,256]{1,0:T(1,128)S(1)} %get-tuple-element.11.refs_2_), channel_id=1, source_target_pairs={{0,1},{1,0},{2,3},{3,2},{4,5},{5,4},{6,7},{7,6},{8,9},{9,8},{10,11... | collective-permute-start | bytes 3080 | tf_op jit(solution)/shard_map/ppermute | solution.py:36
  24.4 0.1 slice.14
  24.5 2.0 %collective-permute-done.1.refs_3_ = f32[1,256]{1,0:T(1,128)S(1)} collective-permute-done((f32[1,256]{1,0:T(1,128)S(1)}, f32[1,256]{1,0:T(1,128)S(1)}, u32[]{:S(2)}, u32[]{:S(2)}) %collective-permute-start.1) | collective-permute-done | bytes 1056 | tf_op jit(solution)/shard_map/ppermute | solution.py:36
  26.5 0.0 copy-start.7
  26.5 1.6 %copy-done.7 = bf16[256,4096]{1,0:T(8,128)(2,1)S(1)} copy-done((bf16[256,4096]{1,0:T(8,128)(2,1)S(1)}, bf16[256,4096]{1,0:T(8,128)(2,1)}, u32[]{:S(2)}) %copy-start.7) | copy-done | bytes 2097176
  28.1 0.0 copy-start.9
  28.1 0.0 copy-start.10
  28.1 1.4 %shard_map.77.local_ref = bf16[256,4096]{1,0:T(8,128)(2,1)S(1)} custom-call(f32[1,256]{1,0:T(1,128)S(1)} %bitcast.30, f32[1,256]{1,0:T(1,128)S(1)} %collective-permute-done.refs_1_, f32[1,256]{1,0:T(1,128)S(1)} %get-tuple-element.11.refs_2_, f32[1,256]{1,0:T(1,128)S(1)} %collective-permute-done.1.refs_3_, bf16[256,4096]{1,0:T(8,128)(2,1)S(1)} %copy-done.7, ...), custom_call_target="tpu_custom_call" | custom-call | flops 3145728 | bytes 6291456 | tf_op jit(solution)/shard_map/pallas_call | solution.py:174
  29.5 0.0 copy-start.4
  29.5 1.3 %copy-done.4 = bf16[256,4096]{1,0:T(8,128)(2,1)} copy-done((bf16[256,4096]{1,0:T(8,128)(2,1)}, bf16[256,4096]{1,0:T(8,128)(2,1)S(1)}, u32[]{:S(2)}) %copy-start.4) | copy-done | bytes 2097176
  30.8 0.0 collective-permute-start.7
  30.8 0.0 collective-permute-done.3
  30.8 1.0 %slice_bitcast_fusion = (bf16[256,256]{1,0:T(8,128)(2,1)S(1)}, bf16[256,256]{1,0:T(8,128)(2,1)S(1)}) fusion(bf16[2,256,256]{2,1,0:T(8,128)(2,1)} %collective-permute-done.3), kind=kLoop, calls=%fused_computation.7 | loop fusion | bytes 524288 | tf_op jit(solution)/shard_map/squeeze | solution.py:318
  31.8 0.0 copy-done.9
  31.8 0.1 fusion
  31.9 1.8 %collective-permute-start.4 = (bf16[256,256]{1,0:T(8,128)(2,1)S(1)}, bf16[256,256]{1,0:T(8,128)(2,1)S(1)}, u32[]{:S(2)}, u32[]{:S(2)}) collective-permute-start(bf16[256,256]{1,0:T(8,128)(2,1)S(1)} %fusion), channel_id=1, source_target_pairs={{0,24},{8,16},{16,8},{24,0},{1,25},{9,17},{17,9},{25,1},{2,26},{10... | collective-permute-start | bytes 393224 | tf_op jit(solution)/shard_map/ppermute | solution.py:53
  33.7 0.0 copy-done.10
  33.7 0.0 collective-permute-done.6.refs_1_
  33.7 3.7 %shard_map.80.refs_2_ = bf16[256,4096]{1,0:T(8,128)(2,1)S(1)} custom-call(bf16[256,512]{1,0:T(8,128)(2,1)S(1)} %pad_maximum_fusion.2.scaled_ref, bf16[256,4096]{1,0:T(8,128)(2,1)S(1)} %bitcast.22, bf16[256,4096]{1,0:T(8,128)(2,1)} %collective-permute-done.6.refs_1_), custom_call_target="tpu_custom_call" | custom-call | flops 1073741824 | bytes 6553600 | tf_op jit(solution)/shard_map/pallas_call | solution.py:224
  37.4 0.0 copy-start.1
  37.4 1.3 %copy-done.1 = bf16[256,4096]{1,0:T(8,128)(2,1)} copy-done((bf16[256,4096]{1,0:T(8,128)(2,1)}, bf16[256,4096]{1,0:T(8,128)(2,1)S(1)}, u32[]{:S(2)}) %copy-start.1) | copy-done | bytes 2097176
  38.7 0.0 collective-permute-done.7
  38.7 0.0 collective-permute-done.4
  38.7 1.5 %collective-permute-start.8 = (bf16[256,1536]{1,0:T(8,128)(2,1)S(1)}, bf16[256,1536]{1,0:T(8,128)(2,1)S(1)}, u32[]{:S(2)}, u32[]{:S(2)}) collective-permute-start(bf16[256,1536]{1,0:T(8,128)(2,1)S(1)} %slice.14), channel_id=1, source_target_pairs={{0,16},{8,24},{16,0},{24,8},{1,17},{9,25},{17,1},{25,9},{2,18},{10... | collective-permute-start | bytes 2359304 | tf_op jit(solution)/shard_map/ppermute | solution.py:53
  40.2 0.0 collective-permute-done.11.refs_4_
  40.2 0.5 collective-permute-start.12
  40.7 0.1 collective-permute-start.9
  40.8 1.6 %collective-permute-start.5 = (bf16[256,256]{1,0:T(8,128)(2,1)S(1)}, bf16[256,256]{1,0:T(8,128)(2,1)S(1)}, u32[]{:S(2)}, u32[]{:S(2)}) collective-permute-start(bf16[256,256]{1,0:T(8,128)(2,1)S(1)} %collective-permute-done.4), channel_id=1, source_target_pairs={{0,1},{1,0},{2,3},{3,2},{4,5},{5,4},{6,7},{7,6},{8,9},{9,8},{10,11... | collective-permute-start | bytes 393224 | tf_op jit(solution)/shard_map/ppermute | solution.py:36
  42.4 0.9 %collective-permute-done.9 = f32[1,4096]{1,0:T(1,128)S(1)} collective-permute-done((f32[1,4096]{1,0:T(1,128)S(1)}, f32[1,4096]{1,0:T(1,128)S(1)}, u32[]{:S(2)}, u32[]{:S(2)}) %collective-permute-start.9) | collective-permute-done | bytes 16416 | tf_op jit(solution)/shard_map/ppermute | solution.py:53
  43.3 0.6 add.107
  43.9 2.8 %collective-permute-done.5 = bf16[256,256]{1,0:T(8,128)(2,1)S(1)} collective-permute-done((bf16[256,256]{1,0:T(8,128)(2,1)S(1)}, bf16[256,256]{1,0:T(8,128)(2,1)S(1)}, u32[]{:S(2)}, u32[]{:S(2)}) %collective-permute-start.5) | collective-permute-done | bytes 131104 | tf_op jit(solution)/shard_map/ppermute | solution.py:36
  46.8 0.0 copy-start.2
  46.8 9.5 %collective-permute-done.2.received_ref = bf16[256,4096]{1,0:T(8,128)(2,1)} collective-permute-done((bf16[256,4096]{1,0:T(8,128)(2,1)}, bf16[256,4096]{1,0:T(8,128)(2,1)}, u32[]{:S(2)}, u32[]{:S(2)}) %collective-permute-start.2) | collective-permute-done | bytes 2097184 | tf_op jit(solution)/shard_map/ppermute | solution.py:300
  56.3 4.0 %shard_map.78 = bf16[256,4096]{1,0:T(8,128)(2,1)} custom-call(bf16[256,4096]{1,0:T(8,128)(2,1)} %copy-done.4, bf16[256,4096]{1,0:T(8,128)(2,1)} %collective-permute-done.2.received_ref), custom_call_target="tpu_custom_call" | custom-call | flops 1048576 | bytes 6291456 | tf_op jit(solution)/shard_map/pallas_call | solution.py:194
  60.3 0.0 collective-permute-done.8.refs_4_
  60.3 0.0 collective-permute-start.10
  60.3 0.0 collective-permute-done.12.refs_3_
  60.3 0.0 copy-done.2
  60.3 3.3 %shard_map.81.refs_5_ = f32[256,4096]{1,0:T(8,128)} custom-call(bf16[256,512]{1,0:T(8,128)(2,1)S(1)} %pad_maximum_fusion.1.refs_0_, f32[1,4096]{1,0:T(1,128)S(1)} %copy-done.8, bf16[256,4096]{1,0:T(8,128)(2,1)S(1)} %copy-done.2, bf16[256,2560]{1,0:T(8,128)(2,1)S(1)} %collective-permute-done.12.refs_3_, bf16[256,2560]{1,0:T(8,128)(2,1)} %collective-permute-done.11.refs_4_), custom_call_target="tpu_custom_call" | custom-call | flops 671088640 | bytes 6815744 | tf_op jit(solution)/shard_map/pallas_call | solution.py:266
  63.7 0.0 collective-permute-done.10.refs_3_
  63.7 2.3 %shard_map.82 = f32[256,4096]{1,0:T(8,128)} custom-call(bf16[256,512]{1,0:T(8,128)(2,1)S(1)} %pad_maximum_fusion.1.refs_0_, f32[1,4096]{1,0:T(1,128)S(1)} %copy-done.8, bf16[256,4096]{1,0:T(8,128)(2,1)S(1)} %copy-done.2, bf16[256,1536]{1,0:T(8,128)(2,1)S(1)} %collective-permute-done.10.refs_3_, ...), custom_call_target="tpu_custom_call", output_to_operand_aliasing={{}: (5, {})} | custom-call | flops 402653184 | bytes 4194304 | tf_op jit(solution)/shard_map/pallas_call | solution.py:266
  (6 shorter events, 0.1 us)
Async XLA Ops:
  0.6 7.1 %copy-start = (bf16[1,256,4096]{2,1,0:T(8,128)(2,1)S(1)}, bf16[1,256,4096]{2,1,0:T(8,128)(2,1)}, u32[]{:S(2)}) copy-start(bf16[1,256,4096]{2,1,0:T(8,128)(2,1)} %param.5) | copy-start | bytes 6291460
  0.6 11.3 %copy-start.5 = (bf16[1,256,1024]{2,1,0:T(8,128)(2,1)S(1)}, bf16[1,256,1024]{2,1,0:T(8,128)(2,1)}, u32[]{:S(2)}) copy-start(bf16[1,256,1024]{2,1,0:T(8,128)(2,1)} %param.8) | copy-start | bytes 1572868
  0.7 33.1 %collective-permute-start.6 = (bf16[256,4096]{1,0:T(8,128)(2,1)}, bf16[256,4096]{1,0:T(8,128)(2,1)}, u32[]{:S(2)}, u32[]{:S(2)}) collective-permute-start(bf16[256,4096]{1,0:T(8,128)(2,1)} %bitcast.17), channel_id=1, source_target_pairs={{0,8},{8,0},{16,24},{24,16},{1,9},{9,1},{17,25},{25,17},{2,10},{10... | collective-permute-start | bytes 6291464 | tf_op jit(solution)/shard_map/ppermute | solution.py:53
  3.9 36.3 %collective-permute-start.11 = (bf16[256,2560]{1,0:T(8,128)(2,1)}, bf16[256,2560]{1,0:T(8,128)(2,1)}, u32[]{:S(2)}, u32[]{:S(2)}) collective-permute-start(bf16[256,2560]{1,0:T(8,128)(2,1)} %slice.18), channel_id=1, source_target_pairs={{0,16},{8,24},{16,0},{24,8},{1,17},{9,25},{17,1},{25,9},{2,18},{10... | collective-permute-start | bytes 3932168 | tf_op jit(solution)/shard_map/ppermute | solution.py:53
  6.4 7.3 %copy-start.8 = (f32[1,4096]{1,0:T(1,128)S(1)}, f32[1,4096]{1,0:T(1,128)}, u32[]{:S(2)}) copy-start(f32[1,4096]{1,0:T(1,128)} %refs_1_.3) | copy-start | bytes 49156
  6.4 49.9 %collective-permute-start.2 = (bf16[256,4096]{1,0:T(8,128)(2,1)}, bf16[256,4096]{1,0:T(8,128)(2,1)}, u32[]{:S(2)}, u32[]{:S(2)}) collective-permute-start(bf16[256,4096]{1,0:T(8,128)(2,1)} %bitcast.33), channel_id=1, source_target_pairs={{2,0},{4,2},{6,4},{3,1},{5,3},{7,5},{10,8},{12,10},{14,12},{11,9},... | collective-permute-start | bytes 6291464 | tf_op jit(solution)/shard_map/ppermute | solution.py:300
  8.3 3.6 %collective-permute-start = (f32[1,256]{1,0:T(1,128)S(1)}, f32[1,256]{1,0:T(1,128)S(1)}, u32[]{:S(2)}, u32[]{:S(2)}) collective-permute-start(f32[1,256]{1,0:T(1,128)S(1)} %bitcast.27), channel_id=1, source_target_pairs={{0,1},{1,0},{2,3},{3,2},{4,5},{5,4},{6,7},{7,6},{8,9},{9,8},{10,11... | collective-permute-start | bytes 3080 | tf_op jit(solution)/shard_map/ppermute | solution.py:36
  13.6 17.2 %collective-permute-start.3 = (bf16[2,256,256]{2,1,0:T(8,128)(2,1)}, bf16[2,256,256]{2,1,0:T(8,128)(2,1)}, u32[]{:S(2)}, u32[]{:S(2)}) collective-permute-start(bf16[2,256,256]{2,1,0:T(8,128)(2,1)} %pad_maximum_fusion), channel_id=1, source_target_pairs={{0,8},{8,0},{16,24},{24,16},{1,9},{9,1},{17,25},{25,17},{2,10},{10... | collective-permute-start | bytes 786440 | tf_op jit(solution)/shard_map/ppermute | solution.py:53
  13.6 3.4 %copy-start.3 = (bf16[1,1024,4096]{2,1,0:T(8,128)(2,1)S(1)}, bf16[1,1024,4096]{2,1,0:T(8,128)(2,1)}, u32[]{:S(2)}) copy-start(bf16[1,1024,4096]{2,1,0:T(8,128)(2,1)} %param.7) | copy-start | bytes 25165828
  21.6 1.3 %copy-start.6 = (bf16[256,4096]{1,0:T(8,128)(2,1)}, bf16[256,4096]{1,0:T(8,128)(2,1)S(1)}, u32[]{:S(2)}) copy-start(bf16[256,4096]{1,0:T(8,128)(2,1)S(1)} %get-tuple-element.12.refs_4_) | copy-start | bytes 6291460
  22.9 3.6 %collective-permute-start.1 = (f32[1,256]{1,0:T(1,128)S(1)}, f32[1,256]{1,0:T(1,128)S(1)}, u32[]{:S(2)}, u32[]{:S(2)}) collective-permute-start(f32[1,256]{1,0:T(1,128)S(1)} %get-tuple-element.11.refs_2_), channel_id=1, source_target_pairs={{0,1},{1,0},{2,3},{3,2},{4,5},{5,4},{6,7},{7,6},{8,9},{9,8},{10,11... | collective-permute-start | bytes 3080 | tf_op jit(solution)/shard_map/ppermute | solution.py:36
  26.5 1.6 %copy-start.7 = (bf16[256,4096]{1,0:T(8,128)(2,1)S(1)}, bf16[256,4096]{1,0:T(8,128)(2,1)}, u32[]{:S(2)}) copy-start(bf16[256,4096]{1,0:T(8,128)(2,1)} %copy-done.6) | copy-start | bytes 6291460
  28.1 3.7 %copy-start.9 = (bf16[256,256]{1,0:T(8,128)(2,1)S(1)}, bf16[256,256]{1,0:T(8,128)(2,1)}, u32[]{:S(2)}) copy-start(bf16[256,256]{1,0:T(8,128)(2,1)} %get-tuple-element.22) | copy-start | bytes 393220
  28.1 5.6 %copy-start.10 = (bf16[256,256]{1,0:T(8,128)(2,1)S(1)}, bf16[256,256]{1,0:T(8,128)(2,1)}, u32[]{:S(2)}) copy-start(bf16[256,256]{1,0:T(8,128)(2,1)} %get-tuple-element.19) | copy-start | bytes 393220
  29.5 1.3 %copy-start.4 = (bf16[256,4096]{1,0:T(8,128)(2,1)}, bf16[256,4096]{1,0:T(8,128)(2,1)S(1)}, u32[]{:S(2)}) copy-start(bf16[256,4096]{1,0:T(8,128)(2,1)S(1)} %shard_map.77.local_ref) | copy-start | bytes 6291460
  30.8 7.9 %collective-permute-start.7 = (f32[1,4096]{1,0:T(1,128)S(1)}, f32[1,4096]{1,0:T(1,128)S(1)}, u32[]{:S(2)}, u32[]{:S(2)}) collective-permute-start(f32[1,4096]{1,0:T(1,128)S(1)} %get-tuple-element.15), channel_id=1, source_target_pairs={{0,24},{8,16},{16,8},{24,0},{1,25},{9,17},{17,9},{25,1},{2,26},{10... | collective-permute-start | bytes 49160 | tf_op jit(solution)/shard_map/ppermute | solution.py:53
  31.9 6.8 %collective-permute-start.4 = (bf16[256,256]{1,0:T(8,128)(2,1)S(1)}, bf16[256,256]{1,0:T(8,128)(2,1)S(1)}, u32[]{:S(2)}, u32[]{:S(2)}) collective-permute-start(bf16[256,256]{1,0:T(8,128)(2,1)S(1)} %fusion), channel_id=1, source_target_pairs={{0,24},{8,16},{16,8},{24,0},{1,25},{9,17},{17,9},{25,1},{2,26},{10... | collective-permute-start | bytes 393224 | tf_op jit(solution)/shard_map/ppermute | solution.py:53
  37.4 1.3 %copy-start.1 = (bf16[256,4096]{1,0:T(8,128)(2,1)}, bf16[256,4096]{1,0:T(8,128)(2,1)S(1)}, u32[]{:S(2)}) copy-start(bf16[256,4096]{1,0:T(8,128)(2,1)S(1)} %shard_map.80.refs_2_) | copy-start | bytes 6291460
  38.7 21.6 %collective-permute-start.8 = (bf16[256,1536]{1,0:T(8,128)(2,1)S(1)}, bf16[256,1536]{1,0:T(8,128)(2,1)S(1)}, u32[]{:S(2)}, u32[]{:S(2)}) collective-permute-start(bf16[256,1536]{1,0:T(8,128)(2,1)S(1)} %slice.14), channel_id=1, source_target_pairs={{0,16},{8,24},{16,0},{24,8},{1,17},{9,25},{17,1},{25,9},{2,18},{10... | collective-permute-start | bytes 2359304 | tf_op jit(solution)/shard_map/ppermute | solution.py:53
  40.2 20.1 %collective-permute-start.12 = (bf16[256,2560]{1,0:T(8,128)(2,1)}, bf16[256,2560]{1,0:T(8,128)(2,1)S(1)}, u32[]{:S(2)}, u32[]{:S(2)}) collective-permute-start(bf16[256,2560]{1,0:T(8,128)(2,1)} %collective-permute-done.11.refs_4_), channel_id=1, source_target_pairs={{0,8},{8,0},{16,24},{24,16},{1,9},{9,1},{17,25},{25,17},{2,10},{10... | collective-permute-start | bytes 3932168 | tf_op jit(solution)/shard_map/ppermute | solution.py:53
  40.7 2.5 %collective-permute-start.9 = (f32[1,4096]{1,0:T(1,128)S(1)}, f32[1,4096]{1,0:T(1,128)S(1)}, u32[]{:S(2)}, u32[]{:S(2)}) collective-permute-start(f32[1,4096]{1,0:T(1,128)S(1)} %add.106), channel_id=1, source_target_pairs={{0,8},{8,0},{16,24},{24,16},{1,9},{9,1},{17,25},{25,17},{2,10},{10... | collective-permute-start | bytes 49160 | tf_op jit(solution)/shard_map/ppermute | solution.py:53
  40.8 5.9 %collective-permute-start.5 = (bf16[256,256]{1,0:T(8,128)(2,1)S(1)}, bf16[256,256]{1,0:T(8,128)(2,1)S(1)}, u32[]{:S(2)}, u32[]{:S(2)}) collective-permute-start(bf16[256,256]{1,0:T(8,128)(2,1)S(1)} %collective-permute-done.4), channel_id=1, source_target_pairs={{0,1},{1,0},{2,3},{3,2},{4,5},{5,4},{6,7},{7,6},{8,9},{9,8},{10,11... | collective-permute-start | bytes 393224 | tf_op jit(solution)/shard_map/ppermute | solution.py:36
  46.8 13.5 %copy-start.2 = (bf16[256,4096]{1,0:T(8,128)(2,1)S(1)}, bf16[256,4096]{1,0:T(8,128)(2,1)}, u32[]{:S(2)}) copy-start(bf16[256,4096]{1,0:T(8,128)(2,1)} %copy-done.1) | copy-start | bytes 6291460
  60.3 3.3 %collective-permute-start.10 = (bf16[256,1536]{1,0:T(8,128)(2,1)S(1)}, bf16[256,1536]{1,0:T(8,128)(2,1)S(1)}, u32[]{:S(2)}, u32[]{:S(2)}) collective-permute-start(bf16[256,1536]{1,0:T(8,128)(2,1)S(1)} %collective-permute-done.8.refs_4_), channel_id=1, source_target_pairs={{0,8},{8,0},{16,24},{24,16},{1,9},{9,1},{17,25},{25,17},{2,10},{10... | collective-permute-start | bytes 2359304 | tf_op jit(solution)/shard_map/ppermute | solution.py:53
